TPU v7x, 32 devices: a whole 2x2x4 slice. The times are simulated.
32 devices in a mesh: grp: 4 (over z), loc: 4 (over y, core), tp: 2 (over x).
Axes of the slice: x: 2, y: 2, z: 4, core: 2. Of those that a mesh axis runs over, the one named last changes fastest.
Arguments:
- tokens: bfloat16 [2048, 2048], P(('grp', 'tp')), may hold values from -6 to 6
- expert_ids: int32 [2048, 8], P(('grp', 'tp')), may hold values from 0 to 15, as said below
- router_weights: bfloat16 [2048, 8], P(('grp', 'tp')), may hold values from 0.19921875 to 1
- w_gate: bfloat16 [16, 2048, 768], P(('grp', 'loc')), may hold values from -0.125 to 0.125
- w_up: bfloat16 [16, 2048, 768], P(('grp', 'loc')), may hold values from -0.125 to 0.125
- w_down: bfloat16 [16, 768, 2048], P(('grp', 'loc'), None, 'tp'), may hold values from -0.21875 to 0.21875
Outputs:
- mixed: bfloat16 [2048, 2048], P(('grp', 'tp'), 'loc')
Inputs may be any that keep to these rules, and one draw needn't show every extreme that they name: `expert_ids`: each row names 8 different experts, two from each of 4 different groups, group g holding experts g * 4 to g * 4 + 3. Within each aligned block of 256 rows, no expert is named by more than 128 rows, and in every block some expert is named by exactly 128 rows.
All inputs are finite; a program needn't handle non-finite values.
Results may differ from a plain program's by a relative error of at most 0.0057.
Values may be sent and summed in bfloat16 or wider, within the bound.
No kernel may reach another device: no remote copies, remote signals or barrier semaphores. Data moves between devices by JAX's collectives and lax.ppermute only.
A program may use at most 64 MiB of HBM per device.

v0:
```python
import jax
import jax.numpy as jnp
from jax import lax
from jax.sharding import PartitionSpec as P


def body(tokens, expert_ids, router_weights, w_gate, w_up, w_down):
    groups = lax.axis_size("grp")
    group_size = lax.axis_size("loc")
    own_local = lax.axis_index("loc")
    tok_rows, width_model = tokens.shape
    choices_per = expert_ids.shape[1]
    quantum = tok_rows // groups
    capacity = (2 * quantum * (4 + min(2, groups - 4)) + group_size - 1) // group_size
    slot_total = groups * capacity
    flat_expert = expert_ids.reshape(-1)
    flat_weight = router_weights.reshape(-1)
    token_row = jnp.arange(tok_rows * choices_per, dtype=jnp.int32) // choices_per
    targets = jnp.arange(groups, dtype=jnp.int32) * group_size + own_local
    hit_table = (flat_expert[:, None] == targets[None, :]).astype(jnp.int32)
    slot_rank = jnp.sum(jnp.cumsum(hit_table, axis=0) * hit_table, axis=1) - 1
    is_mine = jnp.sum(hit_table, axis=1) > 0
    slot_index = jnp.where(is_mine, flat_expert // group_size * capacity + slot_rank, slot_total)
    source_rows = (
        jnp.full((slot_total,), tok_rows, jnp.int32).at[slot_index].set(token_row, mode="drop")
    )
    outgoing = jnp.take(tokens, source_rows, axis=0, mode="fill", fill_value=0)
    arriving = lax.all_to_all(
        outgoing.reshape(groups, capacity, width_model),
        "grp",
        split_axis=0,
        concat_axis=0,
        tiled=True,
    )
    arriving = arriving.reshape(slot_total, width_model)
    gate_act = jnp.dot(arriving, w_gate[0], preferred_element_type=jnp.float32)
    upward = jnp.dot(arriving, w_up[0], preferred_element_type=jnp.float32)
    hidden = (jax.nn.silu(gate_act) * upward).astype(jnp.bfloat16)
    expert_out = jnp.dot(
        hidden,
        lax.all_gather(w_down[0], "tp", axis=1, tiled=True),
        preferred_element_type=jnp.float32,
    ).astype(jnp.bfloat16)
    mixing = (
        jnp.zeros((tok_rows, slot_total), jnp.bfloat16)
        .at[token_row, slot_index]
        .set(flat_weight, mode="drop")
    )
    returned = lax.all_to_all(
        expert_out.reshape(groups, capacity, width_model),
        "grp",
        split_axis=0,
        concat_axis=0,
        tiled=True,
    )
    local_sum = jnp.dot(
        mixing, returned.reshape(slot_total, width_model), preferred_element_type=jnp.float32
    )
    summed = lax.psum_scatter(local_sum, "loc", scatter_dimension=1, tiled=True)
    return summed.astype(jnp.bfloat16)


def solution(mesh):
    placed = (
        P(("grp", "tp"), None),
        P(("grp", "tp"), None),
        P(("grp", "tp"), None),
        P(("grp", "loc"), None, None),
        P(("grp", "loc"), None, None),
        P(("grp", "loc"), None, "tp"),
    )
    return jax.shard_map(
        body, mesh=mesh, in_specs=placed, out_specs=P(("grp", "tp"), "loc"), check_vma=False
    )
```

profile of v0, /device:TPU:0, one launch (start us, length us, event | category | flops | bytes accessed | tf_op | source)
XLA Modules:
  0.0 191.5 jit_solution(1412043414097618468)
XLA Ops:
  6.5 1.0 copy.7
  7.5 0.1 eq.29
  7.6 0.1 eq.25
  7.7 0.1 reshape.200
  7.9 0.1 compare_convert_fusion.1
  8.0 1.1 reduce-window.6
  9.1 0.2 slice_reduce_fusion
  9.3 0.2 reduce-window.9
  9.5 0.1 add_bitcast_fusion
  9.6 0.1 fusion.16
  9.7 0.1 compare_select_fusion
  9.8 8.0 %scatter_custom_fusion = s32[512]{0:T(512)S(1)} fusion(s32[2048]{0:T(1024)S(1)} %bitcast.40, s32[2048]{0:T(1024)S(1)} %add_select_fusion, s32[]{:T(128)} %constant.63.clone.1), kind=kCustom, calls=%fused_computation.49 | custom fusion | bytes 2052 | tf_op jit(solution)/shard_map/scatter | solution.py:25
  17.9 6.7 %gather_fusion = bf16[512,2048]{1,0:T(8,128)(2,1)} fusion(bf16[256,2048]{1,0:T(8,128)(2,1)} %param.6, s32[1024]{0:T(1024)S(1)} %pad_clamp_fusion), kind=kCustom, calls=%fused_computation | custom fusion | bytes 4196352 | tf_op jit(solution)/shard_map/jit(_take)/gather | solution.py:27
  24.5 3.2 %broadcast_select_fusion = bf16[4,128,2048]{2,1,0:T(8,128)(2,1)} fusion(bf16[4,128,2048]{2,1,0:T(8,128)(2,1)} %bitcast.38, pred[4,128]{1,0:T(4,128)(4,1)S(1)} %and_bitcast_fusion), kind=kLoop, calls=%fused_computation.10 | loop fusion | flops 1048576 | bytes 4194816 | tf_op jit(solution)/shard_map/jit(_take)/select_n | solution.py:27
  27.7 6.3 %all-to-all-start = ((bf16[4,128,2048]{2,1,0:T(8,128)(2,1)}), bf16[4,128,2048]{2,1,0:T(8,128)(2,1)}, u32[]{:S(2)}, u32[]{:S(2)}) async-start(bf16[4,128,2048]{2,1,0:T(8,128)(2,1)} %broadcast_select_fusion), calls=%async_computation | async-start | bytes 4194304 | tf_op jit(solution)/shard_map/all_to_all | solution.py:28
  34.0 0.7 all-gather.3.cloned.1.call-update
  34.7 47.6 %all-to-all-done = bf16[4,128,2048]{2,1,0:T(8,128)(2,1)} async-done(((bf16[4,128,2048]{2,1,0:T(8,128)(2,1)}), bf16[4,128,2048]{2,1,0:T(8,128)(2,1)}, u32[]{:S(2)}, u32[]{:S(2)}) %all-to-all-start) | async-done | bytes 2097184 | tf_op jit(solution)/shard_map/all_to_all | solution.py:28
  82.3 5.5 %fusion.4 = f32[512,768]{1,0:T(8,128)} fusion(bf16[512,2048]{1,0:T(8,128)(2,1)} %bitcast.5, bf16[1,2048,768]{2,1,0:T(8,128)(2,1)} %param.9), kind=kOutput, calls=%fused_computation.7 | convolution fusion | flops 1610612736 | bytes 6815744 | tf_op jit(solution)/shard_map/dot_general | solution.py:36
  87.9 8.3 %fusion.6 = bf16[512,2048]{1,0:T(8,128)(2,1)} fusion(bf16[1,768,2048]{2,1,0:T(8,128)(2,1)} %all-gather.3.cloned.1.call-done, f32[512,768]{1,0:T(8,128)} %fusion.4, bf16[512,2048]{1,0:T(8,128)(2,1)} %bitcast.5, bf16[1,2048,768]{2,1,0:T(8,128)(2,1)S(1)} %copy-done), kind=kOutput, calls=%fused_computation.9 | convolution fusion | flops 3224633344 | bytes 12058624 | tf_op jit(solution)/shard_map/dot_general | solution.py:39
  96.2 4.6 %all-to-all-start.1 = ((bf16[4,128,2048]{2,1,0:T(8,128)(2,1)}), bf16[4,128,2048]{2,1,0:T(8,128)(2,1)}, u32[]{:S(2)}, u32[]{:S(2)}) async-start(bf16[4,128,2048]{2,1,0:T(8,128)(2,1)} %bitcast.39), calls=%async_computation.1 | async-start | bytes 4194304 | tf_op jit(solution)/shard_map/all_to_all | solution.py:49
  100.8 0.2 reduce-scatter.2.cloned.1.call-start
  101.0 0.1 copy.10
  101.1 0.1 reshape.228
  101.3 0.1 multiply_reduce_fusion
  101.4 0.1 and_reduce_fusion
  101.5 15.3 %scatter_custom_fusion.1 = bf16[131072]{0:T(1024)(128)(2,1)} fusion(s32[2048]{0:T(1024)S(1)} %broadcast_select_fusion.1, bf16[2048]{0:T(1024)(128)(2,1)S(1)} %reshape.228, bf16[]{:T(256)} %constant.57.clone.1), kind=kCustom, calls=%fused_computation.12 | custom fusion | bytes 262146
  116.8 1.1 reshape.209
  117.9 30.6 %all-to-all-done.1 = bf16[4,128,2048]{2,1,0:T(8,128)(2,1)} async-done(((bf16[4,128,2048]{2,1,0:T(8,128)(2,1)}), bf16[4,128,2048]{2,1,0:T(8,128)(2,1)}, u32[]{:S(2)}, u32[]{:S(2)}) %all-to-all-start.1) | async-done | bytes 2097184 | tf_op jit(solution)/shard_map/all_to_all | solution.py:49
  148.5 3.6 %fusion.23 = f32[256,2048]{1,0:T(8,128)} fusion(bf16[256,512]{1,0:T(8,128)(2,1)S(1)} %reshape.209, bf16[512,2048]{1,0:T(8,128)(2,1)} %bitcast.10), kind=kOutput, calls=%fused_computation.53 | convolution fusion | flops 536870912 | bytes 4456448 | tf_op jit(solution)/shard_map/dot_general | solution.py:56
  152.1 0.0 reduce-scatter.2.cloned.1.call-update
  152.2 30.7 %reduce-scatter.2.cloned.1.call-done = f32[256,512]{1,0:T(8,128)} async-done(((f32[256,2048]{1,0:T(8,128)}), f32[256,512]{1,0:T(8,128)}) %reduce-scatter.2.cloned.1.call-update) | async-done | bytes 524304 | tf_op jit(solution)/shard_map/reduce_scatter | solution.py:59
  182.8 1.8 convert_element_type.20
  (18 shorter events, 0.1 us)
Async XLA Ops:
  6.5 81.3 %copy-start = (bf16[1,2048,768]{2,1,0:T(8,128)(2,1)S(1)}, bf16[1,2048,768]{2,1,0:T(8,128)(2,1)}, u32[]{:S(2)}) copy-start(bf16[1,2048,768]{2,1,0:T(8,128)(2,1)} %param.10) | copy-start | bytes 9437188
  27.7 54.6 %all-to-all-start = ((bf16[4,128,2048]{2,1,0:T(8,128)(2,1)}), bf16[4,128,2048]{2,1,0:T(8,128)(2,1)}, u32[]{:S(2)}, u32[]{:S(2)}) async-start(bf16[4,128,2048]{2,1,0:T(8,128)(2,1)} %broadcast_select_fusion), calls=%async_computation | async-start | bytes 4194304 | tf_op jit(solution)/shard_map/all_to_all | solution.py:28
  34.0 53.8 %all-gather.3.cloned.1.call-start = ((), (), s32[]{:S(2)}) async-start(), calls=%async_computation.4 | async-start | bytes 4718592 | tf_op jit(solution)/shard_map/all_gather | solution.py:41
  96.2 4.8 %copy-start.1 = (bf16[256,8]{0,1:T(8,128)(2,1)S(1)}, bf16[256,8]{0,1:T(8,128)(2,1)}, u32[]{:S(2)}) copy-start(bf16[256,8]{0,1:T(8,128)(2,1)} %param.8) | copy-start | bytes 12292
  96.2 5.1 %copy-start.3 = (s32[2]{0:T(128)S(1)}, s32[2]{0:T(128)}, u32[]{:S(2)}) copy-start(s32[2]{0:T(128)} %constant.75) | copy-start | bytes 28
  96.2 5.2 %copy-start.2 = (s32[2]{0:T(128)S(1)}, s32[2]{0:T(128)}, u32[]{:S(2)}) copy-start(s32[2]{0:T(128)} %constant.78) | copy-start | bytes 28
  96.2 52.3 %all-to-all-start.1 = ((bf16[4,128,2048]{2,1,0:T(8,128)(2,1)}), bf16[4,128,2048]{2,1,0:T(8,128)(2,1)}, u32[]{:S(2)}, u32[]{:S(2)}) async-start(bf16[4,128,2048]{2,1,0:T(8,128)(2,1)} %bitcast.39), calls=%async_computation.1 | async-start | bytes 4194304 | tf_op jit(solution)/shard_map/all_to_all | solution.py:49
  100.8 82.1 %reduce-scatter.2.cloned.1.call-start = ((), (), s32[]{:S(2)}) async-start(), calls=%async_computation.3 | async-start | bytes 2621440 | tf_op jit(solution)/shard_map/reduce_scatter | solution.py:59
Sparse Core Ops, SparseCore 0:
  36.4 46.3 all-gather.2
  152.3 30.5 reduce-scatter.1
where the time goes:
time: 192 us; the launch traced here: 191 us
  waiting for transfers between devices  110 us (57%)
  local copies, waits for them, and re-layouts  32.9 us (17%)
  matrix products  17.5 us (9%)
  between operations  13.5 us (7%)
  starting transfers between devices  11.1 us (6%)
  other arithmetic  6.84 us (4%)
    all_to_all x1, waiting for transfers between devices, body(): lax.all_to_all(outgoing.reshape(groups, capacity, width_model), 'grp', sp...  47.6 us
    reduce_scatter x1, waiting for transfers between devices, body(): summed = lax.psum_scatter(local_sum, 'loc', scatter_dimension=1, tiled=True)  30.7 us
    all_to_all x1, waiting for transfers between devices, body(): lax.all_to_all(expert_out.reshape(groups, capacity, width_model), 'grp',...  30.6 us
    unnamed x11, local copies, waits for them, and re-layouts  16.4 us
    dot_general x1, matrix products, body(): jnp.dot(hidden, lax.all_gather(w_down[0], 'tp', axis=1, tiled=True), pref...  8.33 us
    scatter x1, local copies, waits for them, and re-layouts, body(): jnp.full((slot_total,), tok_rows, jnp.int32).at[slot_index]  8.04 us
    gather x1, local copies, waits for them, and re-layouts, body(): outgoing = jnp.take(tokens, source_rows, axis=0, mode='fill', fill_value=0)  6.65 us
    all_to_all x1, starting transfers between devices, body(): lax.all_to_all(outgoing.reshape(groups, capacity, width_model), 'grp', sp...  6.32 us
  transfers between devices with their start and end apart: 4, of which 3 were waited for; matrix products, arithmetic and copies ran while one was open for 12% of the time, Pallas kernels for 0%

commit v1 on v0

v1 whole, which is shorter than its diff:
```python
import jax
import jax.numpy as jnp
from jax import lax
from jax.sharding import PartitionSpec as P


def swap_bit(value, axis, bit):
    size = lax.axis_size(axis)
    return lax.ppermute(value, axis, [(i, i ^ bit) for i in range(size)])


def shift_by(value, axis, step):
    size = lax.axis_size(axis)
    return lax.ppermute(value, axis, [(i, (i + step) % size) for i in range(size)])


def bits_of(size):
    return [1 << i for i in range(size.bit_length() - 1)]


def body(tokens, expert_ids, router_weights, w_gate, w_up, w_down):
    groups = lax.axis_size("grp")
    group_size = lax.axis_size("loc")
    tp_size = lax.axis_size("tp")
    own_group = lax.axis_index("grp")
    own_local = lax.axis_index("loc")
    own_tp = lax.axis_index("tp")
    rows, width = tokens.shape
    part = rows // group_size
    out_cols = width // group_size
    shifts = sorted(range(1, groups), key=lambda s: -min(s, groups - s))

    mine = lax.dynamic_slice_in_dim(tokens, own_local * part, part, 0)
    sent = {s: shift_by(mine, "grp", s) for s in shifts}

    weight_of = {}
    for s in range(groups):
        target = ((own_group + s) % groups) * group_size + own_local
        hit = expert_ids == target
        dense = jnp.sum(jnp.where(hit, router_weights.astype(jnp.float32), 0.0), axis=1)
        weight_of[s] = dense.astype(jnp.bfloat16)
    for s in shifts:
        weight_of[s] = shift_by(weight_of[s], "grp", s)

    down = w_down[0]
    for bit in bits_of(tp_size):
        other = swap_bit(down, "tp", bit)
        down = jnp.where(
            own_tp & bit > 0,
            jnp.concatenate([other, down], axis=1),
            jnp.concatenate([down, other], axis=1),
        )

    def whole_block(piece):
        got = piece[None]
        order = [own_local]
        for bit in reversed(bits_of(group_size)):
            got = jnp.concatenate([got, swap_bit(got, "loc", bit)], axis=0)
        index = [0]
        for bit in reversed(bits_of(group_size)):
            index = index + [i ^ bit for i in index]
        inverse = jnp.asarray([index.index(i) for i in range(group_size)], jnp.int32)
        take = inverse[jnp.arange(group_size, dtype=jnp.int32) ^ own_local]
        return jnp.take(got, take, axis=0).reshape(rows, width)

    def ffn(block):
        gate_act = jnp.dot(block, w_gate[0], preferred_element_type=jnp.float32)
        upward = jnp.dot(block, w_up[0], preferred_element_type=jnp.float32)
        return (jax.nn.silu(gate_act) * upward).astype(jnp.bfloat16)

    hidden = {}
    for s in shifts:
        hidden[s] = ffn(whole_block(sent[s]))
    hidden[0] = ffn(tokens)

    def group_sum(s):
        scale = weight_of[s].astype(jnp.float32)[:, None]
        pieces = []
        for k in range(group_size):
            cols = lax.dynamic_slice_in_dim(down, (own_local ^ k) * out_cols, out_cols, 1)
            result = jnp.dot(hidden[s], cols, preferred_element_type=jnp.float32)
            pieces.append(result.astype(jnp.bfloat16).astype(jnp.float32) * scale)
        held = {k: pieces[k] for k in range(group_size)}
        for bit in bits_of(group_size):
            leaving = [k for k in held if k & bit]
            arrived = swap_bit(
                jnp.stack([held[k].astype(jnp.bfloat16) for k in leaving]), "loc", bit
            )
            held = {
                k ^ bit: held[k ^ bit] + arrived[n].astype(jnp.float32)
                for n, k in enumerate(leaving)
            }
        return held[0]

    total = None
    back = []
    for s in shifts:
        back.append(shift_by(group_sum(s).astype(jnp.bfloat16), "grp", groups - s))
    total = group_sum(0)
    for value in back:
        total = total + value.astype(jnp.float32)
    return total.astype(jnp.bfloat16)


def solution(mesh):
    placed = (
        P(("grp", "tp"), None),
        P(("grp", "tp"), None),
        P(("grp", "tp"), None),
        P(("grp", "loc"), None, None),
        P(("grp", "loc"), None, None),
        P(("grp", "loc"), None, "tp"),
    )
    return jax.shard_map(
        body, mesh=mesh, in_specs=placed, out_specs=P(("grp", "tp"), "loc"), check_vma=False
    )
```

time: 192 us -> 130 us (0.68)
  waiting for transfers between devices: 110 us -> 33.3 us
  other arithmetic: 6.84 us -> 27.4 us
  local copies, waits for them, and re-layouts: 32.9 us -> 13.8 us
  starting transfers between devices: 11.1 us -> 28.8 us
  between operations: 13.5 us -> 0.42 us
  matrix products: 17.5 us -> 24.9 us
    all_to_all x2 -> x0, waiting for transfers between devices: 78.2 us -> none  [the longest x1 47.6 us: body(): lax.all_to_all(outgoing.reshape(groups, capacity, width_model), 'grp', sp...]
    ppermute x0 -> x24, waiting for transfers between devices: none -> 33.3 us  [the longest x9 17.3 us: shift_by(): lax.ppermute(value, axis, [(i, (i + step) % size) for i in range(size)])]
    reduce_scatter x1 -> x0, waiting for transfers between devices: 30.7 us -> none  [body(): summed = lax.psum_scatter(local_sum, 'loc', scatter_dimension=1, tiled=True)]
    ppermute x0 -> x24, starting transfers between devices: none -> 28.8 us  [the longest x9 16.7 us: shift_by(): lax.ppermute(value, axis, [(i, (i + step) % size) for i in range(size)])]
    unnamed x11 -> x36, local copies, waits for them, and re-layouts: 16.4 us -> 2.35 us
    concatenate x0 -> x6, other arithmetic: none -> 12.3 us  [whole_block(): got = jnp.concatenate([got, swap_bit(got, 'loc', bit)], axis=0)]
    all_to_all x2 -> x0, starting transfers between devices: 10.9 us -> none  [the longest x1 6.32 us: body(): lax.all_to_all(outgoing.reshape(groups, capacity, width_model), 'grp', sp...]
    scatter x2 -> x0, local copies, waits for them, and re-layouts: 9.15 us -> none  [the longest x1 8.04 us: body(): jnp.full((slot_total,), tok_rows, jnp.int32).at[slot_index]]
  transfers between devices with their start and end apart: 4 -> 24, of which waited for: 3 -> 10; matrix products, arithmetic and copies ran while one was open for 12% -> 41% of each run, Pallas kernels for 0% -> 0%
where the time goes in v1:
time: 130 us; the launch traced here: 129 us
  waiting for transfers between devices  33.3 us (26%)
  starting transfers between devices  28.8 us (22%)
  other arithmetic  27.4 us (21%)
  matrix products  24.9 us (19%)
  local copies, waits for them, and re-layouts  13.8 us (11%)
    ppermute x9, waiting for transfers between devices, shift_by(): lax.ppermute(value, axis, [(i, (i + step) % size) for i in range(size)])  17.3 us
    ppermute x9, starting transfers between devices, shift_by(): lax.ppermute(value, axis, [(i, (i + step) % size) for i in range(size)])  16.7 us
    ppermute x15, waiting for transfers between devices, swap_bit(): return lax.ppermute(value, axis, [(i, i ^ bit) for i in range(size)])  16 us
    dot_general x16, matrix products, group_sum(): result = jnp.dot(hidden[s], cols, preferred_element_type=jnp.float32)  15.5 us
    concatenate x6, other arithmetic, whole_block(): got = jnp.concatenate([got, swap_bit(got, 'loc', bit)], axis=0)  12.3 us
    ppermute x15, starting transfers between devices, swap_bit(): return lax.ppermute(value, axis, [(i, i ^ bit) for i in range(size)])  12.1 us
    gather x3, local copies, waits for them, and re-layouts, whole_block(): return jnp.take(got, take, axis=0).reshape(rows, width)  8.46 us
    dot_general x4, matrix products, ffn(): gate_act = jnp.dot(block, w_gate[0], preferred_element_type=jnp.float32)  5.19 us
  transfers between devices with their start and end apart: 24, of which 10 were waited for; matrix products, arithmetic and copies ran while one was open for 41% of the time, Pallas kernels for 0%

profile of v1, /device:TPU:0, one launch (start us, length us, event | category | flops | bytes accessed | tf_op | source)
XLA Modules:
  0.0 128.5 jit_solution(13099280325859839051)
XLA Ops:
  0.0 1.8 %constant_dynamic-slice_fusion = bf16[64,2048]{1,0:T(8,128)(2,1)} fusion(bf16[256,2048]{1,0:T(8,128)(2,1)} %param.11, s32[]{:T(128)S(6)} %select_n.94), kind=kLoop, calls=%fused_computation.182 | loop fusion | bytes 524292 | tf_op jit(solution)/shard_map/dynamic_slice | solution.py:33
  1.8 3.0 %collective-permute-start.10 = (bf16[64,2048]{1,0:T(8,128)(2,1)}, bf16[64,2048]{1,0:T(8,128)(2,1)}, u32[]{:S(2)}, u32[]{:S(2)}) collective-permute-start(bf16[64,2048]{1,0:T(8,128)(2,1)} %constant_dynamic-slice_fusion), channel_id=1, source_target_pairs={{0,8},{8,16},{16,24},{24,0},{1,9},{9,17},{17,25},{25,1},{2,10},{10... | collective-permute-start | bytes 786440 | tf_op jit(solution)/shard_map/ppermute | solution.py:14
  4.8 2.0 %collective-permute-start.17 = (bf16[64,2048]{1,0:T(8,128)(2,1)}, bf16[64,2048]{1,0:T(8,128)(2,1)}, u32[]{:S(2)}, u32[]{:S(2)}) collective-permute-start(bf16[64,2048]{1,0:T(8,128)(2,1)} %constant_dynamic-slice_fusion), channel_id=1, source_target_pairs={{0,24},{8,0},{16,8},{24,16},{1,25},{9,1},{17,9},{25,17},{2,26},{10... | collective-permute-start | bytes 786440 | tf_op jit(solution)/shard_map/ppermute | solution.py:14
  9.3 1.9 %collective-permute-start.6 = (bf16[256]{0:T(256)(128)(2,1)}, bf16[256]{0:T(256)(128)(2,1)}, u32[]{:S(2)}, u32[]{:S(2)}) collective-permute-start(bf16[256]{0:T(256)(128)(2,1)} %get-tuple-element.7), channel_id=1, source_target_pairs={{0,16},{8,24},{16,0},{24,8},{1,17},{9,25},{17,1},{25,9},{2,18},{10... | collective-permute-start | bytes 1544 | tf_op jit(solution)/shard_map/ppermute | solution.py:14
  11.3 2.2 %fusion.14 = f32[256,768]{1,0:T(8,128)S(1)} fusion(bf16[256,2048]{1,0:T(8,128)(2,1)} %param.11, bf16[1,2048,768]{2,1,0:T(8,128)(2,1)S(1)} %copy-done), kind=kOutput, calls=%fused_computation.19 | convolution fusion | flops 805306368 | bytes 4980736 | tf_op jit(solution)/shard_map/dot_general | solution.py:67
  15.7 1.7 %collective-permute-start.11 = (bf16[1,64,2048]{2,1,0:T(8,128)(2,1)}, bf16[1,64,2048]{2,1,0:T(8,128)(2,1)S(1)}, u32[]{:S(2)}, u32[]{:S(2)}) collective-permute-start(bf16[1,64,2048]{2,1,0:T(8,128)(2,1)} %bitcast.18), channel_id=1, source_target_pairs={{0,4},{2,6},{4,0},{6,2},{1,5},{3,7},{5,1},{7,3},{8,12},{10,14},{12... | collective-permute-start | bytes 786440 | tf_op jit(solution)/shard_map/ppermute | solution.py:9
  18.5 1.5 %collective-permute-start.18 = (bf16[1,64,2048]{2,1,0:T(8,128)(2,1)}, bf16[1,64,2048]{2,1,0:T(8,128)(2,1)S(1)}, u32[]{:S(2)}, u32[]{:S(2)}) collective-permute-start(bf16[1,64,2048]{2,1,0:T(8,128)(2,1)} %bitcast.26), channel_id=1, source_target_pairs={{0,4},{2,6},{4,0},{6,2},{1,5},{3,7},{5,1},{7,3},{8,12},{10,14},{12... | collective-permute-start | bytes 786440 | tf_op jit(solution)/shard_map/ppermute | solution.py:9
  21.2 9.2 %collective-permute-done.3 = bf16[64,2048]{1,0:T(8,128)(2,1)} collective-permute-done((bf16[64,2048]{1,0:T(8,128)(2,1)}, bf16[64,2048]{1,0:T(8,128)(2,1)}, u32[]{:S(2)}, u32[]{:S(2)}) %collective-permute-start.3) | collective-permute-done | bytes 262176 | tf_op jit(solution)/shard_map/ppermute | solution.py:14
  31.9 1.9 %pad_maximum_fusion.6 = bf16[2,64,2048]{2,1,0:T(8,128)(2,1)} fusion(bf16[1,64,2048]{2,1,0:T(8,128)(2,1)S(1)} %collective-permute-done.11, bf16[1,64,2048]{2,1,0:T(8,128)(2,1)} %bitcast.18), kind=kLoop, calls=%fused_computation.129 | loop fusion | flops 262144 | bytes 1048576 | tf_op jit(solution)/shard_map/concatenate | solution.py:58
  34.5 1.8 %pad_maximum_fusion.8 = bf16[2,64,2048]{2,1,0:T(8,128)(2,1)} fusion(bf16[1,64,2048]{2,1,0:T(8,128)(2,1)S(1)} %collective-permute-done.18, bf16[1,64,2048]{2,1,0:T(8,128)(2,1)} %bitcast.26), kind=kLoop, calls=%fused_computation.131 | loop fusion | flops 262144 | bytes 1048576 | tf_op jit(solution)/shard_map/concatenate | solution.py:58
  36.8 2.0 %collective-permute-done.4 = bf16[1,64,2048]{2,1,0:T(8,128)(2,1)S(1)} collective-permute-done((bf16[1,64,2048]{2,1,0:T(8,128)(2,1)}, bf16[1,64,2048]{2,1,0:T(8,128)(2,1)S(1)}, u32[]{:S(2)}, u32[]{:S(2)}) %collective-permute-start.4) | collective-permute-done | bytes 262176 | tf_op jit(solution)/shard_map/ppermute | solution.py:9
  39.5 1.8 %pad_maximum_fusion.4 = bf16[2,64,2048]{2,1,0:T(8,128)(2,1)} fusion(bf16[1,64,2048]{2,1,0:T(8,128)(2,1)S(1)} %collective-permute-done.4, bf16[1,64,2048]{2,1,0:T(8,128)(2,1)} %bitcast.10), kind=kLoop, calls=%fused_computation.127 | loop fusion | flops 262144 | bytes 1048576 | tf_op jit(solution)/shard_map/concatenate | solution.py:58
  46.8 2.3 %pad_maximum_fusion.1 = bf16[4,64,2048]{2,1,0:T(8,128)(2,1)} fusion(bf16[2,64,2048]{2,1,0:T(8,128)(2,1)} %collective-permute-done.12, bf16[1,64,2048]{2,1,0:T(8,128)(2,1)} %copy-done.13, bf16[1,64,2048]{2,1,0:T(8,128)(2,1)} %bitcast.18), kind=kLoop, calls=%fused_computation.121 | loop fusion | flops 1048576 | bytes 2097152 | tf_op jit(solution)/shard_map/concatenate | solution.py:58
  49.1 2.8 %gather_fusion.2 = bf16[4,64,2048]{2,1,0:T(8,128)(2,1)} fusion(bf16[4,64,2048]{2,1,0:T(8,128)(2,1)} %pad_maximum_fusion.1, s32[1024]{0:T(1024)S(1)} %pad_clamp_fusion), kind=kCustom, calls=%fused_computation.1.clone | custom fusion | bytes 2097168 | tf_op jit(solution)/shard_map/jit(_take)/gather | solution.py:64
  51.9 2.3 %pad_maximum_fusion.2 = bf16[4,64,2048]{2,1,0:T(8,128)(2,1)} fusion(bf16[2,64,2048]{2,1,0:T(8,128)(2,1)} %collective-permute-done.19, bf16[1,64,2048]{2,1,0:T(8,128)(2,1)} %copy-done.11, bf16[1,64,2048]{2,1,0:T(8,128)(2,1)} %bitcast.26), kind=kLoop, calls=%fused_computation.122 | loop fusion | flops 1048576 | bytes 2097152 | tf_op jit(solution)/shard_map/concatenate | solution.py:58
  54.2 2.8 %gather_fusion.3 = bf16[4,64,2048]{2,1,0:T(8,128)(2,1)} fusion(bf16[4,64,2048]{2,1,0:T(8,128)(2,1)} %pad_maximum_fusion.2, s32[1024]{0:T(1024)S(1)} %pad_clamp_fusion), kind=kCustom, calls=%fused_computation.2.clone | custom fusion | bytes 2097168 | tf_op jit(solution)/shard_map/jit(_take)/gather | solution.py:64
  57.0 2.3 %pad_maximum_fusion = bf16[4,64,2048]{2,1,0:T(8,128)(2,1)} fusion(bf16[2,64,2048]{2,1,0:T(8,128)(2,1)} %collective-permute-done.5, bf16[1,64,2048]{2,1,0:T(8,128)(2,1)} %copy-done.12, bf16[1,64,2048]{2,1,0:T(8,128)(2,1)} %bitcast.10), kind=kLoop, calls=%fused_computation.120 | loop fusion | flops 1048576 | bytes 2097152 | tf_op jit(solution)/shard_map/concatenate | solution.py:58
  59.3 2.8 %gather_fusion.1 = bf16[4,64,2048]{2,1,0:T(8,128)(2,1)} fusion(bf16[4,64,2048]{2,1,0:T(8,128)(2,1)} %pad_maximum_fusion, s32[1024]{0:T(1024)S(1)} %pad_clamp_fusion), kind=kCustom, calls=%fused_computation.clone | custom fusion | bytes 2097168 | tf_op jit(solution)/shard_map/jit(_take)/gather | solution.py:64
  62.1 2.2 %broadcast_select_fusion.2 = (bf16[4,64,2048]{2,1,0:T(8,128)(2,1)S(1)}, bf16[4,64,2048]{2,1,0:T(8,128)(2,1)S(1)}, bf16[4,64,2048]{2,1,0:T(8,128)(2,1)S(1)}) fusion(bf16[4,64,2048]{2,1,0:T(8,128)(2,1)} %gather_fusion.1, pred[4]{0:T(512)(128)(4,1)} %compare_and_fusion, bf16[4,64,2048]{2,1,0:T(8,128)(2,1)} %gather_fusion.2, bf16[4,64,2048]{2,1,0:T(8,128)(2,1)} %gather_fusion.3), kind=kLoop, calls=%fused_computation.125 | loop fusion | flops 1572864 | bytes 6291460 | tf_op jit(solution)/shard_map/jit(_take)/select_n | solution.py:64
  71.4 9.5 %collective-permute-done = bf16[768,1024]{1,0:T(8,128)(2,1)} collective-permute-done((bf16[768,1024]{1,0:T(8,128)(2,1)}, bf16[768,1024]{1,0:T(8,128)(2,1)}, u32[]{:S(2)}, u32[]{:S(2)}) %collective-permute-start) | collective-permute-done | bytes 1572896 | tf_op jit(solution)/shard_map/ppermute | solution.py:9
  80.9 3.2 %maximum_select_fusion = bf16[768,2048]{1,0:T(8,128)(2,1)S(1)} fusion(bf16[768,1024]{1,0:T(8,128)(2,1)S(1)} %bitcast.144, bf16[768,1024]{1,0:T(8,128)(2,1)} %collective-permute-done, pred[]{:T(512)S(6)} %gt.3), kind=kLoop, calls=%fused_computation.4 | loop fusion | flops 14155776 | bytes 6291457 | tf_op jit(solution)/shard_map/jit(_where)/select_n | solution.py:48
  91.7 1.8 %fusion.105 = bf16[1,256,512]{2,1,0:T(8,128)(2,1)S(1)} fusion(bf16[256,768]{1,0:T(8,128)(2,1)} %copy-done.9, bf16[768,2048]{1,0:T(8,128)(2,1)} %copy-done.2, s32[]{:T(128)S(6)} %select_n.93, bf16[2,256,512]{2,1,0:T(8,128)(2,1)} %collective-permute-done.7, f32[256]{0:T(256)S(1)} %copy-done.15), kind=kOutput, calls=%fused_computation.110 | convolution fusion | flops 202113024 | bytes 1704964 | tf_op jit(solution)/shard_map/dot_general | solution.py:81
  93.5 1.6 %collective-permute-start.8 = (bf16[1,256,512]{2,1,0:T(8,128)(2,1)S(1)}, bf16[1,256,512]{2,1,0:T(8,128)(2,1)S(1)}, u32[]{:S(2)}, u32[]{:S(2)}) collective-permute-start(bf16[1,256,512]{2,1,0:T(8,128)(2,1)S(1)} %fusion.105), channel_id=1, source_target_pairs={{0,4},{2,6},{4,0},{6,2},{1,5},{3,7},{5,1},{7,3},{8,12},{10,14},{12... | collective-permute-start | bytes 786440 | tf_op jit(solution)/shard_map/ppermute | solution.py:9
  95.1 1.7 %fusion.104 = bf16[1,256,512]{2,1,0:T(8,128)(2,1)S(1)} fusion(bf16[256,768]{1,0:T(8,128)(2,1)} %copy-done.7, bf16[768,2048]{1,0:T(8,128)(2,1)} %copy-done.2, s32[]{:T(128)S(6)} %select_n.93, bf16[2,256,512]{2,1,0:T(8,128)(2,1)} %collective-permute-done.14, f32[256]{0:T(256)S(1)} %convert_element_type.322), kind=kOutput, calls=%fused_computation.109 | convolution fusion | flops 202113024 | bytes 1704964 | tf_op jit(solution)/shard_map/dot_general | solution.py:81
  98.8 1.6 %collective-permute-start.22 = (bf16[1,256,512]{2,1,0:T(8,128)(2,1)S(1)}, bf16[1,256,512]{2,1,0:T(8,128)(2,1)S(1)}, u32[]{:S(2)}, u32[]{:S(2)}) collective-permute-start(bf16[1,256,512]{2,1,0:T(8,128)(2,1)S(1)} %fusion.103), channel_id=1, source_target_pairs={{0,4},{2,6},{4,0},{6,2},{1,5},{3,7},{5,1},{7,3},{8,12},{10,14},{12... | collective-permute-start | bytes 786440 | tf_op jit(solution)/shard_map/ppermute | solution.py:9
  104.1 2.6 %collective-permute-start.9 = (bf16[256,512]{1,0:T(8,128)(2,1)S(1)}, bf16[256,512]{1,0:T(8,128)(2,1)S(1)}, u32[]{:S(2)}, u32[]{:S(2)}) collective-permute-start(bf16[256,512]{1,0:T(8,128)(2,1)S(1)} %fusion.62), channel_id=1, source_target_pairs={{0,16},{8,24},{16,0},{24,8},{1,17},{9,25},{17,1},{25,9},{2,18},{10... | collective-permute-start | bytes 786440 | tf_op jit(solution)/shard_map/ppermute | solution.py:14
  106.8 1.6 %collective-permute-done.15 = bf16[1,256,512]{2,1,0:T(8,128)(2,1)S(1)} collective-permute-done((bf16[1,256,512]{2,1,0:T(8,128)(2,1)S(1)}, bf16[1,256,512]{2,1,0:T(8,128)(2,1)S(1)}, u32[]{:S(2)}, u32[]{:S(2)}) %collective-permute-start.15) | collective-permute-done | bytes 262176 | tf_op jit(solution)/shard_map/ppermute | solution.py:9
  109.8 3.8 %collective-permute-start.16 = (bf16[256,512]{1,0:T(8,128)(2,1)S(1)}, bf16[256,512]{1,0:T(8,128)(2,1)S(1)}, u32[]{:S(2)}, u32[]{:S(2)}) collective-permute-start(bf16[256,512]{1,0:T(8,128)(2,1)S(1)} %fusion.77), channel_id=1, source_target_pairs={{0,24},{8,0},{16,8},{24,16},{1,25},{9,1},{17,9},{25,17},{2,26},{10... | collective-permute-start | bytes 786440 | tf_op jit(solution)/shard_map/ppermute | solution.py:14
  116.9 1.8 %collective-permute-done.2 = bf16[1,256,512]{2,1,0:T(8,128)(2,1)S(1)} collective-permute-done((bf16[1,256,512]{2,1,0:T(8,128)(2,1)S(1)}, bf16[1,256,512]{2,1,0:T(8,128)(2,1)S(1)}, u32[]{:S(2)}, u32[]{:S(2)}) %collective-permute-start.2) | collective-permute-done | bytes 262176 | tf_op jit(solution)/shard_map/ppermute | solution.py:9
  118.7 5.6 %collective-permute-done.9 = bf16[256,512]{1,0:T(8,128)(2,1)S(1)} collective-permute-done((bf16[256,512]{1,0:T(8,128)(2,1)S(1)}, bf16[256,512]{1,0:T(8,128)(2,1)S(1)}, u32[]{:S(2)}, u32[]{:S(2)}) %collective-permute-start.9) | collective-permute-done | bytes 262176 | tf_op jit(solution)/shard_map/ppermute | solution.py:14
  124.3 2.1 %collective-permute-done.16 = bf16[256,512]{1,0:T(8,128)(2,1)S(1)} collective-permute-done((bf16[256,512]{1,0:T(8,128)(2,1)S(1)}, bf16[256,512]{1,0:T(8,128)(2,1)S(1)}, u32[]{:S(2)}, u32[]{:S(2)}) %collective-permute-start.16) | collective-permute-done | bytes 262176 | tf_op jit(solution)/shard_map/ppermute | solution.py:14
  126.4 2.2 %fusion.47 = bf16[256,512]{1,0:T(8,128)(2,1)} fusion(bf16[256,768]{1,0:T(8,128)(2,1)S(1)} %fusion.37, bf16[256,512]{1,0:T(8,128)(2,1)S(1)} %collective-permute-done.23, bf16[256,512]{1,0:T(8,128)(2,1)S(1)} %collective-permute-done.16, bf16[256,512]{1,0:T(8,128)(2,1)S(1)} %collective-permute-done.9, bf16[768,2048]{1,0:T(8,128)(2,1)S(1)} %copy-done.3, ...), kind=kOutput, calls=%fused_computation.52 | convolution fusion | flops 203161600 | bytes 2753540 | tf_op jit(solution)/shard_map/dot_general | solution.py:81
  (103 shorter events, 40.7 us)
Async XLA Ops:
  0.0 11.3 %copy-start = (bf16[1,2048,768]{2,1,0:T(8,128)(2,1)S(1)}, bf16[1,2048,768]{2,1,0:T(8,128)(2,1)}, u32[]{:S(2)}) copy-start(bf16[1,2048,768]{2,1,0:T(8,128)(2,1)} %param.14) | copy-start | bytes 9437188
  1.8 13.9 %collective-permute-start.10 = (bf16[64,2048]{1,0:T(8,128)(2,1)}, bf16[64,2048]{1,0:T(8,128)(2,1)}, u32[]{:S(2)}, u32[]{:S(2)}) collective-permute-start(bf16[64,2048]{1,0:T(8,128)(2,1)} %constant_dynamic-slice_fusion), channel_id=1, source_target_pairs={{0,8},{8,16},{16,24},{24,0},{1,9},{9,17},{17,25},{25,1},{2,10},{10... | collective-permute-start | bytes 786440 | tf_op jit(solution)/shard_map/ppermute | solution.py:14
  4.8 13.7 %collective-permute-start.17 = (bf16[64,2048]{1,0:T(8,128)(2,1)}, bf16[64,2048]{1,0:T(8,128)(2,1)}, u32[]{:S(2)}, u32[]{:S(2)}) collective-permute-start(bf16[64,2048]{1,0:T(8,128)(2,1)} %constant_dynamic-slice_fusion), channel_id=1, source_target_pairs={{0,24},{8,0},{16,8},{24,16},{1,25},{9,1},{17,9},{25,17},{2,26},{10... | collective-permute-start | bytes 786440 | tf_op jit(solution)/shard_map/ppermute | solution.py:14
  6.9 23.5 %collective-permute-start.3 = (bf16[64,2048]{1,0:T(8,128)(2,1)}, bf16[64,2048]{1,0:T(8,128)(2,1)}, u32[]{:S(2)}, u32[]{:S(2)}) collective-permute-start(bf16[64,2048]{1,0:T(8,128)(2,1)} %constant_dynamic-slice_fusion), channel_id=1, source_target_pairs={{0,16},{8,24},{16,0},{24,8},{1,17},{9,25},{17,1},{25,9},{2,18},{10... | collective-permute-start | bytes 786440 | tf_op jit(solution)/shard_map/ppermute | solution.py:14
  9.3 32.0 %collective-permute-start.6 = (bf16[256]{0:T(256)(128)(2,1)}, bf16[256]{0:T(256)(128)(2,1)}, u32[]{:S(2)}, u32[]{:S(2)}) collective-permute-start(bf16[256]{0:T(256)(128)(2,1)} %get-tuple-element.7), channel_id=1, source_target_pairs={{0,16},{8,24},{16,0},{24,8},{1,17},{9,25},{17,1},{25,9},{2,18},{10... | collective-permute-start | bytes 1544 | tf_op jit(solution)/shard_map/ppermute | solution.py:14
  11.2 32.8 %collective-permute-start.13 = (bf16[256]{0:T(256)(128)(2,1)S(1)}, bf16[256]{0:T(256)(128)(2,1)}, u32[]{:S(2)}, u32[]{:S(2)}) collective-permute-start(bf16[256]{0:T(256)(128)(2,1)S(1)} %get-tuple-element.8), channel_id=1, source_target_pairs={{0,8},{8,16},{16,24},{24,0},{1,9},{9,17},{17,25},{25,1},{2,10},{10... | collective-permute-start | bytes 1544 | tf_op jit(solution)/shard_map/ppermute | solution.py:14
  15.7 16.2 %collective-permute-start.11 = (bf16[1,64,2048]{2,1,0:T(8,128)(2,1)}, bf16[1,64,2048]{2,1,0:T(8,128)(2,1)S(1)}, u32[]{:S(2)}, u32[]{:S(2)}) collective-permute-start(bf16[1,64,2048]{2,1,0:T(8,128)(2,1)} %bitcast.18), channel_id=1, source_target_pairs={{0,4},{2,6},{4,0},{6,2},{1,5},{3,7},{5,1},{7,3},{8,12},{10,14},{12... | collective-permute-start | bytes 786440 | tf_op jit(solution)/shard_map/ppermute | solution.py:9
  18.5 15.2 %collective-permute-start.18 = (bf16[1,64,2048]{2,1,0:T(8,128)(2,1)}, bf16[1,64,2048]{2,1,0:T(8,128)(2,1)S(1)}, u32[]{:S(2)}, u32[]{:S(2)}) collective-permute-start(bf16[1,64,2048]{2,1,0:T(8,128)(2,1)} %bitcast.26), channel_id=1, source_target_pairs={{0,4},{2,6},{4,0},{6,2},{1,5},{3,7},{5,1},{7,3},{8,12},{10,14},{12... | collective-permute-start | bytes 786440 | tf_op jit(solution)/shard_map/ppermute | solution.py:9
  30.4 8.4 %collective-permute-start.4 = (bf16[1,64,2048]{2,1,0:T(8,128)(2,1)}, bf16[1,64,2048]{2,1,0:T(8,128)(2,1)S(1)}, u32[]{:S(2)}, u32[]{:S(2)}) collective-permute-start(bf16[1,64,2048]{2,1,0:T(8,128)(2,1)} %bitcast.10), channel_id=1, source_target_pairs={{0,4},{2,6},{4,0},{6,2},{1,5},{3,7},{5,1},{7,3},{8,12},{10,14},{12... | collective-permute-start | bytes 786440 | tf_op jit(solution)/shard_map/ppermute | solution.py:9
  33.8 13.0 %collective-permute-start.12 = (bf16[2,64,2048]{2,1,0:T(8,128)(2,1)}, bf16[2,64,2048]{2,1,0:T(8,128)(2,1)}, u32[]{:S(2)}, u32[]{:S(2)}) collective-permute-start(bf16[2,64,2048]{2,1,0:T(8,128)(2,1)} %pad_maximum_fusion.6), channel_id=1, source_target_pairs={{0,2},{2,0},{4,6},{6,4},{1,3},{3,1},{5,7},{7,5},{8,10},{10,8},{12,... | collective-permute-start | bytes 1572872 | tf_op jit(solution)/shard_map/ppermute | solution.py:9
  36.3 15.6 %collective-permute-start.19 = (bf16[2,64,2048]{2,1,0:T(8,128)(2,1)}, bf16[2,64,2048]{2,1,0:T(8,128)(2,1)}, u32[]{:S(2)}, u32[]{:S(2)}) collective-permute-start(bf16[2,64,2048]{2,1,0:T(8,128)(2,1)} %pad_maximum_fusion.8), channel_id=1, source_target_pairs={{0,2},{2,0},{4,6},{6,4},{1,3},{3,1},{5,7},{7,5},{8,10},{10,8},{12,... | collective-permute-start | bytes 1572872 | tf_op jit(solution)/shard_map/ppermute | solution.py:9
  41.3 15.7 %collective-permute-start.5 = (bf16[2,64,2048]{2,1,0:T(8,128)(2,1)}, bf16[2,64,2048]{2,1,0:T(8,128)(2,1)}, u32[]{:S(2)}, u32[]{:S(2)}) collective-permute-start(bf16[2,64,2048]{2,1,0:T(8,128)(2,1)} %pad_maximum_fusion.4), channel_id=1, source_target_pairs={{0,2},{2,0},{4,6},{6,4},{1,3},{3,1},{5,7},{7,5},{8,10},{10,8},{12,... | collective-permute-start | bytes 1572872 | tf_op jit(solution)/shard_map/ppermute | solution.py:9
  41.4 4.8 %collective-permute-start.20 = (bf16[256]{0:T(256)(128)(2,1)S(1)}, bf16[256]{0:T(256)(128)(2,1)}, u32[]{:S(2)}, u32[]{:S(2)}) collective-permute-start(bf16[256]{0:T(256)(128)(2,1)S(1)} %get-tuple-element.9), channel_id=1, source_target_pairs={{0,24},{8,0},{16,8},{24,16},{1,25},{9,1},{17,9},{25,17},{2,26},{10... | collective-permute-start | bytes 1544 | tf_op jit(solution)/shard_map/ppermute | solution.py:14
  44.1 36.8 %collective-permute-start = (bf16[768,1024]{1,0:T(8,128)(2,1)}, bf16[768,1024]{1,0:T(8,128)(2,1)}, u32[]{:S(2)}, u32[]{:S(2)}) collective-permute-start(bf16[768,1024]{1,0:T(8,128)(2,1)} %bitcast.143), channel_id=1, source_target_pairs={{0,1},{1,0},{2,3},{3,2},{4,5},{5,4},{6,7},{7,6},{8,9},{9,8},{10,11... | collective-permute-start | bytes 4718600 | tf_op jit(solution)/shard_map/ppermute | solution.py:9
  69.3 15.2 %copy-start.9 = (bf16[256,768]{1,0:T(8,128)(2,1)}, bf16[256,768]{1,0:T(8,128)(2,1)S(1)}, u32[]{:S(2)}) copy-start(bf16[256,768]{1,0:T(8,128)(2,1)S(1)} %fusion.34) | copy-start | bytes 1179652
  70.3 15.0 %copy-start.7 = (bf16[256,768]{1,0:T(8,128)(2,1)}, bf16[256,768]{1,0:T(8,128)(2,1)S(1)}, u32[]{:S(2)}) copy-start(bf16[256,768]{1,0:T(8,128)(2,1)S(1)} %fusion.31) | copy-start | bytes 1179652
  70.3 10.6 %copy-start.4 = (bf16[1,768,1024]{2,1,0:T(8,128)(2,1)S(1)}, bf16[1,768,1024]{2,1,0:T(8,128)(2,1)}, u32[]{:S(2)}) copy-start(bf16[1,768,1024]{2,1,0:T(8,128)(2,1)} %param.16) | copy-start | bytes 4718596
  71.4 14.7 %copy-start.5 = (bf16[256,768]{1,0:T(8,128)(2,1)}, bf16[256,768]{1,0:T(8,128)(2,1)S(1)}, u32[]{:S(2)}) copy-start(bf16[256,768]{1,0:T(8,128)(2,1)S(1)} %fusion.28) | copy-start | bytes 1179652
  71.4 12.7 %copy-start.15 = (f32[256]{0:T(256)S(1)}, f32[256]{0:T(256)}, u32[]{:S(2)}) copy-start(f32[256]{0:T(256)} %convert_element_type.300) | copy-start | bytes 3076
  87.4 4.4 %collective-permute-start.7 = (bf16[2,256,512]{2,1,0:T(8,128)(2,1)}, bf16[2,256,512]{2,1,0:T(8,128)(2,1)}, u32[]{:S(2)}, u32[]{:S(2)}) collective-permute-start(bf16[2,256,512]{2,1,0:T(8,128)(2,1)} %pad_maximum_fusion.5), channel_id=1, source_target_pairs={{0,2},{2,0},{4,6},{6,4},{1,3},{3,1},{5,7},{7,5},{8,10},{10,8},{12,... | collective-permute-start | bytes 1572872 | tf_op jit(solution)/shard_map/ppermute | solution.py:9
  88.2 6.9 %collective-permute-start.14 = (bf16[2,256,512]{2,1,0:T(8,128)(2,1)}, bf16[2,256,512]{2,1,0:T(8,128)(2,1)}, u32[]{:S(2)}, u32[]{:S(2)}) collective-permute-start(bf16[2,256,512]{2,1,0:T(8,128)(2,1)} %pad_maximum_fusion.7), channel_id=1, source_target_pairs={{0,2},{2,0},{4,6},{6,4},{1,3},{3,1},{5,7},{7,5},{8,10},{10,8},{12,... | collective-permute-start | bytes 1572872 | tf_op jit(solution)/shard_map/ppermute | solution.py:9
  89.5 7.9 %collective-permute-start.21 = (bf16[2,256,512]{2,1,0:T(8,128)(2,1)}, bf16[2,256,512]{2,1,0:T(8,128)(2,1)}, u32[]{:S(2)}, u32[]{:S(2)}) collective-permute-start(bf16[2,256,512]{2,1,0:T(8,128)(2,1)} %pad_maximum_fusion.9), channel_id=1, source_target_pairs={{0,2},{2,0},{4,6},{6,4},{1,3},{3,1},{5,7},{7,5},{8,10},{10,8},{12,... | collective-permute-start | bytes 1572872 | tf_op jit(solution)/shard_map/ppermute | solution.py:9
  91.2 9.1 %collective-permute-start.1 = (bf16[2,256,512]{2,1,0:T(8,128)(2,1)}, bf16[2,256,512]{2,1,0:T(8,128)(2,1)}, u32[]{:S(2)}, u32[]{:S(2)}) collective-permute-start(bf16[2,256,512]{2,1,0:T(8,128)(2,1)} %pad_maximum_fusion.3), channel_id=1, source_target_pairs={{0,2},{2,0},{4,6},{6,4},{1,3},{3,1},{5,7},{7,5},{8,10},{10,8},{12,... | collective-permute-start | bytes 1572872 | tf_op jit(solution)/shard_map/ppermute | solution.py:9
  91.7 11.1 %copy-start.10 = (bf16[256,768]{1,0:T(8,128)(2,1)S(1)}, bf16[256,768]{1,0:T(8,128)(2,1)}, u32[]{:S(2)}) copy-start(bf16[256,768]{1,0:T(8,128)(2,1)} %copy-done.9) | copy-start | bytes 1179652
  93.5 9.2 %collective-permute-start.8 = (bf16[1,256,512]{2,1,0:T(8,128)(2,1)S(1)}, bf16[1,256,512]{2,1,0:T(8,128)(2,1)S(1)}, u32[]{:S(2)}, u32[]{:S(2)}) collective-permute-start(bf16[1,256,512]{2,1,0:T(8,128)(2,1)S(1)} %fusion.105), channel_id=1, source_target_pairs={{0,4},{2,6},{4,0},{6,2},{1,5},{3,7},{5,1},{7,3},{8,12},{10,14},{12... | collective-permute-start | bytes 786440 | tf_op jit(solution)/shard_map/ppermute | solution.py:9
  96.8 11.6 %copy-start.8 = (bf16[256,768]{1,0:T(8,128)(2,1)S(1)}, bf16[256,768]{1,0:T(8,128)(2,1)}, u32[]{:S(2)}) copy-start(bf16[256,768]{1,0:T(8,128)(2,1)} %copy-done.7) | copy-start | bytes 1179652
  96.8 11.6 %collective-permute-start.15 = (bf16[1,256,512]{2,1,0:T(8,128)(2,1)S(1)}, bf16[1,256,512]{2,1,0:T(8,128)(2,1)S(1)}, u32[]{:S(2)}, u32[]{:S(2)}) collective-permute-start(bf16[1,256,512]{2,1,0:T(8,128)(2,1)S(1)} %fusion.104), channel_id=1, source_target_pairs={{0,4},{2,6},{4,0},{6,2},{1,5},{3,7},{5,1},{7,3},{8,12},{10,14},{12... | collective-permute-start | bytes 786440 | tf_op jit(solution)/shard_map/ppermute | solution.py:9
  98.8 15.3 %collective-permute-start.22 = (bf16[1,256,512]{2,1,0:T(8,128)(2,1)S(1)}, bf16[1,256,512]{2,1,0:T(8,128)(2,1)S(1)}, u32[]{:S(2)}, u32[]{:S(2)}) collective-permute-start(bf16[1,256,512]{2,1,0:T(8,128)(2,1)S(1)} %fusion.103), channel_id=1, source_target_pairs={{0,4},{2,6},{4,0},{6,2},{1,5},{3,7},{5,1},{7,3},{8,12},{10,14},{12... | collective-permute-start | bytes 786440 | tf_op jit(solution)/shard_map/ppermute | solution.py:9
  101.7 17.0 %collective-permute-start.2 = (bf16[1,256,512]{2,1,0:T(8,128)(2,1)S(1)}, bf16[1,256,512]{2,1,0:T(8,128)(2,1)S(1)}, u32[]{:S(2)}, u32[]{:S(2)}) collective-permute-start(bf16[1,256,512]{2,1,0:T(8,128)(2,1)S(1)} %fusion.106), channel_id=1, source_target_pairs={{0,4},{2,6},{4,0},{6,2},{1,5},{3,7},{5,1},{7,3},{8,12},{10,14},{12... | collective-permute-start | bytes 786440 | tf_op jit(solution)/shard_map/ppermute | solution.py:9
  104.1 20.1 %collective-permute-start.9 = (bf16[256,512]{1,0:T(8,128)(2,1)S(1)}, bf16[256,512]{1,0:T(8,128)(2,1)S(1)}, u32[]{:S(2)}, u32[]{:S(2)}) collective-permute-start(bf16[256,512]{1,0:T(8,128)(2,1)S(1)} %fusion.62), channel_id=1, source_target_pairs={{0,16},{8,24},{16,0},{24,8},{1,17},{9,25},{17,1},{25,9},{2,18},{10... | collective-permute-start | bytes 786440 | tf_op jit(solution)/shard_map/ppermute | solution.py:14
  109.8 16.6 %collective-permute-start.16 = (bf16[256,512]{1,0:T(8,128)(2,1)S(1)}, bf16[256,512]{1,0:T(8,128)(2,1)S(1)}, u32[]{:S(2)}, u32[]{:S(2)}) collective-permute-start(bf16[256,512]{1,0:T(8,128)(2,1)S(1)} %fusion.77), channel_id=1, source_target_pairs={{0,24},{8,0},{16,8},{24,16},{1,25},{9,1},{17,9},{25,17},{2,26},{10... | collective-permute-start | bytes 786440 | tf_op jit(solution)/shard_map/ppermute | solution.py:14
  115.4 11.0 %collective-permute-start.23 = (bf16[256,512]{1,0:T(8,128)(2,1)S(1)}, bf16[256,512]{1,0:T(8,128)(2,1)S(1)}, u32[]{:S(2)}, u32[]{:S(2)}) collective-permute-start(bf16[256,512]{1,0:T(8,128)(2,1)S(1)} %fusion.92), channel_id=1, source_target_pairs={{0,8},{8,16},{16,24},{24,0},{1,9},{9,17},{17,25},{25,1},{2,10},{10... | collective-permute-start | bytes 786440 | tf_op jit(solution)/shard_map/ppermute | solution.py:14
  (10 other events, 42.2 us)

commit v2 on v1

v2 whole, which is shorter than its diff:
```python
import functools

import jax
import jax.numpy as jnp
from jax import lax
from jax.experimental import pallas as pl
from jax.experimental.pallas import tpu as pltpu
from jax.sharding import PartitionSpec as P

VM = pl.BlockSpec(memory_space=pltpu.VMEM)
SM = pl.BlockSpec(memory_space=pltpu.SMEM)
STEP = 256


def swap_bit(value, axis, bit):
    size = lax.axis_size(axis)
    return lax.ppermute(value, axis, [(i, i ^ bit) for i in range(size)])


def shift_by(value, axis, step):
    size = lax.axis_size(axis)
    return lax.ppermute(value, axis, [(i, (i + step) % size) for i in range(size)])


def bits_of(size):
    return [1 << i for i in range(size.bit_length() - 1)]


def part_order(size):
    order = [0]
    for bit in reversed(bits_of(size)):
        order = order + [i ^ bit for i in order]
    return order


def call(kernel, outs, scratch, scalars, *arrays):
    return pl.pallas_call(
        kernel,
        out_shape=outs,
        in_specs=[SM] + [VM] * len(arrays),
        out_specs=jax.tree.map(lambda _: VM, outs),
        scratch_shapes=scratch,
        compiler_params=pltpu.CompilerParams(vmem_limit_bytes=40 << 20),
    )(scalars, *arrays)


def rows_at(index, part):
    return pl.ds(pl.multiple_of(index * part, part), part)


def hidden_kernel(order, part, scalars, *refs):
    *pieces, gate, up, hidden, block = refs
    for n, k in enumerate(order):
        if len(pieces) == 1:
            block[n * part : (n + 1) * part, :] = pieces[0][rows_at(scalars[0] ^ k, part), :]
        else:
            block[n * part : (n + 1) * part, :] = pieces[n][...]
    for j in range(0, gate.shape[1], STEP):
        a = jnp.dot(block[...], gate[:, j : j + STEP], preferred_element_type=jnp.float32)
        b = jnp.dot(block[...], up[:, j : j + STEP], preferred_element_type=jnp.float32)
        hidden[:, j : j + STEP] = (a / (1.0 + jnp.exp(-a)) * b).astype(jnp.bfloat16)


def scaled(hidden, weights, scale, j):
    out = jnp.dot(hidden[...], weights[:, j : j + STEP], preferred_element_type=jnp.float32)
    return out.astype(jnp.bfloat16).astype(jnp.float32) * scale


def scale_rows(scalars, scale, order, part):
    return jnp.concatenate([scale[rows_at(scalars[0] ^ k, part), :] for k in order], axis=0)


def leave_kernel(order, part, bit, scalars, hidden, scale, *refs):
    *columns, message = refs
    factor = scale_rows(scalars, scale, order, part)
    for u, weights in enumerate(columns):
        place = scalars[1] ^ u
        for j in range(0, weights.shape[1], STEP):
            value = scaled(hidden, weights, factor, j).astype(jnp.bfloat16)
            for n, k in enumerate(order):
                m = order.index(k ^ bit)
                message[place, n * part : (n + 1) * part, j : j + STEP] = value[m * part : (m + 1) * part]


def stay_kernel(order, part, bit, with_sum, scalars, hidden, scale, *refs):
    if with_sum:
        arrived, *refs = refs
    *columns, keep, message, total = refs
    half = len(columns) // 2
    factor = scale_rows(scalars, scale, order, part)
    for u, weights in enumerate(columns):
        place = scalars[1] ^ u
        for j in range(0, weights.shape[1], STEP):
            value = scaled(hidden, weights, factor, j)
            if with_sum:
                value = value + arrived[place, :, j : j + STEP].astype(jnp.float32)
            total[place, :, j : j + STEP] = value
    for i in range(half):
        keep[i] = total[i]
        for n, k in enumerate(order):
            m = order.index(k ^ bit)
            message[i, n * part : (n + 1) * part, :] = total[half + i, m * part : (m + 1) * part, :].astype(
                jnp.bfloat16
            )


def finish_kernel(order, part, scalars, keep, arrived, *refs):
    *others, out = refs
    for n, k in enumerate(order):
        at = slice(n * part, (n + 1) * part)
        value = keep[at, :] + arrived[at, :].astype(jnp.float32)
        for other in others:
            value = value + other[at, :].astype(jnp.float32)
        out[rows_at(scalars[0] ^ k, part), :] = value.astype(jnp.bfloat16)


def body(tokens, expert_ids, router_weights, w_gate, w_up, w_down):
    groups = lax.axis_size("grp")
    group_size = lax.axis_size("loc")
    tp_size = lax.axis_size("tp")
    own_group = lax.axis_index("grp")
    own_local = lax.axis_index("loc")
    own_tp = lax.axis_index("tp")
    rows, width = tokens.shape
    hidden_width = w_gate.shape[2]
    part = rows // group_size
    out_cols = width // group_size
    per_shard = group_size // tp_size
    order = part_order(group_size)
    shifts = sorted(range(1, groups), key=lambda s: -min(s, groups - s))
    scalars = jnp.stack([own_local, own_tp ^ (own_local // per_shard)]).astype(jnp.int32)

    down = []
    for j in reversed(range(per_shard)):
        start = ((own_local % per_shard) ^ j) * out_cols
        held = [lax.dynamic_slice_in_dim(w_down[0], start, out_cols, 1)]
        for bit in bits_of(tp_size):
            held = held + [swap_bit(value, "tp", bit) for value in held]
        down.insert(0, held)

    mine = lax.dynamic_slice_in_dim(tokens, own_local * part, part, 0)
    sent = {s: shift_by(mine, "grp", s) for s in shifts}

    scale = {}
    for s in range(groups):
        target = ((own_group + s) % groups) * group_size + own_local
        hit = expert_ids == target
        dense = jnp.sum(jnp.where(hit, router_weights.astype(jnp.float32), 0.0), axis=1)
        dense = dense.astype(jnp.bfloat16)
        if s > 0:
            dense = shift_by(dense, "grp", s)
        scale[s] = dense.astype(jnp.float32)[:, None]

    def whole_block(piece):
        pieces = [piece]
        for bit in reversed(bits_of(group_size)):
            pieces = pieces + [swap_bit(value, "loc", bit) for value in pieces]
        return pieces

    def ffn(pieces):
        return call(
            functools.partial(hidden_kernel, order, part),
            jax.ShapeDtypeStruct((rows, hidden_width), jnp.bfloat16),
            [pltpu.VMEM((rows, width), jnp.bfloat16)],
            scalars,
            *pieces,
            w_gate[0],
            w_up[0],
        )

    def group_parts(s, pieces):
        hidden = ffn(pieces)
        arrived = []
        if per_shard == 2:
            message = call(
                functools.partial(leave_kernel, order, part, 1),
                jax.ShapeDtypeStruct((tp_size, rows, out_cols), jnp.bfloat16),
                [],
                scalars,
                hidden,
                scale[s],
                *down[1],
            )
            arrived = [swap_bit(message, "loc", 1)]
        half = tp_size // 2
        keep, message = call(
            functools.partial(stay_kernel, order, part, half * per_shard, len(arrived) > 0),
            (
                jax.ShapeDtypeStruct((half, rows, out_cols), jnp.float32),
                jax.ShapeDtypeStruct((half, rows, out_cols), jnp.bfloat16),
            ),
            [pltpu.VMEM((tp_size, rows, out_cols), jnp.float32)],
            scalars,
            hidden,
            scale[s],
            *arrived,
            *down[0],
        )
        arrived = swap_bit(message, "loc", half * per_shard)
        while half > 1:
            half = half // 2
            keep = keep + arrived.astype(jnp.float32)
            bit = half * per_shard
            there = [order.index(k ^ bit) for k in order]
            message = keep[half:].astype(jnp.bfloat16).reshape(half, group_size, part, out_cols)
            message = jnp.stack([message[:, m] for m in there], axis=1)
            arrived = swap_bit(message.reshape(half, rows, out_cols), "loc", bit)
            keep = keep[:half]
        return keep[0], arrived[0]

    back = []
    for s in shifts:
        keep, arrived = group_parts(s, whole_block(sent[s]))
        both = (keep + arrived.astype(jnp.float32)).astype(jnp.bfloat16)
        back.append(shift_by(both, "grp", groups - s))
    keep, arrived = group_parts(0, [tokens])
    return call(
        functools.partial(finish_kernel, order, part),
        jax.ShapeDtypeStruct((rows, out_cols), jnp.bfloat16),
        [],
        scalars,
        keep,
        arrived,
        *back,
    )


def solution(mesh):
    placed = (
        P(("grp", "tp"), None),
        P(("grp", "tp"), None),
        P(("grp", "tp"), None),
        P(("grp", "loc"), None, None),
        P(("grp", "loc"), None, None),
        P(("grp", "loc"), None, "tp"),
    )
    return jax.shard_map(
        body, mesh=mesh, in_specs=placed, out_specs=P(("grp", "tp"), "loc"), check_vma=False
    )
```

time: 130 us -> 128 us (0.985)
  Pallas kernels: 0 us -> 31 us
  other arithmetic: 27.4 us -> 0.33 us
  matrix products: 24.9 us -> 0 us
  waiting for transfers between devices: 33.3 us -> 42.4 us
  local copies, waits for them, and re-layouts: 13.8 us -> 19.1 us
  starting transfers between devices: 28.8 us -> 34 us
    pallas_call x0 -> x13, Pallas kernels: none -> 31 us  [call(): pl.pallas_call(kernel, out_shape=outs, in_specs=[SM] + [VM] * len(arrays)...]
    dot_general x24 -> x0, matrix products: 24.9 us -> none  [the longest x16 15.5 us: group_sum(): result = jnp.dot(hidden[s], cols, preferred_element_type=jnp.float32)]
    concatenate x6 -> x0, other arithmetic: 12.3 us -> none  [whole_block(): got = jnp.concatenate([got, swap_bit(got, 'loc', bit)], axis=0)]
    unnamed x36 -> x58, local copies, waits for them, and re-layouts: 2.35 us -> 13.4 us
    gather x4 -> x0, local copies, waits for them, and re-layouts: 9.6 us -> none  [the longest x3 8.46 us: whole_block(): return jnp.take(got, take, axis=0).reshape(rows, width)]
    select_n x4 -> x0, other arithmetic: 5.96 us -> none  [the longest x1 3.16 us: body(): jnp.where(own_tp & bit > 0, jnp.concatenate([other, down], axis=1), jnp.c...]
    ppermute x9, starting transfers between devices: 16.7 us -> 22.3 us  [shift_by(): lax.ppermute(value, axis, [(i, (i + step) % size) for i in range(size)])]
    ppermute x9, waiting for transfers between devices: 17.3 us -> 21.9 us  [shift_by(): lax.ppermute(value, axis, [(i, (i + step) % size) for i in range(size)])]
  transfers between devices with their start and end apart: 24 -> 28, of which waited for: 10 -> 9; matrix products, arithmetic and copies ran while one was open for 41% -> 3% of each run, Pallas kernels for 0% -> 23%
where the time goes in v2:
time: 128 us; the launch traced here: 127 us
  waiting for transfers between devices  42.4 us (33%)
  starting transfers between devices  34 us (27%)
  Pallas kernels  31 us (24%)
  local copies, waits for them, and re-layouts  19.1 us (15%)
    pallas_call x13, Pallas kernels, call(): pl.pallas_call(kernel, out_shape=outs, in_specs=[SM] + [VM] * len(arrays)...  31 us
    ppermute x9, starting transfers between devices, shift_by(): lax.ppermute(value, axis, [(i, (i + step) % size) for i in range(size)])  22.3 us
    ppermute x9, waiting for transfers between devices, shift_by(): lax.ppermute(value, axis, [(i, (i + step) % size) for i in range(size)])  21.9 us
    ppermute x19, waiting for transfers between devices, swap_bit(): return lax.ppermute(value, axis, [(i, i ^ bit) for i in range(size)])  20.5 us
    unnamed x58, local copies, waits for them, and re-layouts  13.4 us
    ppermute x19, starting transfers between devices, swap_bit(): return lax.ppermute(value, axis, [(i, i ^ bit) for i in range(size)])  11.7 us
    dynamic_slice x1, local copies, waits for them, and re-layouts, body(): held = [lax.dynamic_slice_in_dim(w_down[0], start, out_cols, 1)]  2.63 us
  transfers between devices with their start and end apart: 28, of which 9 were waited for; matrix products, arithmetic and copies ran while one was open for 3% of the time, Pallas kernels for 23%

profile of v2, /device:TPU:0, one launch (start us, length us, event | category | flops | bytes accessed | tf_op | source)
XLA Modules:
  0.0 127.1 jit_solution(16199158383012370395)
XLA Ops:
  0.0 1.8 %constant_dynamic-slice_fusion = bf16[64,2048]{1,0:T(8,128)(2,1)} fusion(bf16[256,2048]{1,0:T(8,128)(2,1)} %refs_0_.1, s32[]{:T(128)S(6)} %select_n.57), kind=kLoop, calls=%fused_computation.16 | loop fusion | bytes 524292 | tf_op jit(solution)/shard_map/dynamic_slice | solution.py:141
  1.8 5.1 %collective-permute-start.20 = (bf16[64,2048]{1,0:T(8,128)(2,1)}, bf16[64,2048]{1,0:T(8,128)(2,1)S(1)}, u32[]{:S(2)}, u32[]{:S(2)}) collective-permute-start(bf16[64,2048]{1,0:T(8,128)(2,1)} %constant_dynamic-slice_fusion), channel_id=1, source_target_pairs={{0,24},{8,0},{16,8},{24,16},{1,25},{9,1},{17,9},{25,17},{2,26},{10... | collective-permute-start | bytes 786440 | tf_op jit(solution)/shard_map/ppermute | solution.py:22
  6.9 2.6 %dynamic-slice_bitcast_fusion = (bf16[768,512]{1,0:T(8,128)(2,1)}, bf16[768,512]{1,0:T(8,128)(2,1)}) fusion(bf16[1,768,1024]{2,1,0:T(8,128)(2,1)} %param.11, s32[]{:T(128)S(6)} %select_n.56, s32[]{:T(128)S(6)} %select_n.55), kind=kLoop, calls=%fused_computation | loop fusion | bytes 3145736 | tf_op jit(solution)/shard_map/dynamic_slice | solution.py:136
  12.1 2.9 %collective-permute-start.24 = (bf16[256]{0:T(256)(128)(2,1)S(1)}, bf16[256]{0:T(256)(128)(2,1)S(1)}, u32[]{:S(2)}, u32[]{:S(2)}) collective-permute-start(bf16[256]{0:T(256)(128)(2,1)S(1)} %get-tuple-element.21), channel_id=1, source_target_pairs={{0,24},{8,0},{16,8},{24,16},{1,25},{9,1},{17,9},{25,17},{2,26},{10... | collective-permute-start | bytes 1544 | tf_op jit(solution)/shard_map/ppermute | solution.py:22
  14.9 9.2 %collective-permute-done.24 = bf16[256]{0:T(256)(128)(2,1)S(1)} collective-permute-done((bf16[256]{0:T(256)(128)(2,1)S(1)}, bf16[256]{0:T(256)(128)(2,1)S(1)}, u32[]{:S(2)}, u32[]{:S(2)}) %collective-permute-start.24) | collective-permute-done | bytes 544 | tf_op jit(solution)/shard_map/ppermute | solution.py:22
  24.1 7.3 %collective-permute-start.16 = (bf16[256]{0:T(256)(128)(2,1)S(1)}, bf16[256]{0:T(256)(128)(2,1)S(1)}, u32[]{:S(2)}, u32[]{:S(2)}) collective-permute-start(bf16[256]{0:T(256)(128)(2,1)S(1)} %get-tuple-element.23), channel_id=1, source_target_pairs={{0,8},{8,16},{16,24},{24,0},{1,9},{9,17},{17,25},{25,1},{2,10},{10... | collective-permute-start | bytes 1544 | tf_op jit(solution)/shard_map/ppermute | solution.py:22
  35.0 4.9 %collective-permute-done.21.refs_1_ = bf16[64,2048]{1,0:T(8,128)(2,1)} collective-permute-done((bf16[64,2048]{1,0:T(8,128)(2,1)S(1)}, bf16[64,2048]{1,0:T(8,128)(2,1)}, u32[]{:S(2)}, u32[]{:S(2)}) %collective-permute-start.21) | collective-permute-done | bytes 262176 | tf_op jit(solution)/shard_map/ppermute | solution.py:17
  41.2 4.4 %collective-permute-done.13.refs_1_ = bf16[64,2048]{1,0:T(8,128)(2,1)} collective-permute-done((bf16[64,2048]{1,0:T(8,128)(2,1)}, bf16[64,2048]{1,0:T(8,128)(2,1)}, u32[]{:S(2)}, u32[]{:S(2)}) %collective-permute-start.13) | collective-permute-done | bytes 262176 | tf_op jit(solution)/shard_map/ppermute | solution.py:17
  45.6 3.8 %collective-permute-done.5.refs_1_ = bf16[64,2048]{1,0:T(8,128)(2,1)} collective-permute-done((bf16[64,2048]{1,0:T(8,128)(2,1)}, bf16[64,2048]{1,0:T(8,128)(2,1)}, u32[]{:S(2)}, u32[]{:S(2)}) %collective-permute-start.5) | collective-permute-done | bytes 262176 | tf_op jit(solution)/shard_map/ppermute | solution.py:17
  50.3 1.9 %copy-done.1 = bf16[1,2048,768]{2,1,0:T(8,128)(2,1)S(1)} copy-done((bf16[1,2048,768]{2,1,0:T(8,128)(2,1)S(1)}, bf16[1,2048,768]{2,1,0:T(8,128)(2,1)}, u32[]{:S(2)}) %copy-start.1) | copy-done | bytes 3145752
  53.2 2.8 %shard_map.73.hidden = bf16[256,768]{1,0:T(8,128)(2,1)S(1)} custom-call(s32[2]{0:T(128)S(1)} %pad_add_fusion.scalars, bf16[64,2048]{1,0:T(8,128)(2,1)S(1)} %collective-permute-done.20.refs_0_, bf16[64,2048]{1,0:T(8,128)(2,1)} %collective-permute-done.21.refs_1_, bf16[64,2048]{1,0:T(8,128)(2,1)S(1)} %copy-done.22, ...), custom_call_target="tpu_custom_call" | custom-call | tf_op jit(solution)/shard_map/pallas_call | solution.py:37
  56.1 2.7 %shard_map.74 = bf16[2,256,512]{2,1,0:T(8,128)(2,1)} custom-call(s32[2]{0:T(128)S(1)} %pad_add_fusion.scalars, bf16[256,768]{1,0:T(8,128)(2,1)S(1)} %shard_map.73.hidden, f32[256,1]{1,0:T(8,128)S(1)} %copy.14.scale, bf16[768,512]{1,0:T(8,128)(2,1)} %get-tuple-element.26.refs_0_, bf16[768,512]{1,0:T(8,128)(2,1)} %collective-permute-done.refs_1_), custom_call_target="tpu_custom_call" | custom-call | tf_op jit(solution)/shard_map/pallas_call | solution.py:37
  60.2 1.9 %copy-done.2 = bf16[1,2048,768]{2,1,0:T(8,128)(2,1)S(1)} copy-done((bf16[1,2048,768]{2,1,0:T(8,128)(2,1)S(1)}, bf16[1,2048,768]{2,1,0:T(8,128)(2,1)}, u32[]{:S(2)}) %copy-start.2) | copy-done | bytes 3145752
  62.0 3.2 %shard_map.70.hidden = bf16[256,768]{1,0:T(8,128)(2,1)S(1)} custom-call(s32[2]{0:T(128)S(1)} %pad_add_fusion.scalars, bf16[64,2048]{1,0:T(8,128)(2,1)} %collective-permute-done.12.refs_0_, bf16[64,2048]{1,0:T(8,128)(2,1)} %collective-permute-done.13.refs_1_, bf16[64,2048]{1,0:T(8,128)(2,1)} %collective-permute-done.14.refs_2_, ...), custom_call_target="tpu_custom_call" | custom-call | tf_op jit(solution)/shard_map/pallas_call | solution.py:37
  65.2 3.0 %shard_map.71 = bf16[2,256,512]{2,1,0:T(8,128)(2,1)} custom-call(s32[2]{0:T(128)S(1)} %pad_add_fusion.scalars, bf16[256,768]{1,0:T(8,128)(2,1)S(1)} %shard_map.70.hidden, f32[256,1]{1,0:T(8,128)S(1)} %copy.12.scale, bf16[768,512]{1,0:T(8,128)(2,1)} %get-tuple-element.26.refs_0_, bf16[768,512]{1,0:T(8,128)(2,1)} %collective-permute-done.refs_1_), custom_call_target="tpu_custom_call" | custom-call | tf_op jit(solution)/shard_map/pallas_call | solution.py:37
  68.8 2.4 %shard_map.64.hidden = bf16[256,768]{1,0:T(8,128)(2,1)S(1)} custom-call(s32[2]{0:T(128)S(1)} %pad_add_fusion.scalars, bf16[256,2048]{1,0:T(8,128)(2,1)S(1)} %copy-done.12, bf16[2048,768]{1,0:T(8,128)(2,1)S(1)} %bitcast.22, bf16[2048,768]{1,0:T(8,128)(2,1)S(1)} %bitcast.26), custom_call_target="tpu_custom_call" | custom-call | tf_op jit(solution)/shard_map/pallas_call | solution.py:37
  72.0 1.9 %copy-done.4 = bf16[1,2048,768]{2,1,0:T(8,128)(2,1)S(1)} copy-done((bf16[1,2048,768]{2,1,0:T(8,128)(2,1)S(1)}, bf16[1,2048,768]{2,1,0:T(8,128)(2,1)}, u32[]{:S(2)}) %copy-start.4) | copy-done | bytes 3145752
  73.9 3.0 %shard_map.67.hidden = bf16[256,768]{1,0:T(8,128)(2,1)S(1)} custom-call(s32[2]{0:T(128)S(1)} %pad_add_fusion.scalars, bf16[64,2048]{1,0:T(8,128)(2,1)} %collective-permute-done.4.refs_0_, bf16[64,2048]{1,0:T(8,128)(2,1)} %collective-permute-done.5.refs_1_, bf16[64,2048]{1,0:T(8,128)(2,1)} %collective-permute-done.6.refs_2_, ...), custom_call_target="tpu_custom_call" | custom-call | tf_op jit(solution)/shard_map/pallas_call | solution.py:37
  77.0 2.8 %shard_map.68 = bf16[2,256,512]{2,1,0:T(8,128)(2,1)} custom-call(s32[2]{0:T(128)S(1)} %pad_add_fusion.scalars, bf16[256,768]{1,0:T(8,128)(2,1)S(1)} %shard_map.67.hidden, f32[256,1]{1,0:T(8,128)S(1)} %copy-done.17, bf16[768,512]{1,0:T(8,128)(2,1)} %get-tuple-element.26.refs_0_, bf16[768,512]{1,0:T(8,128)(2,1)} %collective-permute-done.refs_1_), custom_call_target="tpu_custom_call" | custom-call | tf_op jit(solution)/shard_map/pallas_call | solution.py:37
  81.1 2.0 %shard_map.65 = bf16[2,256,512]{2,1,0:T(8,128)(2,1)S(1)} custom-call(s32[2]{0:T(128)S(1)} %pad_add_fusion.scalars, bf16[256,768]{1,0:T(8,128)(2,1)S(1)} %shard_map.64.hidden, f32[256,1]{1,0:T(8,128)S(1)} %copy.8.scale, bf16[768,512]{1,0:T(8,128)(2,1)} %get-tuple-element.26.refs_0_, bf16[768,512]{1,0:T(8,128)(2,1)} %collective-permute-done.refs_1_), custom_call_target="tpu_custom_call" | custom-call | tf_op jit(solution)/shard_map/pallas_call | solution.py:37
  85.4 2.0 %shard_map.75 = (f32[1,256,512]{2,1,0:T(8,128)S(1)}, bf16[1,256,512]{2,1,0:T(8,128)(2,1)S(1)}) custom-call(s32[2]{0:T(128)S(1)} %pad_add_fusion.scalars, bf16[256,768]{1,0:T(8,128)(2,1)S(1)} %copy-done.7, f32[256,1]{1,0:T(8,128)S(1)} %copy-done.14, bf16[2,256,512]{2,1,0:T(8,128)(2,1)} %collective-permute-done.25.refs_0_, bf16[768,512]{1,0:T(8,128)(2,1)S(1)} %copy-done.5, ...), custom_call_target="tpu_custom_call" | custom-call | tf_op jit(solution)/shard_map/pallas_call | solution.py:37
  87.4 1.6 %collective-permute-start.26 = (bf16[1,256,512]{2,1,0:T(8,128)(2,1)S(1)}, bf16[1,256,512]{2,1,0:T(8,128)(2,1)S(1)}, u32[]{:S(2)}, u32[]{:S(2)}) collective-permute-start(bf16[1,256,512]{2,1,0:T(8,128)(2,1)S(1)} %get-tuple-element.20), channel_id=1, source_target_pairs={{0,4},{2,6},{4,0},{6,2},{1,5},{3,7},{5,1},{7,3},{8,12},{10,14},{12... | collective-permute-start | bytes 786440 | tf_op jit(solution)/shard_map/ppermute | solution.py:17
  90.9 2.0 %shard_map.72 = (f32[1,256,512]{2,1,0:T(8,128)S(1)}, bf16[1,256,512]{2,1,0:T(8,128)(2,1)S(1)}) custom-call(s32[2]{0:T(128)S(1)} %pad_add_fusion.scalars, bf16[256,768]{1,0:T(8,128)(2,1)S(1)} %copy-done.9, f32[256,1]{1,0:T(8,128)S(1)} %copy-done.16, bf16[2,256,512]{2,1,0:T(8,128)(2,1)} %collective-permute-done.17.refs_0_, bf16[768,512]{1,0:T(8,128)(2,1)S(1)} %copy-done.5, ...), custom_call_target="tpu_custom_call" | custom-call | tf_op jit(solution)/shard_map/pallas_call | solution.py:37
  93.5 2.0 %shard_map.69 = (f32[1,256,512]{2,1,0:T(8,128)S(1)}, bf16[1,256,512]{2,1,0:T(8,128)(2,1)S(1)}) custom-call(s32[2]{0:T(128)S(1)} %pad_add_fusion.scalars, bf16[256,768]{1,0:T(8,128)(2,1)S(1)} %copy-done.11, f32[256,1]{1,0:T(8,128)S(1)} %copy-done.18, bf16[2,256,512]{2,1,0:T(8,128)(2,1)} %collective-permute-done.9.refs_0_, bf16[768,512]{1,0:T(8,128)(2,1)S(1)} %copy-done.5, ...), custom_call_target="tpu_custom_call" | custom-call | tf_op jit(solution)/shard_map/pallas_call | solution.py:37
  95.5 1.6 %collective-permute-start.10 = (bf16[1,256,512]{2,1,0:T(8,128)(2,1)S(1)}, bf16[1,256,512]{2,1,0:T(8,128)(2,1)S(1)}, u32[]{:S(2)}, u32[]{:S(2)}) collective-permute-start(bf16[1,256,512]{2,1,0:T(8,128)(2,1)S(1)} %get-tuple-element.16), channel_id=1, source_target_pairs={{0,4},{2,6},{4,0},{6,2},{1,5},{3,7},{5,1},{7,3},{8,12},{10,14},{12... | collective-permute-start | bytes 786440 | tf_op jit(solution)/shard_map/ppermute | solution.py:17
  97.0 1.8 %shard_map.66 = (f32[1,256,512]{2,1,0:T(8,128)S(1)}, bf16[1,256,512]{2,1,0:T(8,128)(2,1)S(1)}) custom-call(s32[2]{0:T(128)S(1)} %pad_add_fusion.scalars, bf16[256,768]{1,0:T(8,128)(2,1)S(1)} %shard_map.64.hidden, f32[256,1]{1,0:T(8,128)S(1)} %copy-done.20, bf16[2,256,512]{2,1,0:T(8,128)(2,1)S(1)} %collective-permute-done.1.refs_0_, ...), custom_call_target="tpu_custom_call" | custom-call | tf_op jit(solution)/shard_map/pallas_call | solution.py:37
  99.8 2.3 %collective-permute-done.18 = bf16[1,256,512]{2,1,0:T(8,128)(2,1)S(1)} collective-permute-done((bf16[1,256,512]{2,1,0:T(8,128)(2,1)S(1)}, bf16[1,256,512]{2,1,0:T(8,128)(2,1)S(1)}, u32[]{:S(2)}, u32[]{:S(2)}) %collective-permute-start.18) | collective-permute-done | bytes 262176 | tf_op jit(solution)/shard_map/ppermute | solution.py:17
  102.2 2.7 %collective-permute-start.19 = (bf16[256,512]{1,0:T(8,128)(2,1)S(1)}, bf16[256,512]{1,0:T(8,128)(2,1)S(1)}, u32[]{:S(2)}, u32[]{:S(2)}) collective-permute-start(bf16[256,512]{1,0:T(8,128)(2,1)S(1)} %fusion.1), channel_id=1, source_target_pairs={{0,24},{8,0},{16,8},{24,16},{1,25},{9,1},{17,9},{25,17},{2,26},{10... | collective-permute-start | bytes 786440 | tf_op jit(solution)/shard_map/ppermute | solution.py:22
  104.9 2.8 %collective-permute-done.10 = bf16[1,256,512]{2,1,0:T(8,128)(2,1)S(1)} collective-permute-done((bf16[1,256,512]{2,1,0:T(8,128)(2,1)S(1)}, bf16[1,256,512]{2,1,0:T(8,128)(2,1)S(1)}, u32[]{:S(2)}, u32[]{:S(2)}) %collective-permute-start.10) | collective-permute-done | bytes 262176 | tf_op jit(solution)/shard_map/ppermute | solution.py:17
  107.8 3.0 %collective-permute-start.11 = (bf16[256,512]{1,0:T(8,128)(2,1)S(1)}, bf16[256,512]{1,0:T(8,128)(2,1)S(1)}, u32[]{:S(2)}, u32[]{:S(2)}) collective-permute-start(bf16[256,512]{1,0:T(8,128)(2,1)S(1)} %fusion), channel_id=1, source_target_pairs={{0,16},{8,24},{16,0},{24,8},{1,17},{9,25},{17,1},{25,9},{2,18},{10... | collective-permute-start | bytes 786440 | tf_op jit(solution)/shard_map/ppermute | solution.py:22
  110.9 2.2 %collective-permute-done.3 = bf16[1,256,512]{2,1,0:T(8,128)(2,1)S(1)} collective-permute-done((bf16[1,256,512]{2,1,0:T(8,128)(2,1)S(1)}, bf16[1,256,512]{2,1,0:T(8,128)(2,1)S(1)}, u32[]{:S(2)}, u32[]{:S(2)}) %collective-permute-start.3) | collective-permute-done | bytes 262176 | tf_op jit(solution)/shard_map/ppermute | solution.py:17
  114.5 11.2 %collective-permute-done.11.refs_0_ = bf16[256,512]{1,0:T(8,128)(2,1)S(1)} collective-permute-done((bf16[256,512]{1,0:T(8,128)(2,1)S(1)}, bf16[256,512]{1,0:T(8,128)(2,1)S(1)}, u32[]{:S(2)}, u32[]{:S(2)}) %collective-permute-start.11) | collective-permute-done | bytes 262176 | tf_op jit(solution)/shard_map/ppermute | solution.py:22
  (110 shorter events, 22.1 us)
Async XLA Ops:
  0.0 50.3 %copy-start = (bf16[1,2048,768]{2,1,0:T(8,128)(2,1)S(1)}, bf16[1,2048,768]{2,1,0:T(8,128)(2,1)}, u32[]{:S(2)}) copy-start(bf16[1,2048,768]{2,1,0:T(8,128)(2,1)} %param.9) | copy-start | bytes 9437188
  1.8 29.6 %collective-permute-start.20 = (bf16[64,2048]{1,0:T(8,128)(2,1)}, bf16[64,2048]{1,0:T(8,128)(2,1)S(1)}, u32[]{:S(2)}, u32[]{:S(2)}) collective-permute-start(bf16[64,2048]{1,0:T(8,128)(2,1)} %constant_dynamic-slice_fusion), channel_id=1, source_target_pairs={{0,24},{8,0},{16,8},{24,16},{1,25},{9,1},{17,9},{25,17},{2,26},{10... | collective-permute-start | bytes 786440 | tf_op jit(solution)/shard_map/ppermute | solution.py:22
  9.5 40.7 %collective-permute-start = (bf16[768,512]{1,0:T(8,128)(2,1)}, bf16[768,512]{1,0:T(8,128)(2,1)}, u32[]{:S(2)}, u32[]{:S(2)}) collective-permute-start(bf16[768,512]{1,0:T(8,128)(2,1)} %get-tuple-element.26.refs_0_), channel_id=1, source_target_pairs={{0,1},{1,0},{2,3},{3,2},{4,5},{5,4},{6,7},{7,6},{8,9},{9,8},{10,11... | collective-permute-start | bytes 2359304 | tf_op jit(solution)/shard_map/ppermute | solution.py:17
  11.0 21.9 %collective-permute-start.12 = (bf16[64,2048]{1,0:T(8,128)(2,1)}, bf16[64,2048]{1,0:T(8,128)(2,1)}, u32[]{:S(2)}, u32[]{:S(2)}) collective-permute-start(bf16[64,2048]{1,0:T(8,128)(2,1)} %constant_dynamic-slice_fusion), channel_id=1, source_target_pairs={{0,8},{8,16},{16,24},{24,0},{1,9},{9,17},{17,25},{25,1},{2,10},{10... | collective-permute-start | bytes 786440 | tf_op jit(solution)/shard_map/ppermute | solution.py:22
  11.0 23.3 %collective-permute-start.4 = (bf16[64,2048]{1,0:T(8,128)(2,1)}, bf16[64,2048]{1,0:T(8,128)(2,1)}, u32[]{:S(2)}, u32[]{:S(2)}) collective-permute-start(bf16[64,2048]{1,0:T(8,128)(2,1)} %constant_dynamic-slice_fusion), channel_id=1, source_target_pairs={{0,16},{8,24},{16,0},{24,8},{1,17},{9,25},{17,1},{25,9},{2,18},{10... | collective-permute-start | bytes 786440 | tf_op jit(solution)/shard_map/ppermute | solution.py:22
  12.1 12.0 %collective-permute-start.24 = (bf16[256]{0:T(256)(128)(2,1)S(1)}, bf16[256]{0:T(256)(128)(2,1)S(1)}, u32[]{:S(2)}, u32[]{:S(2)}) collective-permute-start(bf16[256]{0:T(256)(128)(2,1)S(1)} %get-tuple-element.21), channel_id=1, source_target_pairs={{0,24},{8,0},{16,8},{24,16},{1,25},{9,1},{17,9},{25,17},{2,26},{10... | collective-permute-start | bytes 1544 | tf_op jit(solution)/shard_map/ppermute | solution.py:22
  24.1 8.8 %collective-permute-start.16 = (bf16[256]{0:T(256)(128)(2,1)S(1)}, bf16[256]{0:T(256)(128)(2,1)S(1)}, u32[]{:S(2)}, u32[]{:S(2)}) collective-permute-start(bf16[256]{0:T(256)(128)(2,1)S(1)} %get-tuple-element.23), channel_id=1, source_target_pairs={{0,8},{8,16},{16,24},{24,0},{1,9},{9,17},{17,25},{25,1},{2,10},{10... | collective-permute-start | bytes 1544 | tf_op jit(solution)/shard_map/ppermute | solution.py:22
  31.4 8.6 %collective-permute-start.21 = (bf16[64,2048]{1,0:T(8,128)(2,1)S(1)}, bf16[64,2048]{1,0:T(8,128)(2,1)}, u32[]{:S(2)}, u32[]{:S(2)}) collective-permute-start(bf16[64,2048]{1,0:T(8,128)(2,1)S(1)} %collective-permute-done.20.refs_0_), channel_id=1, source_target_pairs={{0,4},{2,6},{4,0},{6,2},{1,5},{3,7},{5,1},{7,3},{8,12},{10,14},{12... | collective-permute-start | bytes 786440 | tf_op jit(solution)/shard_map/ppermute | solution.py:17
  32.9 16.5 %copy-start.25 = (bf16[256]{0:T(256)(128)(2,1)}, bf16[256]{0:T(256)(128)(2,1)S(1)}, u32[]{:S(2)}) copy-start(bf16[256]{0:T(256)(128)(2,1)S(1)} %collective-permute-done.16) | copy-start | bytes 1540
  32.9 7.1 %collective-permute-start.22 = (bf16[64,2048]{1,0:T(8,128)(2,1)S(1)}, bf16[64,2048]{1,0:T(8,128)(2,1)S(1)}, u32[]{:S(2)}, u32[]{:S(2)}) collective-permute-start(bf16[64,2048]{1,0:T(8,128)(2,1)S(1)} %collective-permute-done.20.refs_0_), channel_id=1, source_target_pairs={{0,2},{2,0},{4,6},{6,4},{1,3},{3,1},{5,7},{7,5},{8,10},{10,8},{12,... | collective-permute-start | bytes 786440 | tf_op jit(solution)/shard_map/ppermute | solution.py:17
  32.9 12.6 %collective-permute-start.13 = (bf16[64,2048]{1,0:T(8,128)(2,1)}, bf16[64,2048]{1,0:T(8,128)(2,1)}, u32[]{:S(2)}, u32[]{:S(2)}) collective-permute-start(bf16[64,2048]{1,0:T(8,128)(2,1)} %collective-permute-done.12.refs_0_), channel_id=1, source_target_pairs={{0,4},{2,6},{4,0},{6,2},{1,5},{3,7},{5,1},{7,3},{8,12},{10,14},{12... | collective-permute-start | bytes 786440 | tf_op jit(solution)/shard_map/ppermute | solution.py:17
  34.3 15.1 %collective-permute-start.5 = (bf16[64,2048]{1,0:T(8,128)(2,1)}, bf16[64,2048]{1,0:T(8,128)(2,1)}, u32[]{:S(2)}, u32[]{:S(2)}) collective-permute-start(bf16[64,2048]{1,0:T(8,128)(2,1)} %collective-permute-done.4.refs_0_), channel_id=1, source_target_pairs={{0,4},{2,6},{4,0},{6,2},{1,5},{3,7},{5,1},{7,3},{8,12},{10,14},{12... | collective-permute-start | bytes 786440 | tf_op jit(solution)/shard_map/ppermute | solution.py:17
  40.0 9.7 %collective-permute-start.23 = (bf16[64,2048]{1,0:T(8,128)(2,1)}, bf16[64,2048]{1,0:T(8,128)(2,1)}, u32[]{:S(2)}, u32[]{:S(2)}) collective-permute-start(bf16[64,2048]{1,0:T(8,128)(2,1)} %collective-permute-done.21.refs_1_), channel_id=1, source_target_pairs={{0,2},{2,0},{4,6},{6,4},{1,3},{3,1},{5,7},{7,5},{8,10},{10,8},{12,... | collective-permute-start | bytes 786440 | tf_op jit(solution)/shard_map/ppermute | solution.py:17
  40.7 42.6 %collective-permute-start.2 = (bf16[768,512]{1,0:T(8,128)(2,1)}, bf16[768,512]{1,0:T(8,128)(2,1)}, u32[]{:S(2)}, u32[]{:S(2)}) collective-permute-start(bf16[768,512]{1,0:T(8,128)(2,1)} %get-tuple-element.25.refs_1_), channel_id=1, source_target_pairs={{0,1},{1,0},{2,3},{3,2},{4,5},{5,4},{6,7},{7,6},{8,9},{9,8},{10,11... | collective-permute-start | bytes 2359304 | tf_op jit(solution)/shard_map/ppermute | solution.py:17
  45.6 14.0 %collective-permute-start.14 = (bf16[64,2048]{1,0:T(8,128)(2,1)}, bf16[64,2048]{1,0:T(8,128)(2,1)}, u32[]{:S(2)}, u32[]{:S(2)}) collective-permute-start(bf16[64,2048]{1,0:T(8,128)(2,1)} %collective-permute-done.12.refs_0_), channel_id=1, source_target_pairs={{0,2},{2,0},{4,6},{6,4},{1,3},{3,1},{5,7},{7,5},{8,10},{10,8},{12,... | collective-permute-start | bytes 786440 | tf_op jit(solution)/shard_map/ppermute | solution.py:17
  49.4 10.6 %collective-permute-start.15 = (bf16[64,2048]{1,0:T(8,128)(2,1)}, bf16[64,2048]{1,0:T(8,128)(2,1)}, u32[]{:S(2)}, u32[]{:S(2)}) collective-permute-start(bf16[64,2048]{1,0:T(8,128)(2,1)} %collective-permute-done.13.refs_1_), channel_id=1, source_target_pairs={{0,2},{2,0},{4,6},{6,4},{1,3},{3,1},{5,7},{7,5},{8,10},{10,8},{12,... | collective-permute-start | bytes 786440 | tf_op jit(solution)/shard_map/ppermute | solution.py:17
  49.7 22.3 %collective-permute-start.6 = (bf16[64,2048]{1,0:T(8,128)(2,1)}, bf16[64,2048]{1,0:T(8,128)(2,1)}, u32[]{:S(2)}, u32[]{:S(2)}) collective-permute-start(bf16[64,2048]{1,0:T(8,128)(2,1)} %collective-permute-done.4.refs_0_), channel_id=1, source_target_pairs={{0,2},{2,0},{4,6},{6,4},{1,3},{3,1},{5,7},{7,5},{8,10},{10,8},{12,... | collective-permute-start | bytes 786440 | tf_op jit(solution)/shard_map/ppermute | solution.py:17
  50.3 21.8 %collective-permute-start.7 = (bf16[64,2048]{1,0:T(8,128)(2,1)}, bf16[64,2048]{1,0:T(8,128)(2,1)}, u32[]{:S(2)}, u32[]{:S(2)}) collective-permute-start(bf16[64,2048]{1,0:T(8,128)(2,1)} %collective-permute-done.5.refs_1_), channel_id=1, source_target_pairs={{0,2},{2,0},{4,6},{6,4},{1,3},{3,1},{5,7},{7,5},{8,10},{10,8},{12,... | collective-permute-start | bytes 786440 | tf_op jit(solution)/shard_map/ppermute | solution.py:17
  59.6 23.7 %collective-permute-start.25 = (bf16[2,256,512]{2,1,0:T(8,128)(2,1)}, bf16[2,256,512]{2,1,0:T(8,128)(2,1)}, u32[]{:S(2)}, u32[]{:S(2)}) collective-permute-start(bf16[2,256,512]{2,1,0:T(8,128)(2,1)} %shard_map.74), channel_id=1, source_target_pairs={{0,2},{2,0},{4,6},{6,4},{1,3},{3,1},{5,7},{7,5},{8,10},{10,8},{12,... | collective-permute-start | bytes 1572872 | tf_op jit(solution)/shard_map/ppermute | solution.py:17
  60.0 8.2 %collective-permute-start.8 = (bf16[256]{0:T(256)(128)(2,1)S(1)}, bf16[256]{0:T(256)(128)(2,1)S(1)}, u32[]{:S(2)}, u32[]{:S(2)}) collective-permute-start(bf16[256]{0:T(256)(128)(2,1)S(1)} %get-tuple-element.22), channel_id=1, source_target_pairs={{0,16},{8,24},{16,0},{24,8},{1,17},{9,25},{17,1},{25,9},{2,18},{10... | collective-permute-start | bytes 1544 | tf_op jit(solution)/shard_map/ppermute | solution.py:22
  68.7 20.3 %collective-permute-start.17 = (bf16[2,256,512]{2,1,0:T(8,128)(2,1)}, bf16[2,256,512]{2,1,0:T(8,128)(2,1)}, u32[]{:S(2)}, u32[]{:S(2)}) collective-permute-start(bf16[2,256,512]{2,1,0:T(8,128)(2,1)} %shard_map.71), channel_id=1, source_target_pairs={{0,2},{2,0},{4,6},{6,4},{1,3},{3,1},{5,7},{7,5},{8,10},{10,8},{12,... | collective-permute-start | bytes 1572872 | tf_op jit(solution)/shard_map/ppermute | solution.py:17
  80.5 13.0 %collective-permute-start.9 = (bf16[2,256,512]{2,1,0:T(8,128)(2,1)}, bf16[2,256,512]{2,1,0:T(8,128)(2,1)}, u32[]{:S(2)}, u32[]{:S(2)}) collective-permute-start(bf16[2,256,512]{2,1,0:T(8,128)(2,1)} %shard_map.68), channel_id=1, source_target_pairs={{0,2},{2,0},{4,6},{6,4},{1,3},{3,1},{5,7},{7,5},{8,10},{10,8},{12,... | collective-permute-start | bytes 1572872 | tf_op jit(solution)/shard_map/ppermute | solution.py:17
  81.1 12.4 %copy-start.11 = (bf16[256,768]{1,0:T(8,128)(2,1)S(1)}, bf16[256,768]{1,0:T(8,128)(2,1)}, u32[]{:S(2)}) copy-start(bf16[256,768]{1,0:T(8,128)(2,1)} %copy-done.10) | copy-start | bytes 1179652
  81.1 12.4 %copy-start.18 = (f32[256,1]{1,0:T(8,128)S(1)}, f32[256,1]{1,0:T(8,128)}, u32[]{:S(2)}) copy-start(f32[256,1]{1,0:T(8,128)} %copy.10.scale) | copy-start | bytes 3076
  83.1 13.9 %collective-permute-start.1 = (bf16[2,256,512]{2,1,0:T(8,128)(2,1)S(1)}, bf16[2,256,512]{2,1,0:T(8,128)(2,1)S(1)}, u32[]{:S(2)}, u32[]{:S(2)}) collective-permute-start(bf16[2,256,512]{2,1,0:T(8,128)(2,1)S(1)} %shard_map.65), channel_id=1, source_target_pairs={{0,2},{2,0},{4,6},{6,4},{1,3},{3,1},{5,7},{7,5},{8,10},{10,8},{12,... | collective-permute-start | bytes 1572872 | tf_op jit(solution)/shard_map/ppermute | solution.py:17
  87.4 12.0 %collective-permute-start.26 = (bf16[1,256,512]{2,1,0:T(8,128)(2,1)S(1)}, bf16[1,256,512]{2,1,0:T(8,128)(2,1)S(1)}, u32[]{:S(2)}, u32[]{:S(2)}) collective-permute-start(bf16[1,256,512]{2,1,0:T(8,128)(2,1)S(1)} %get-tuple-element.20), channel_id=1, source_target_pairs={{0,4},{2,6},{4,0},{6,2},{1,5},{3,7},{5,1},{7,3},{8,12},{10,14},{12... | collective-permute-start | bytes 786440 | tf_op jit(solution)/shard_map/ppermute | solution.py:17
  92.9 9.2 %collective-permute-start.18 = (bf16[1,256,512]{2,1,0:T(8,128)(2,1)S(1)}, bf16[1,256,512]{2,1,0:T(8,128)(2,1)S(1)}, u32[]{:S(2)}, u32[]{:S(2)}) collective-permute-start(bf16[1,256,512]{2,1,0:T(8,128)(2,1)S(1)} %get-tuple-element.18), channel_id=1, source_target_pairs={{0,4},{2,6},{4,0},{6,2},{1,5},{3,7},{5,1},{7,3},{8,12},{10,14},{12... | collective-permute-start | bytes 786440 | tf_op jit(solution)/shard_map/ppermute | solution.py:17
  95.5 12.3 %collective-permute-start.10 = (bf16[1,256,512]{2,1,0:T(8,128)(2,1)S(1)}, bf16[1,256,512]{2,1,0:T(8,128)(2,1)S(1)}, u32[]{:S(2)}, u32[]{:S(2)}) collective-permute-start(bf16[1,256,512]{2,1,0:T(8,128)(2,1)S(1)} %get-tuple-element.16), channel_id=1, source_target_pairs={{0,4},{2,6},{4,0},{6,2},{1,5},{3,7},{5,1},{7,3},{8,12},{10,14},{12... | collective-permute-start | bytes 786440 | tf_op jit(solution)/shard_map/ppermute | solution.py:17
  98.9 14.2 %collective-permute-start.3 = (bf16[1,256,512]{2,1,0:T(8,128)(2,1)S(1)}, bf16[1,256,512]{2,1,0:T(8,128)(2,1)S(1)}, u32[]{:S(2)}, u32[]{:S(2)}) collective-permute-start(bf16[1,256,512]{2,1,0:T(8,128)(2,1)S(1)} %get-tuple-element.14), channel_id=1, source_target_pairs={{0,4},{2,6},{4,0},{6,2},{1,5},{3,7},{5,1},{7,3},{8,12},{10,14},{12... | collective-permute-start | bytes 786440 | tf_op jit(solution)/shard_map/ppermute | solution.py:17
  99.5 13.5 %collective-permute-start.27 = (bf16[256,512]{1,0:T(8,128)(2,1)S(1)}, bf16[256,512]{1,0:T(8,128)(2,1)S(1)}, u32[]{:S(2)}, u32[]{:S(2)}) collective-permute-start(bf16[256,512]{1,0:T(8,128)(2,1)S(1)} %fusion.2), channel_id=1, source_target_pairs={{0,8},{8,16},{16,24},{24,0},{1,9},{9,17},{17,25},{25,1},{2,10},{10... | collective-permute-start | bytes 786440 | tf_op jit(solution)/shard_map/ppermute | solution.py:22
  102.2 12.3 %collective-permute-start.19 = (bf16[256,512]{1,0:T(8,128)(2,1)S(1)}, bf16[256,512]{1,0:T(8,128)(2,1)S(1)}, u32[]{:S(2)}, u32[]{:S(2)}) collective-permute-start(bf16[256,512]{1,0:T(8,128)(2,1)S(1)} %fusion.1), channel_id=1, source_target_pairs={{0,24},{8,0},{16,8},{24,16},{1,25},{9,1},{17,9},{25,17},{2,26},{10... | collective-permute-start | bytes 786440 | tf_op jit(solution)/shard_map/ppermute | solution.py:22
  107.8 17.9 %collective-permute-start.11 = (bf16[256,512]{1,0:T(8,128)(2,1)S(1)}, bf16[256,512]{1,0:T(8,128)(2,1)S(1)}, u32[]{:S(2)}, u32[]{:S(2)}) collective-permute-start(bf16[256,512]{1,0:T(8,128)(2,1)S(1)} %fusion), channel_id=1, source_target_pairs={{0,16},{8,24},{16,0},{24,8},{1,17},{9,25},{17,1},{25,9},{2,18},{10... | collective-permute-start | bytes 786440 | tf_op jit(solution)/shard_map/ppermute | solution.py:22
  (25 other events, 95.7 us)

commit v3 on v2

v3 whole, which is shorter than its diff:
```python
import functools

import jax
import jax.numpy as jnp
from jax import lax
from jax.experimental import pallas as pl
from jax.experimental.pallas import tpu as pltpu
from jax.sharding import PartitionSpec as P

VM = pl.BlockSpec(memory_space=pltpu.VMEM)
ANY = pl.BlockSpec(memory_space=pl.ANY)
STEP = 256
LANES = 128


def swap_bit(value, axis, bit):
    size = lax.axis_size(axis)
    return lax.ppermute(value, axis, [(i, i ^ bit) for i in range(size)])


def shift_by(value, axis, step):
    size = lax.axis_size(axis)
    return lax.ppermute(value, axis, [(i, (i + step) % size) for i in range(size)])


def bits_of(size):
    return [1 << i for i in range(size.bit_length() - 1)]


def part_order(size):
    order = [0]
    for bit in reversed(bits_of(size)):
        order = order + [i ^ bit for i in order]
    return order


def call(kernel, outs, arrays, scratch=(), in_specs=None, out_specs=None, flops=0):
    moved = sum(a.size * a.dtype.itemsize for a in (*arrays, *jax.tree.leaves(outs)))
    return pl.pallas_call(
        kernel,
        out_shape=outs,
        in_specs=in_specs or [VM] * len(arrays),
        out_specs=out_specs or jax.tree.map(lambda _: VM, outs),
        scratch_shapes=list(scratch),
        compiler_params=pltpu.CompilerParams(vmem_limit_bytes=12 << 20),
        cost_estimate=pl.CostEstimate(flops=flops, bytes_accessed=moved, transcendentals=0),
    )(*arrays)


def rows_at(index, part):
    return pl.ds(pl.multiple_of(index * part, part), part)


def own_expert():
    return lax.axis_index("grp") * lax.axis_size("loc") + lax.axis_index("loc")


def column_place(per_shard):
    return lax.axis_index("tp") ^ (lax.axis_index("loc") // per_shard)


def prepare_kernel(per_shard, part, tokens, ids, weights, down, message, table, *rest):
    *chunks, sems = rest
    width = tokens.shape[1]
    local = lax.axis_index("loc")
    copies = [
        pltpu.make_async_copy(tokens.at[rows_at(local, part), :], message.at[:, :width], sems.at[0])
    ]
    for j, chunk in enumerate(chunks):
        cols = chunk.shape[1]
        at = pl.multiple_of(((local % per_shard) ^ j) * cols, cols)
        copies.append(pltpu.make_async_copy(down.at[:, pl.ds(at, cols)], chunk, sems.at[1 + j]))
    for copy in copies:
        copy.start()
    lanes, rows = table.shape[1], table.shape[0]
    expert = lax.broadcasted_iota(jnp.int32, (lanes, rows), 0)
    dense = jnp.zeros((lanes, rows), jnp.float32)
    for k in range(ids.shape[0]):
        dense = jnp.where(expert == ids[k : k + 1, :], weights[k : k + 1, :].astype(jnp.float32), dense)
    table[...] = dense.T.astype(jnp.bfloat16)
    message[:, width:] = table[rows_at(local, part), :]
    for copy in copies:
        copy.wait()


def hidden_kernel(order, part, *refs):
    *pieces, gate, up, hidden, scale, block, routes = refs
    width = gate.shape[0]
    local = lax.axis_index("loc")
    for n, k in enumerate(order):
        at = slice(n * part, (n + 1) * part)
        if len(pieces) == 2:
            block[at, :] = pieces[0][rows_at(local ^ k, part), :]
            routes[at, :] = pieces[1][rows_at(local ^ k, part), :].astype(jnp.float32)
        else:
            block[at, :] = pieces[n][:, :width]
            routes[at, :] = pieces[n][:, width:].astype(jnp.float32)
    expert = lax.broadcasted_iota(jnp.int32, routes.shape, 1)
    own = jnp.sum(jnp.where(expert == own_expert(), routes[...], 0.0), axis=1, keepdims=True)
    scale[...] = jnp.broadcast_to(own, scale.shape)
    for j in range(0, gate.shape[1], STEP):
        a = jnp.dot(block[...], gate[:, j : j + STEP], preferred_element_type=jnp.float32)
        b = jnp.dot(block[...], up[:, j : j + STEP], preferred_element_type=jnp.float32)
        hidden[:, j : j + STEP] = (a / (1.0 + jnp.exp(-a)) * b).astype(jnp.bfloat16)


def scaled(hidden, weights, scale, j):
    out = jnp.dot(hidden[...], weights[:, j : j + STEP], preferred_element_type=jnp.float32)
    out = out.astype(jnp.bfloat16).astype(jnp.float32)
    factor = scale[...]
    return jnp.concatenate(
        [out[:, i : i + LANES] * factor for i in range(0, out.shape[1], LANES)], axis=1
    )


def leave_kernel(order, part, per_shard, bit, hidden, scale, *refs):
    *columns, message = refs
    own = column_place(per_shard)
    for u, weights in enumerate(columns):
        place = own ^ u
        for j in range(0, weights.shape[1], STEP):
            value = scaled(hidden, weights, scale, j).astype(jnp.bfloat16)
            for n, k in enumerate(order):
                m = order.index(k ^ bit)
                message[place, n * part : (n + 1) * part, j : j + STEP] = value[m * part : (m + 1) * part]


def stay_kernel(order, part, per_shard, bit, with_sum, hidden, scale, *refs):
    if with_sum:
        arrived, *refs = refs
    *columns, keep, message, total = refs
    half = len(columns) // 2
    own = column_place(per_shard)
    for u, weights in enumerate(columns):
        place = own ^ u
        for j in range(0, weights.shape[1], STEP):
            value = scaled(hidden, weights, scale, j)
            if with_sum:
                value = value + arrived[place, :, j : j + STEP].astype(jnp.float32)
            total[place, :, j : j + STEP] = value
    for i in range(half):
        keep[i] = total[i]
        for n, k in enumerate(order):
            m = order.index(k ^ bit)
            message[i, n * part : (n + 1) * part, :] = total[half + i, m * part : (m + 1) * part, :].astype(
                jnp.bfloat16
            )


def finish_kernel(order, part, keep, arrived, *refs):
    *others, out = refs
    local = lax.axis_index("loc")
    for n, k in enumerate(order):
        at = slice(n * part, (n + 1) * part)
        value = keep[at, :] + arrived[at, :].astype(jnp.float32)
        for other in others:
            value = value + other[at, :].astype(jnp.float32)
        out[rows_at(local ^ k, part), :] = value.astype(jnp.bfloat16)


def body(tokens, expert_ids, router_weights, w_gate, w_up, w_down):
    groups = lax.axis_size("grp")
    group_size = lax.axis_size("loc")
    tp_size = lax.axis_size("tp")
    rows, width = tokens.shape
    hidden_width = w_gate.shape[2]
    part = rows // group_size
    out_cols = width // group_size
    per_shard = group_size // tp_size
    lanes = -(-groups * group_size // LANES) * LANES
    order = part_order(group_size)
    shifts = sorted(range(1, groups), key=lambda s: -min(s, groups - s))
    shape = jax.ShapeDtypeStruct
    bf16, f32 = jnp.bfloat16, jnp.float32

    sliced = per_shard if per_shard > 1 else 0
    message, table, *chunks = call(
        functools.partial(prepare_kernel, per_shard, part),
        [shape((part, width + lanes), bf16), shape((rows, lanes), bf16)]
        + [shape((hidden_width, out_cols), bf16)] * sliced,
        (tokens, expert_ids.T, router_weights.T, w_down[0]),
        in_specs=[ANY, VM, VM, ANY],
        out_specs=[VM, VM] + [ANY] * sliced,
        scratch=[pltpu.SemaphoreType.DMA((1 + sliced,))],
    )
    if not chunks:
        chunks = [w_down[0]]

    down = []
    for chunk in reversed(chunks):
        held = [chunk]
        for bit in bits_of(tp_size):
            held = held + [swap_bit(value, "tp", bit) for value in held]
        down.insert(0, held)

    sent = {s: shift_by(message, "grp", s) for s in shifts}

    def whole_block(piece):
        pieces = [piece]
        for bit in reversed(bits_of(group_size)):
            pieces = pieces + [swap_bit(value, "loc", bit) for value in pieces]
        return pieces

    def ffn(pieces):
        return call(
            functools.partial(hidden_kernel, order, part),
            (shape((rows, hidden_width), bf16), shape((rows, LANES), f32)),
            (*pieces, w_gate[0], w_up[0]),
            scratch=[pltpu.VMEM((rows, width), bf16), pltpu.VMEM((rows, lanes), f32)],
            flops=4 * rows * width * hidden_width,
        )

    def group_parts(pieces):
        hidden, scale = ffn(pieces)
        flops = 2 * rows * hidden_width * out_cols * tp_size
        arrived = []
        if per_shard == 2:
            leaving = call(
                functools.partial(leave_kernel, order, part, per_shard, 1),
                shape((tp_size, rows, out_cols), bf16),
                (hidden, scale, *down[1]),
                flops=flops,
            )
            arrived = [swap_bit(leaving, "loc", 1)]
        half = tp_size // 2
        keep, leaving = call(
            functools.partial(
                stay_kernel, order, part, per_shard, half * per_shard, len(arrived) > 0
            ),
            (shape((half, rows, out_cols), f32), shape((half, rows, out_cols), bf16)),
            (hidden, scale, *arrived, *down[0]),
            scratch=[pltpu.VMEM((tp_size, rows, out_cols), f32)],
            flops=flops,
        )
        arrived = swap_bit(leaving, "loc", half * per_shard)
        while half > 1:
            half = half // 2
            keep = keep + arrived.astype(f32)
            bit = half * per_shard
            there = [order.index(k ^ bit) for k in order]
            leaving = keep[half:].astype(bf16).reshape(half, group_size, part, out_cols)
            leaving = jnp.stack([leaving[:, m] for m in there], axis=1)
            arrived = swap_bit(leaving.reshape(half, rows, out_cols), "loc", bit)
            keep = keep[:half]
        return keep[0], arrived[0]

    back = []
    for s in shifts:
        keep, arrived = group_parts(whole_block(sent[s]))
        both = (keep + arrived.astype(f32)).astype(bf16)
        back.append(shift_by(both, "grp", groups - s))
    keep, arrived = group_parts([tokens, table])
    return call(
        functools.partial(finish_kernel, order, part),
        shape((rows, out_cols), bf16),
        (keep, arrived, *back),
    )


def solution(mesh):
    placed = (
        P(("grp", "tp"), None),
        P(("grp", "tp"), None),
        P(("grp", "tp"), None),
        P(("grp", "loc"), None, None),
        P(("grp", "loc"), None, None),
        P(("grp", "loc"), None, "tp"),
    )
    return jax.shard_map(
        body, mesh=mesh, in_specs=placed, out_specs=P(("grp", "tp"), "loc"), check_vma=False
    )
```

time: 128 us -> 107 us (0.84)
  Pallas kernels: 31 us -> 13.4 us
  local copies, waits for them, and re-layouts: 19.1 us -> 7.8 us
  waiting for transfers between devices: 42.4 us -> 52.4 us
  starting transfers between devices: 34 us -> 32.7 us
    pallas_call x13 -> x14, Pallas kernels: 31 us -> 13.4 us  [call(): pl.pallas_call(kernel, out_shape=outs, in_specs=in_specs or [VM] * len(ar...]
    ppermute x9 -> x6, waiting for transfers between devices: 21.9 us -> 33 us  [shift_by(): lax.ppermute(value, axis, [(i, (i + step) % size) for i in range(size)])]
    unnamed x58 -> x16, local copies, waits for them, and re-layouts: 13.4 us -> 7.8 us
    dynamic_slice x2 -> x0, local copies, waits for them, and re-layouts: 4.45 us -> none  [the longest x1 2.63 us: body(): held = [lax.dynamic_slice_in_dim(w_down[0], start, out_cols, 1)]]
    ppermute x9 -> x6, starting transfers between devices: 22.3 us -> 17.9 us  [shift_by(): lax.ppermute(value, axis, [(i, (i + step) % size) for i in range(size)])]
    ppermute x19, starting transfers between devices: 11.7 us -> 14.8 us  [swap_bit(): return lax.ppermute(value, axis, [(i, i ^ bit) for i in range(size)])]
  transfers between devices with their start and end apart: 28 -> 25, of which waited for: 9 -> 9; matrix products, arithmetic and copies ran while one was open for 3% -> 0% of each run, Pallas kernels for 23% -> 11%
where the time goes in v3:
time: 107 us
  waiting for transfers between devices  52.4 us (49%)
  starting transfers between devices  32.7 us (31%)
  Pallas kernels  13.4 us (13%)
  local copies, waits for them, and re-layouts  7.8 us (7%)
    ppermute x6, waiting for transfers between devices, shift_by(): lax.ppermute(value, axis, [(i, (i + step) % size) for i in range(size)])  33 us
    ppermute x19, waiting for transfers between devices, swap_bit(): return lax.ppermute(value, axis, [(i, i ^ bit) for i in range(size)])  19.4 us
    ppermute x6, starting transfers between devices, shift_by(): lax.ppermute(value, axis, [(i, (i + step) % size) for i in range(size)])  17.9 us
    ppermute x19, starting transfers between devices, swap_bit(): return lax.ppermute(value, axis, [(i, i ^ bit) for i in range(size)])  14.8 us
    pallas_call x14, Pallas kernels, call(): pl.pallas_call(kernel, out_shape=outs, in_specs=in_specs or [VM] * len(ar...  13.4 us
    unnamed x16, local copies, waits for them, and re-layouts  7.8 us
  transfers between devices with their start and end apart: 25, of which 9 were waited for; matrix products, arithmetic and copies ran while one was open for 0% of the time, Pallas kernels for 11%

profile of v3, /device:TPU:0, one launch (start us, length us, event | category | flops | bytes accessed | tf_op | source)
XLA Modules:
  0.0 106.7 jit_solution(2662199273189268502)
XLA Ops:
  0.0 1.2 %copy-done.4 = bf16[256,2048]{1,0:T(8,128)(2,1)S(1)} copy-done((bf16[256,2048]{1,0:T(8,128)(2,1)S(1)}, bf16[256,2048]{1,0:T(8,128)(2,1)}, u32[]{:S(2)}) %copy-start.4) | copy-done | bytes 1048600
  1.2 1.4 %copy-done.5 = bf16[1,768,1024]{2,1,0:T(8,128)(2,1)S(1)} copy-done((bf16[1,768,1024]{2,1,0:T(8,128)(2,1)S(1)}, bf16[1,768,1024]{2,1,0:T(8,128)(2,1)}, u32[]{:S(2)}) %copy-start.5) | copy-done | bytes 1572888
  2.6 0.7 copy-done.6
  3.3 0.7 copy-done.7
  4.4 3.0 %collective-permute-start = (bf16[768,512]{1,0:T(8,128)(2,1)S(1)}, bf16[768,512]{1,0:T(8,128)(2,1)S(1)}, u32[]{:S(2)}, u32[]{:S(2)}) collective-permute-start(bf16[768,512]{1,0:T(8,128)(2,1)S(1)} %get-tuple-element.28.refs_0_), channel_id=1, source_target_pairs={{0,1},{1,0},{2,3},{3,2},{4,5},{5,4},{6,7},{7,6},{8,9},{9,8},{10,11... | collective-permute-start | bytes 2359304 | tf_op jit(solution)/shard_map/ppermute | solution.py:18
  7.4 3.6 %collective-permute-start.18 = (bf16[64,2176]{1,0:T(8,128)(2,1)S(1)}, bf16[64,2176]{1,0:T(8,128)(2,1)S(1)}, u32[]{:S(2)}, u32[]{:S(2)}) collective-permute-start(bf16[64,2176]{1,0:T(8,128)(2,1)S(1)} %get-tuple-element.32), channel_id=1, source_target_pairs={{0,24},{8,0},{16,8},{24,16},{1,25},{9,1},{17,9},{25,17},{2,26},{10... | collective-permute-start | bytes 835592 | tf_op jit(solution)/shard_map/ppermute | solution.py:23
  11.0 1.0 collective-permute-start.4
  12.0 6.1 %collective-permute-done.18.refs_0_ = bf16[64,2176]{1,0:T(8,128)(2,1)S(1)} collective-permute-done((bf16[64,2176]{1,0:T(8,128)(2,1)S(1)}, bf16[64,2176]{1,0:T(8,128)(2,1)S(1)}, u32[]{:S(2)}, u32[]{:S(2)}) %collective-permute-start.18) | collective-permute-done | bytes 278560 | tf_op jit(solution)/shard_map/ppermute | solution.py:23
  18.1 1.5 %collective-permute-start.19 = (bf16[64,2176]{1,0:T(8,128)(2,1)S(1)}, bf16[64,2176]{1,0:T(8,128)(2,1)S(1)}, u32[]{:S(2)}, u32[]{:S(2)}) collective-permute-start(bf16[64,2176]{1,0:T(8,128)(2,1)S(1)} %collective-permute-done.18.refs_0_), channel_id=1, source_target_pairs={{0,4},{2,6},{4,0},{6,2},{1,5},{3,7},{5,1},{7,3},{8,12},{10,14},{12... | collective-permute-start | bytes 835592 | tf_op jit(solution)/shard_map/ppermute | solution.py:18
  19.7 5.5 %collective-permute-done.11.refs_0_ = bf16[64,2176]{1,0:T(8,128)(2,1)S(1)} collective-permute-done((bf16[64,2176]{1,0:T(8,128)(2,1)S(1)}, bf16[64,2176]{1,0:T(8,128)(2,1)S(1)}, u32[]{:S(2)}, u32[]{:S(2)}) %collective-permute-start.11) | collective-permute-done | bytes 278560 | tf_op jit(solution)/shard_map/ppermute | solution.py:23
  25.1 1.5 %collective-permute-start.12 = (bf16[64,2176]{1,0:T(8,128)(2,1)S(1)}, bf16[64,2176]{1,0:T(8,128)(2,1)S(1)}, u32[]{:S(2)}, u32[]{:S(2)}) collective-permute-start(bf16[64,2176]{1,0:T(8,128)(2,1)S(1)} %collective-permute-done.11.refs_0_), channel_id=1, source_target_pairs={{0,4},{2,6},{4,0},{6,2},{1,5},{3,7},{5,1},{7,3},{8,12},{10,14},{12... | collective-permute-start | bytes 835592 | tf_op jit(solution)/shard_map/ppermute | solution.py:18
  26.6 7.8 %collective-permute-done.4.refs_0_ = bf16[64,2176]{1,0:T(8,128)(2,1)S(1)} collective-permute-done((bf16[64,2176]{1,0:T(8,128)(2,1)S(1)}, bf16[64,2176]{1,0:T(8,128)(2,1)S(1)}, u32[]{:S(2)}, u32[]{:S(2)}) %collective-permute-start.4) | collective-permute-done | bytes 278560 | tf_op jit(solution)/shard_map/ppermute | solution.py:23
  34.5 1.5 %collective-permute-start.5 = (bf16[64,2176]{1,0:T(8,128)(2,1)S(1)}, bf16[64,2176]{1,0:T(8,128)(2,1)S(1)}, u32[]{:S(2)}, u32[]{:S(2)}) collective-permute-start(bf16[64,2176]{1,0:T(8,128)(2,1)S(1)} %collective-permute-done.4.refs_0_), channel_id=1, source_target_pairs={{0,4},{2,6},{4,0},{6,2},{1,5},{3,7},{5,1},{7,3},{8,12},{10,14},{12... | collective-permute-start | bytes 835592 | tf_op jit(solution)/shard_map/ppermute | solution.py:18
  36.6 1.9 %copy-done = bf16[1,2048,768]{2,1,0:T(8,128)(2,1)S(1)} copy-done((bf16[1,2048,768]{2,1,0:T(8,128)(2,1)S(1)}, bf16[1,2048,768]{2,1,0:T(8,128)(2,1)}, u32[]{:S(2)}) %copy-start) | copy-done | bytes 3145752
  38.5 1.9 %copy-done.2 = bf16[1,2048,768]{2,1,0:T(8,128)(2,1)S(1)} copy-done((bf16[1,2048,768]{2,1,0:T(8,128)(2,1)S(1)}, bf16[1,2048,768]{2,1,0:T(8,128)(2,1)}, u32[]{:S(2)}) %copy-start.2) | copy-done | bytes 3145752
  40.4 1.8 %shard_map.65 = (bf16[256,768]{1,0:T(8,128)(2,1)S(1)}, f32[256,128]{1,0:T(8,128)S(1)}) custom-call(bf16[256,2048]{1,0:T(8,128)(2,1)S(1)} %copy-done.4, bf16[256,128]{1,0:T(8,128)(2,1)S(1)} %get-tuple-element.25.refs_1_, bf16[2048,768]{1,0:T(8,128)(2,1)S(1)} %bitcast.13, bf16[2048,768]{1,0:T(8,128)(2,1)S(1)} %bitcast.17), custom_call_target="tpu_custom_call" | custom-call | flops 1610612736 | bytes 7929856 | tf_op jit(solution)/shard_map/pallas_call | solution.py:39
  43.9 1.8 %shard_map.74 = (bf16[256,768]{1,0:T(8,128)(2,1)S(1)}, f32[256,128]{1,0:T(8,128)S(1)}) custom-call(bf16[64,2176]{1,0:T(8,128)(2,1)S(1)} %collective-permute-done.18.refs_0_, bf16[64,2176]{1,0:T(8,128)(2,1)S(1)} %collective-permute-done.19.refs_1_, bf16[64,2176]{1,0:T(8,128)(2,1)S(1)} %collective-permute-done.20.refs_2_, ...), custom_call_target="tpu_custom_call" | custom-call | flops 1610612736 | bytes 7929856 | tf_op jit(solution)/shard_map/pallas_call | solution.py:39
  46.9 1.8 %shard_map.71 = (bf16[256,768]{1,0:T(8,128)(2,1)S(1)}, f32[256,128]{1,0:T(8,128)S(1)}) custom-call(bf16[64,2176]{1,0:T(8,128)(2,1)S(1)} %collective-permute-done.11.refs_0_, bf16[64,2176]{1,0:T(8,128)(2,1)S(1)} %collective-permute-done.12.refs_1_, bf16[64,2176]{1,0:T(8,128)(2,1)S(1)} %collective-permute-done.13.refs_2_, ...), custom_call_target="tpu_custom_call" | custom-call | flops 1610612736 | bytes 7929856 | tf_op jit(solution)/shard_map/pallas_call | solution.py:39
  49.5 1.8 %shard_map.68 = (bf16[256,768]{1,0:T(8,128)(2,1)S(1)}, f32[256,128]{1,0:T(8,128)S(1)}) custom-call(bf16[64,2176]{1,0:T(8,128)(2,1)S(1)} %collective-permute-done.4.refs_0_, bf16[64,2176]{1,0:T(8,128)(2,1)S(1)} %collective-permute-done.5.refs_1_, bf16[64,2176]{1,0:T(8,128)(2,1)S(1)} %collective-permute-done.6.refs_2_, ...), custom_call_target="tpu_custom_call" | custom-call | flops 1610612736 | bytes 7929856 | tf_op jit(solution)/shard_map/pallas_call | solution.py:39
  52.4 10.4 %collective-permute-done.2.refs_2_ = bf16[768,512]{1,0:T(8,128)(2,1)S(1)} collective-permute-done((bf16[768,512]{1,0:T(8,128)(2,1)S(1)}, bf16[768,512]{1,0:T(8,128)(2,1)S(1)}, u32[]{:S(2)}, u32[]{:S(2)}) %collective-permute-start.2) | collective-permute-done | bytes 786464 | tf_op jit(solution)/shard_map/ppermute | solution.py:18
  62.7 0.7 shard_map.76
  64.6 1.6 %collective-permute-start.3 = (bf16[1,256,512]{2,1,0:T(8,128)(2,1)S(1)}, bf16[1,256,512]{2,1,0:T(8,128)(2,1)S(1)}, u32[]{:S(2)}, u32[]{:S(2)}) collective-permute-start(bf16[1,256,512]{2,1,0:T(8,128)(2,1)S(1)} %get-tuple-element.31), channel_id=1, source_target_pairs={{0,4},{2,6},{4,0},{6,2},{1,5},{3,7},{5,1},{7,3},{8,12},{10,14},{12... | collective-permute-start | bytes 786440 | tf_op jit(solution)/shard_map/ppermute | solution.py:18
  68.1 1.6 %collective-permute-start.9 = (bf16[1,256,512]{2,1,0:T(8,128)(2,1)S(1)}, bf16[1,256,512]{2,1,0:T(8,128)(2,1)S(1)}, u32[]{:S(2)}, u32[]{:S(2)}) collective-permute-start(bf16[1,256,512]{2,1,0:T(8,128)(2,1)S(1)} %get-tuple-element.36), channel_id=1, source_target_pairs={{0,4},{2,6},{4,0},{6,2},{1,5},{3,7},{5,1},{7,3},{8,12},{10,14},{12... | collective-permute-start | bytes 786440 | tf_op jit(solution)/shard_map/ppermute | solution.py:18
  69.7 3.0 %collective-permute-done.23 = bf16[1,256,512]{2,1,0:T(8,128)(2,1)S(1)} collective-permute-done((bf16[1,256,512]{2,1,0:T(8,128)(2,1)S(1)}, bf16[1,256,512]{2,1,0:T(8,128)(2,1)S(1)}, u32[]{:S(2)}, u32[]{:S(2)}) %collective-permute-start.23) | collective-permute-done | bytes 262176 | tf_op jit(solution)/shard_map/ppermute | solution.py:18
  72.8 6.6 %collective-permute-start.24 = (bf16[256,512]{1,0:T(8,128)(2,1)S(1)}, bf16[256,512]{1,0:T(8,128)(2,1)S(1)}, u32[]{:S(2)}, u32[]{:S(2)}) collective-permute-start(bf16[256,512]{1,0:T(8,128)(2,1)S(1)} %fusion.2), channel_id=1, source_target_pairs={{0,8},{8,16},{16,24},{24,0},{1,9},{9,17},{17,25},{25,1},{2,10},{10... | collective-permute-start | bytes 786440 | tf_op jit(solution)/shard_map/ppermute | solution.py:23
  79.4 4.6 %collective-permute-done.16 = bf16[1,256,512]{2,1,0:T(8,128)(2,1)S(1)} collective-permute-done((bf16[1,256,512]{2,1,0:T(8,128)(2,1)S(1)}, bf16[1,256,512]{2,1,0:T(8,128)(2,1)S(1)}, u32[]{:S(2)}, u32[]{:S(2)}) %collective-permute-start.16) | collective-permute-done | bytes 262176 | tf_op jit(solution)/shard_map/ppermute | solution.py:18
  84.0 2.7 %collective-permute-start.17 = (bf16[256,512]{1,0:T(8,128)(2,1)S(1)}, bf16[256,512]{1,0:T(8,128)(2,1)S(1)}, u32[]{:S(2)}, u32[]{:S(2)}) collective-permute-start(bf16[256,512]{1,0:T(8,128)(2,1)S(1)} %fusion.1), channel_id=1, source_target_pairs={{0,24},{8,0},{16,8},{24,16},{1,25},{9,1},{17,9},{25,17},{2,26},{10... | collective-permute-start | bytes 786440 | tf_op jit(solution)/shard_map/ppermute | solution.py:23
  86.7 1.5 %collective-permute-done.9 = bf16[1,256,512]{2,1,0:T(8,128)(2,1)S(1)} collective-permute-done((bf16[1,256,512]{2,1,0:T(8,128)(2,1)S(1)}, bf16[1,256,512]{2,1,0:T(8,128)(2,1)S(1)}, u32[]{:S(2)}, u32[]{:S(2)}) %collective-permute-start.9) | collective-permute-done | bytes 262176 | tf_op jit(solution)/shard_map/ppermute | solution.py:18
  88.3 4.0 %collective-permute-start.10 = (bf16[256,512]{1,0:T(8,128)(2,1)S(1)}, bf16[256,512]{1,0:T(8,128)(2,1)S(1)}, u32[]{:S(2)}, u32[]{:S(2)}) collective-permute-start(bf16[256,512]{1,0:T(8,128)(2,1)S(1)} %fusion), channel_id=1, source_target_pairs={{0,16},{8,24},{16,0},{24,8},{1,17},{9,25},{17,1},{25,9},{2,18},{10... | collective-permute-start | bytes 786440 | tf_op jit(solution)/shard_map/ppermute | solution.py:23
  92.2 5.2 %collective-permute-done.17.refs_1_ = bf16[256,512]{1,0:T(8,128)(2,1)S(1)} collective-permute-done((bf16[256,512]{1,0:T(8,128)(2,1)S(1)}, bf16[256,512]{1,0:T(8,128)(2,1)S(1)}, u32[]{:S(2)}, u32[]{:S(2)}) %collective-permute-start.17) | collective-permute-done | bytes 262176 | tf_op jit(solution)/shard_map/ppermute | solution.py:23
  97.4 8.4 %collective-permute-done.10.refs_0_ = bf16[256,512]{1,0:T(8,128)(2,1)S(1)} collective-permute-done((bf16[256,512]{1,0:T(8,128)(2,1)S(1)}, bf16[256,512]{1,0:T(8,128)(2,1)S(1)}, u32[]{:S(2)}, u32[]{:S(2)}) %collective-permute-start.10) | collective-permute-done | bytes 262176 | tf_op jit(solution)/shard_map/ppermute | solution.py:23
  105.8 0.9 shard_map.77
  (51 shorter events, 9.0 us)
Async XLA Ops:
  0.0 1.2 %copy-start.4 = (bf16[256,2048]{1,0:T(8,128)(2,1)S(1)}, bf16[256,2048]{1,0:T(8,128)(2,1)}, u32[]{:S(2)}) copy-start(bf16[256,2048]{1,0:T(8,128)(2,1)} %refs_0_.1) | copy-start | bytes 3145732
  1.2 1.4 %copy-start.5 = (bf16[1,768,1024]{2,1,0:T(8,128)(2,1)S(1)}, bf16[1,768,1024]{2,1,0:T(8,128)(2,1)}, u32[]{:S(2)}) copy-start(bf16[1,768,1024]{2,1,0:T(8,128)(2,1)} %param.11) | copy-start | bytes 4718596
  2.6 0.7 copy-start.6
  4.4 32.1 %collective-permute-start = (bf16[768,512]{1,0:T(8,128)(2,1)S(1)}, bf16[768,512]{1,0:T(8,128)(2,1)S(1)}, u32[]{:S(2)}, u32[]{:S(2)}) collective-permute-start(bf16[768,512]{1,0:T(8,128)(2,1)S(1)} %get-tuple-element.28.refs_0_), channel_id=1, source_target_pairs={{0,1},{1,0},{2,3},{3,2},{4,5},{5,4},{6,7},{7,6},{8,9},{9,8},{10,11... | collective-permute-start | bytes 2359304 | tf_op jit(solution)/shard_map/ppermute | solution.py:18
  7.4 10.7 %collective-permute-start.18 = (bf16[64,2176]{1,0:T(8,128)(2,1)S(1)}, bf16[64,2176]{1,0:T(8,128)(2,1)S(1)}, u32[]{:S(2)}, u32[]{:S(2)}) collective-permute-start(bf16[64,2176]{1,0:T(8,128)(2,1)S(1)} %get-tuple-element.32), channel_id=1, source_target_pairs={{0,24},{8,0},{16,8},{24,16},{1,25},{9,1},{17,9},{25,17},{2,26},{10... | collective-permute-start | bytes 835592 | tf_op jit(solution)/shard_map/ppermute | solution.py:23
  11.0 14.1 %collective-permute-start.11 = (bf16[64,2176]{1,0:T(8,128)(2,1)S(1)}, bf16[64,2176]{1,0:T(8,128)(2,1)S(1)}, u32[]{:S(2)}, u32[]{:S(2)}) collective-permute-start(bf16[64,2176]{1,0:T(8,128)(2,1)S(1)} %get-tuple-element.32), channel_id=1, source_target_pairs={{0,8},{8,16},{16,24},{24,0},{1,9},{9,17},{17,25},{25,1},{2,10},{10... | collective-permute-start | bytes 835592 | tf_op jit(solution)/shard_map/ppermute | solution.py:23
  11.0 23.4 %collective-permute-start.4 = (bf16[64,2176]{1,0:T(8,128)(2,1)S(1)}, bf16[64,2176]{1,0:T(8,128)(2,1)S(1)}, u32[]{:S(2)}, u32[]{:S(2)}) collective-permute-start(bf16[64,2176]{1,0:T(8,128)(2,1)S(1)} %get-tuple-element.32), channel_id=1, source_target_pairs={{0,16},{8,24},{16,0},{24,8},{1,17},{9,25},{17,1},{25,9},{2,18},{10... | collective-permute-start | bytes 835592 | tf_op jit(solution)/shard_map/ppermute | solution.py:23
  18.1 17.9 %collective-permute-start.19 = (bf16[64,2176]{1,0:T(8,128)(2,1)S(1)}, bf16[64,2176]{1,0:T(8,128)(2,1)S(1)}, u32[]{:S(2)}, u32[]{:S(2)}) collective-permute-start(bf16[64,2176]{1,0:T(8,128)(2,1)S(1)} %collective-permute-done.18.refs_0_), channel_id=1, source_target_pairs={{0,4},{2,6},{4,0},{6,2},{1,5},{3,7},{5,1},{7,3},{8,12},{10,14},{12... | collective-permute-start | bytes 835592 | tf_op jit(solution)/shard_map/ppermute | solution.py:18
  25.1 10.9 %collective-permute-start.12 = (bf16[64,2176]{1,0:T(8,128)(2,1)S(1)}, bf16[64,2176]{1,0:T(8,128)(2,1)S(1)}, u32[]{:S(2)}, u32[]{:S(2)}) collective-permute-start(bf16[64,2176]{1,0:T(8,128)(2,1)S(1)} %collective-permute-done.11.refs_0_), channel_id=1, source_target_pairs={{0,4},{2,6},{4,0},{6,2},{1,5},{3,7},{5,1},{7,3},{8,12},{10,14},{12... | collective-permute-start | bytes 835592 | tf_op jit(solution)/shard_map/ppermute | solution.py:18
  26.6 16.1 %collective-permute-start.20 = (bf16[64,2176]{1,0:T(8,128)(2,1)S(1)}, bf16[64,2176]{1,0:T(8,128)(2,1)S(1)}, u32[]{:S(2)}, u32[]{:S(2)}) collective-permute-start(bf16[64,2176]{1,0:T(8,128)(2,1)S(1)} %collective-permute-done.18.refs_0_), channel_id=1, source_target_pairs={{0,2},{2,0},{4,6},{6,4},{1,3},{3,1},{5,7},{7,5},{8,10},{10,8},{12,... | collective-permute-start | bytes 835592 | tf_op jit(solution)/shard_map/ppermute | solution.py:18
  34.5 8.9 %collective-permute-start.5 = (bf16[64,2176]{1,0:T(8,128)(2,1)S(1)}, bf16[64,2176]{1,0:T(8,128)(2,1)S(1)}, u32[]{:S(2)}, u32[]{:S(2)}) collective-permute-start(bf16[64,2176]{1,0:T(8,128)(2,1)S(1)} %collective-permute-done.4.refs_0_), channel_id=1, source_target_pairs={{0,4},{2,6},{4,0},{6,2},{1,5},{3,7},{5,1},{7,3},{8,12},{10,14},{12... | collective-permute-start | bytes 835592 | tf_op jit(solution)/shard_map/ppermute | solution.py:18
  36.0 7.6 %collective-permute-start.21 = (bf16[64,2176]{1,0:T(8,128)(2,1)S(1)}, bf16[64,2176]{1,0:T(8,128)(2,1)S(1)}, u32[]{:S(2)}, u32[]{:S(2)}) collective-permute-start(bf16[64,2176]{1,0:T(8,128)(2,1)S(1)} %collective-permute-done.19.refs_1_), channel_id=1, source_target_pairs={{0,2},{2,0},{4,6},{6,4},{1,3},{3,1},{5,7},{7,5},{8,10},{10,8},{12,... | collective-permute-start | bytes 835592 | tf_op jit(solution)/shard_map/ppermute | solution.py:18
  36.0 10.3 %collective-permute-start.13 = (bf16[64,2176]{1,0:T(8,128)(2,1)S(1)}, bf16[64,2176]{1,0:T(8,128)(2,1)S(1)}, u32[]{:S(2)}, u32[]{:S(2)}) collective-permute-start(bf16[64,2176]{1,0:T(8,128)(2,1)S(1)} %collective-permute-done.11.refs_0_), channel_id=1, source_target_pairs={{0,2},{2,0},{4,6},{6,4},{1,3},{3,1},{5,7},{7,5},{8,10},{10,8},{12,... | collective-permute-start | bytes 835592 | tf_op jit(solution)/shard_map/ppermute | solution.py:18
  36.5 10.0 %collective-permute-start.14 = (bf16[64,2176]{1,0:T(8,128)(2,1)S(1)}, bf16[64,2176]{1,0:T(8,128)(2,1)S(1)}, u32[]{:S(2)}, u32[]{:S(2)}) collective-permute-start(bf16[64,2176]{1,0:T(8,128)(2,1)S(1)} %collective-permute-done.12.refs_1_), channel_id=1, source_target_pairs={{0,2},{2,0},{4,6},{6,4},{1,3},{3,1},{5,7},{7,5},{8,10},{10,8},{12,... | collective-permute-start | bytes 835592 | tf_op jit(solution)/shard_map/ppermute | solution.py:18
  36.6 1.9 %copy-start = (bf16[1,2048,768]{2,1,0:T(8,128)(2,1)S(1)}, bf16[1,2048,768]{2,1,0:T(8,128)(2,1)}, u32[]{:S(2)}) copy-start(bf16[1,2048,768]{2,1,0:T(8,128)(2,1)} %param.9) | copy-start | bytes 9437188
  38.5 1.9 %copy-start.2 = (bf16[1,2048,768]{2,1,0:T(8,128)(2,1)S(1)}, bf16[1,2048,768]{2,1,0:T(8,128)(2,1)}, u32[]{:S(2)}) copy-start(bf16[1,2048,768]{2,1,0:T(8,128)(2,1)} %param.10) | copy-start | bytes 9437188
  40.4 3.5 %copy-start.1 = (bf16[1,2048,768]{2,1,0:T(8,128)(2,1)S(1)}, bf16[1,2048,768]{2,1,0:T(8,128)(2,1)}, u32[]{:S(2)}) copy-start(bf16[1,2048,768]{2,1,0:T(8,128)(2,1)} %param.9) | copy-start | bytes 9437188
  40.4 3.5 %copy-start.3 = (bf16[1,2048,768]{2,1,0:T(8,128)(2,1)S(1)}, bf16[1,2048,768]{2,1,0:T(8,128)(2,1)}, u32[]{:S(2)}) copy-start(bf16[1,2048,768]{2,1,0:T(8,128)(2,1)} %param.10) | copy-start | bytes 9437188
  42.8 20.0 %collective-permute-start.2 = (bf16[768,512]{1,0:T(8,128)(2,1)S(1)}, bf16[768,512]{1,0:T(8,128)(2,1)S(1)}, u32[]{:S(2)}, u32[]{:S(2)}) collective-permute-start(bf16[768,512]{1,0:T(8,128)(2,1)S(1)} %get-tuple-element.29.refs_1_), channel_id=1, source_target_pairs={{0,1},{1,0},{2,3},{3,2},{4,5},{5,4},{6,7},{7,6},{8,9},{9,8},{10,11... | collective-permute-start | bytes 2359304 | tf_op jit(solution)/shard_map/ppermute | solution.py:18
  43.4 5.9 %collective-permute-start.6 = (bf16[64,2176]{1,0:T(8,128)(2,1)S(1)}, bf16[64,2176]{1,0:T(8,128)(2,1)S(1)}, u32[]{:S(2)}, u32[]{:S(2)}) collective-permute-start(bf16[64,2176]{1,0:T(8,128)(2,1)S(1)} %collective-permute-done.4.refs_0_), channel_id=1, source_target_pairs={{0,2},{2,0},{4,6},{6,4},{1,3},{3,1},{5,7},{7,5},{8,10},{10,8},{12,... | collective-permute-start | bytes 835592 | tf_op jit(solution)/shard_map/ppermute | solution.py:18
  43.6 6.0 %collective-permute-start.7 = (bf16[64,2176]{1,0:T(8,128)(2,1)S(1)}, bf16[64,2176]{1,0:T(8,128)(2,1)S(1)}, u32[]{:S(2)}, u32[]{:S(2)}) collective-permute-start(bf16[64,2176]{1,0:T(8,128)(2,1)S(1)} %collective-permute-done.5.refs_1_), channel_id=1, source_target_pairs={{0,2},{2,0},{4,6},{6,4},{1,3},{3,1},{5,7},{7,5},{8,10},{10,8},{12,... | collective-permute-start | bytes 835592 | tf_op jit(solution)/shard_map/ppermute | solution.py:18
  46.3 17.7 %collective-permute-start.1 = (bf16[2,256,512]{2,1,0:T(8,128)(2,1)S(1)}, bf16[2,256,512]{2,1,0:T(8,128)(2,1)S(1)}, u32[]{:S(2)}, u32[]{:S(2)}) collective-permute-start(bf16[2,256,512]{2,1,0:T(8,128)(2,1)S(1)} %shard_map.66), channel_id=1, source_target_pairs={{0,2},{2,0},{4,6},{6,4},{1,3},{3,1},{5,7},{7,5},{8,10},{10,8},{12,... | collective-permute-start | bytes 1572872 | tf_op jit(solution)/shard_map/ppermute | solution.py:18
  46.6 16.2 %collective-permute-start.22 = (bf16[2,256,512]{2,1,0:T(8,128)(2,1)S(1)}, bf16[2,256,512]{2,1,0:T(8,128)(2,1)S(1)}, u32[]{:S(2)}, u32[]{:S(2)}) collective-permute-start(bf16[2,256,512]{2,1,0:T(8,128)(2,1)S(1)} %shard_map.75), channel_id=1, source_target_pairs={{0,2},{2,0},{4,6},{6,4},{1,3},{3,1},{5,7},{7,5},{8,10},{10,8},{12,... | collective-permute-start | bytes 1572872 | tf_op jit(solution)/shard_map/ppermute | solution.py:18
  49.3 16.9 %collective-permute-start.15 = (bf16[2,256,512]{2,1,0:T(8,128)(2,1)S(1)}, bf16[2,256,512]{2,1,0:T(8,128)(2,1)S(1)}, u32[]{:S(2)}, u32[]{:S(2)}) collective-permute-start(bf16[2,256,512]{2,1,0:T(8,128)(2,1)S(1)} %shard_map.72), channel_id=1, source_target_pairs={{0,2},{2,0},{4,6},{6,4},{1,3},{3,1},{5,7},{7,5},{8,10},{10,8},{12,... | collective-permute-start | bytes 1572872 | tf_op jit(solution)/shard_map/ppermute | solution.py:18
  52.0 15.5 %collective-permute-start.8 = (bf16[2,256,512]{2,1,0:T(8,128)(2,1)S(1)}, bf16[2,256,512]{2,1,0:T(8,128)(2,1)S(1)}, u32[]{:S(2)}, u32[]{:S(2)}) collective-permute-start(bf16[2,256,512]{2,1,0:T(8,128)(2,1)S(1)} %shard_map.69), channel_id=1, source_target_pairs={{0,2},{2,0},{4,6},{6,4},{1,3},{3,1},{5,7},{7,5},{8,10},{10,8},{12,... | collective-permute-start | bytes 1572872 | tf_op jit(solution)/shard_map/ppermute | solution.py:18
  63.4 9.3 %collective-permute-start.23 = (bf16[1,256,512]{2,1,0:T(8,128)(2,1)S(1)}, bf16[1,256,512]{2,1,0:T(8,128)(2,1)S(1)}, u32[]{:S(2)}, u32[]{:S(2)}) collective-permute-start(bf16[1,256,512]{2,1,0:T(8,128)(2,1)S(1)} %get-tuple-element.44), channel_id=1, source_target_pairs={{0,4},{2,6},{4,0},{6,2},{1,5},{3,7},{5,1},{7,3},{8,12},{10,14},{12... | collective-permute-start | bytes 786440 | tf_op jit(solution)/shard_map/ppermute | solution.py:18
  64.6 27.6 %collective-permute-start.3 = (bf16[1,256,512]{2,1,0:T(8,128)(2,1)S(1)}, bf16[1,256,512]{2,1,0:T(8,128)(2,1)S(1)}, u32[]{:S(2)}, u32[]{:S(2)}) collective-permute-start(bf16[1,256,512]{2,1,0:T(8,128)(2,1)S(1)} %get-tuple-element.31), channel_id=1, source_target_pairs={{0,4},{2,6},{4,0},{6,2},{1,5},{3,7},{5,1},{7,3},{8,12},{10,14},{12... | collective-permute-start | bytes 786440 | tf_op jit(solution)/shard_map/ppermute | solution.py:18
  66.9 17.0 %collective-permute-start.16 = (bf16[1,256,512]{2,1,0:T(8,128)(2,1)S(1)}, bf16[1,256,512]{2,1,0:T(8,128)(2,1)S(1)}, u32[]{:S(2)}, u32[]{:S(2)}) collective-permute-start(bf16[1,256,512]{2,1,0:T(8,128)(2,1)S(1)} %get-tuple-element.40), channel_id=1, source_target_pairs={{0,4},{2,6},{4,0},{6,2},{1,5},{3,7},{5,1},{7,3},{8,12},{10,14},{12... | collective-permute-start | bytes 786440 | tf_op jit(solution)/shard_map/ppermute | solution.py:18
  68.1 20.1 %collective-permute-start.9 = (bf16[1,256,512]{2,1,0:T(8,128)(2,1)S(1)}, bf16[1,256,512]{2,1,0:T(8,128)(2,1)S(1)}, u32[]{:S(2)}, u32[]{:S(2)}) collective-permute-start(bf16[1,256,512]{2,1,0:T(8,128)(2,1)S(1)} %get-tuple-element.36), channel_id=1, source_target_pairs={{0,4},{2,6},{4,0},{6,2},{1,5},{3,7},{5,1},{7,3},{8,12},{10,14},{12... | collective-permute-start | bytes 786440 | tf_op jit(solution)/shard_map/ppermute | solution.py:18
  72.8 19.5 %collective-permute-start.24 = (bf16[256,512]{1,0:T(8,128)(2,1)S(1)}, bf16[256,512]{1,0:T(8,128)(2,1)S(1)}, u32[]{:S(2)}, u32[]{:S(2)}) collective-permute-start(bf16[256,512]{1,0:T(8,128)(2,1)S(1)} %fusion.2), channel_id=1, source_target_pairs={{0,8},{8,16},{16,24},{24,0},{1,9},{9,17},{17,25},{25,1},{2,10},{10... | collective-permute-start | bytes 786440 | tf_op jit(solution)/shard_map/ppermute | solution.py:23
  84.0 13.4 %collective-permute-start.17 = (bf16[256,512]{1,0:T(8,128)(2,1)S(1)}, bf16[256,512]{1,0:T(8,128)(2,1)S(1)}, u32[]{:S(2)}, u32[]{:S(2)}) collective-permute-start(bf16[256,512]{1,0:T(8,128)(2,1)S(1)} %fusion.1), channel_id=1, source_target_pairs={{0,24},{8,0},{16,8},{24,16},{1,25},{9,1},{17,9},{25,17},{2,26},{10... | collective-permute-start | bytes 786440 | tf_op jit(solution)/shard_map/ppermute | solution.py:23
  88.3 17.6 %collective-permute-start.10 = (bf16[256,512]{1,0:T(8,128)(2,1)S(1)}, bf16[256,512]{1,0:T(8,128)(2,1)S(1)}, u32[]{:S(2)}, u32[]{:S(2)}) collective-permute-start(bf16[256,512]{1,0:T(8,128)(2,1)S(1)} %fusion), channel_id=1, source_target_pairs={{0,16},{8,24},{16,0},{24,8},{1,17},{9,25},{17,1},{25,9},{2,18},{10... | collective-permute-start | bytes 786440 | tf_op jit(solution)/shard_map/ppermute | solution.py:23
  (1 other events, 0.7 us)

commit v4 on v3

v4 whole, which is shorter than its diff:
```python
import functools

import jax
import jax.numpy as jnp
from jax import lax
from jax.experimental import pallas as pl
from jax.experimental.pallas import tpu as pltpu
from jax.sharding import PartitionSpec as P

VM = pl.BlockSpec(memory_space=pltpu.VMEM)
HBM = pl.BlockSpec(memory_space=pltpu.HBM)
STEP = 256
LANES = 128


def swap_bit(value, axis, bit):
    size = lax.axis_size(axis)
    return lax.ppermute(value, axis, [(i, i ^ bit) for i in range(size)])


def after(value, *others):
    return lax.optimization_barrier((value, others))[0]


def bits_of(size):
    return [1 << i for i in range(size.bit_length() - 1)]


def part_order(size):
    order = [0]
    for bit in reversed(bits_of(size)):
        order = order + [i ^ bit for i in order]
    return order


def call(kernel, outs, arrays, scratch=(), in_specs=None, out_specs=None, flops=None):
    moved = sum(a.size * a.dtype.itemsize for a in (*arrays, *jax.tree.leaves(outs)))
    cost = pl.CostEstimate(flops=flops or 0, bytes_accessed=moved, transcendentals=0)
    return pl.pallas_call(
        kernel,
        out_shape=outs,
        in_specs=in_specs or [VM] * len(arrays),
        out_specs=out_specs or jax.tree.map(lambda _: VM, outs),
        scratch_shapes=list(scratch),
        compiler_params=pltpu.CompilerParams(vmem_limit_bytes=12 << 20),
    )(*arrays)


def rows_at(index, part):
    return pl.ds(pl.multiple_of(index * part, part), part)


def own_expert():
    return lax.axis_index("grp") * lax.axis_size("loc") + lax.axis_index("loc")


def prepare_kernel(part, tokens, ids, weights, message, table, ids_here, weights_here, sems):
    width = tokens.shape[1]
    local = lax.axis_index("loc")
    copies = [
        pltpu.make_async_copy(ids, ids_here, sems.at[0]),
        pltpu.make_async_copy(weights, weights_here, sems.at[1]),
        pltpu.make_async_copy(tokens.at[rows_at(local, part), :], message.at[:, :width], sems.at[2]),
    ]
    for copy in copies:
        copy.start()
    lanes, rows = table.shape[1], table.shape[0]
    expert = lax.broadcasted_iota(jnp.int32, (lanes, rows), 0)
    dense = jnp.zeros((lanes, rows), jnp.float32)
    copies[0].wait()
    copies[1].wait()
    for k in range(ids.shape[0]):
        weight = weights_here[k : k + 1, :].astype(jnp.float32)
        dense = jnp.where(expert == ids_here[k : k + 1, :], weight, dense)
    table[...] = dense.T.astype(jnp.bfloat16)
    message[:, width:] = table[rows_at(local, part), :]
    copies[2].wait()


def hidden_kernel(order, part, *refs):
    *pieces, gate, up, hidden, scale, block, routes, sems = refs
    width = gate.shape[0]
    local = lax.axis_index("loc")
    copies = []
    for n, k in enumerate(order):
        at = slice(n * part, (n + 1) * part)
        if len(pieces) == 2:
            whole = pieces[0].at[rows_at(local ^ k, part), :]
            copies.append(pltpu.make_async_copy(whole, block.at[at, :], sems.at[n]))
            copies[n].start()
            routes[at, :] = pieces[1][rows_at(local ^ k, part), :].astype(jnp.float32)
        else:
            block[at, :] = pieces[n][:, :width]
            routes[at, :] = pieces[n][:, width:].astype(jnp.float32)
    expert = lax.broadcasted_iota(jnp.int32, routes.shape, 1)
    own = jnp.sum(jnp.where(expert == own_expert(), routes[...], 0.0), axis=1, keepdims=True)
    scale[...] = jnp.broadcast_to(own, scale.shape)
    for copy in copies:
        copy.wait()
    for j in range(0, gate.shape[1], STEP):
        a = jnp.dot(block[...], gate[:, j : j + STEP], preferred_element_type=jnp.float32)
        b = jnp.dot(block[...], up[:, j : j + STEP], preferred_element_type=jnp.float32)
        hidden[:, j : j + STEP] = (a / (1.0 + jnp.exp(-a)) * b).astype(jnp.bfloat16)


def column_results(hidden, scale, shards, cols, part_of):
    per_shard = shards[0].shape[1] // cols
    first = (lax.axis_index("loc") % per_shard) ^ part_of
    own = lax.axis_index("tp") ^ (lax.axis_index("loc") // per_shard)
    factor = scale[...]
    for u, weights in enumerate(shards):
        for j in range(0, cols, STEP):
            at = pl.ds(pl.multiple_of(first * cols + j, STEP), STEP)
            out = jnp.dot(hidden[...], weights[:, at], preferred_element_type=jnp.float32)
            out = out.astype(jnp.bfloat16).astype(jnp.float32)
            out = [out[:, i : i + LANES] * factor for i in range(0, STEP, LANES)]
            yield own ^ u, slice(j, j + STEP), jnp.concatenate(out, axis=1)


def leave_kernel(order, part, bit, hidden, scale, *refs):
    *shards, message = refs
    for place, cols, value in column_results(hidden, scale, shards, message.shape[2], bit):
        value = value.astype(jnp.bfloat16)
        for n, k in enumerate(order):
            m = order.index(k ^ bit)
            message[place, n * part : (n + 1) * part, cols] = value[m * part : (m + 1) * part]


def stay_kernel(order, part, bit, with_sum, hidden, scale, *refs):
    if with_sum:
        arrived, *refs = refs
    *shards, keep, message, total = refs
    half = len(shards) // 2
    for place, cols, value in column_results(hidden, scale, shards, total.shape[2], 0):
        if with_sum:
            value = value + arrived[place, :, cols].astype(jnp.float32)
        total[place, :, cols] = value
    for i in range(half):
        keep[i] = total[i]
        for n, k in enumerate(order):
            m = order.index(k ^ bit)
            message[i, n * part : (n + 1) * part, :] = total[half + i, m * part : (m + 1) * part, :].astype(
                jnp.bfloat16
            )


def finish_kernel(order, part, keep, arrived, *refs):
    *others, out = refs
    local = lax.axis_index("loc")
    for n, k in enumerate(order):
        at = slice(n * part, (n + 1) * part)
        value = keep[at, :] + arrived[at, :].astype(jnp.float32)
        for other in others:
            value = value + other[at, :].astype(jnp.float32)
        out[rows_at(local ^ k, part), :] = value.astype(jnp.bfloat16)


def body(tokens, expert_ids, router_weights, w_gate, w_up, w_down):
    groups = lax.axis_size("grp")
    group_size = lax.axis_size("loc")
    tp_size = lax.axis_size("tp")
    rows, width = tokens.shape
    hidden_width = w_gate.shape[2]
    part = rows // group_size
    out_cols = width // group_size
    per_shard = group_size // tp_size
    lanes = -(-groups * group_size // LANES) * LANES
    order = part_order(group_size)
    partners = [1] + list(range(groups - 1, 1, -1))
    shape = jax.ShapeDtypeStruct
    bf16, f32 = jnp.bfloat16, jnp.float32

    message, table = call(
        functools.partial(prepare_kernel, part),
        (shape((part, width + lanes), bf16), shape((rows, lanes), bf16)),
        (tokens, expert_ids.T, router_weights.T),
        in_specs=[HBM] * 3,
        scratch=[
            pltpu.VMEM(expert_ids.shape[::-1], jnp.int32),
            pltpu.VMEM(router_weights.shape[::-1], bf16),
            pltpu.SemaphoreType.DMA((3,)),
        ],
    )

    down = [w_down[0]]
    for bit in bits_of(tp_size):
        down = down + [swap_bit(value, "tp", bit) for value in down]

    def ffn(pieces):
        return call(
            functools.partial(hidden_kernel, order, part),
            (shape((rows, hidden_width), bf16), shape((rows, LANES), f32)),
            (*pieces, w_gate[0], w_up[0]),
            in_specs=[HBM] + [VM] * 3 if len(pieces) == 2 else None,
            scratch=[
                pltpu.VMEM((rows, width), bf16),
                pltpu.VMEM((rows, lanes), f32),
                pltpu.SemaphoreType.DMA((len(order),)),
            ],
            flops=4 * rows * width * hidden_width,
        )

    flops = 2 * rows * hidden_width * out_cols * tp_size

    def leave(hidden, scale):
        message = call(
            functools.partial(leave_kernel, order, part, 1),
            shape((tp_size, rows, out_cols), bf16),
            (hidden, scale, *down),
            flops=flops,
        )
        return swap_bit(message, "loc", 1)

    def stay(hidden, scale, arrived):
        half = tp_size // 2
        return call(
            functools.partial(stay_kernel, order, part, half * per_shard, len(arrived) > 0),
            (shape((half, rows, out_cols), f32), shape((half, rows, out_cols), bf16)),
            (hidden, scale, *arrived, *down),
            scratch=[pltpu.VMEM((tp_size, rows, out_cols), f32)],
            flops=flops,
        )

    def across(keep, message):
        half = tp_size // 2
        arrived = swap_bit(message, "loc", half * per_shard)
        while half > 1:
            half = half // 2
            keep = keep + arrived.astype(f32)
            bit = half * per_shard
            there = [order.index(k ^ bit) for k in order]
            message = keep[half:].astype(bf16).reshape(half, group_size, part, out_cols)
            message = jnp.stack([message[:, m] for m in there], axis=1)
            arrived = swap_bit(message.reshape(half, rows, out_cols), "loc", bit)
            keep = keep[:half]
        return keep[0], arrived[0]

    sent, hidden = {}, {0: ffn([tokens, table])}
    for s in partners:
        sent[s] = swap_bit(message, "grp", s)
    for n, s in enumerate(partners):
        pieces = [after(sent[s], hidden[0])]
        for bit in reversed(bits_of(group_size)):
            if n > 0 and bit == 1:
                pieces[1:] = [after(value, hidden[partners[n - 1]]) for value in pieces[1:]]
            pieces = pieces + [swap_bit(value, "loc", bit) for value in pieces]
        hidden[s] = ffn(pieces)

    turns = partners[1:2] + partners[:1] + partners[2:] + [0]
    left, stayed, sums, back = {}, {}, {}, {}

    def first_half(n):
        if n < len(turns):
            s = turns[n]
            order_after = [stayed[turns[n - 2]]] if n > 1 else [left[turns[n - 1]]] if n > 0 else []
            left[s] = [leave(*after(hidden[s], *order_after))] if per_shard == 2 else []

    first_half(0)
    first_half(1)
    for n, s in enumerate(turns):
        order_after = [stayed[turns[n - 1]]] if n > 0 else []
        stayed[s] = stay(*after(hidden[s], *order_after), left[s])
        first_half(n + 2)
    for n, s in enumerate(turns):
        keep, message = stayed[s]
        if n > 1:
            message = after(message, sums[turns[n - 2]][1])
        keep, arrived = across(keep, message)
        sums[s] = keep, arrived
        if s > 0:
            both = (keep + arrived.astype(f32)).astype(bf16)
            back[s] = swap_bit(both, "grp", s)
    return call(
        functools.partial(finish_kernel, order, part),
        shape((rows, out_cols), bf16),
        (*sums[0], *back.values()),
    )


def solution(mesh):
    placed = (
        P(("grp", "tp"), None),
        P(("grp", "tp"), None),
        P(("grp", "tp"), None),
        P(("grp", "loc"), None, None),
        P(("grp", "loc"), None, None),
        P(("grp", "loc"), None, "tp"),
    )
    return jax.shard_map(
        body, mesh=mesh, in_specs=placed, out_specs=P(("grp", "tp"), "loc"), check_vma=False
    )
```

time: 107 us -> 88.9 us (0.83)
  starting transfers between devices: 32.7 us -> 19.4 us
  waiting for transfers between devices: 52.4 us -> 48.4 us
  local copies, waits for them, and re-layouts: 7.8 us -> 6.4 us
    ppermute x6 -> x0, waiting for transfers between devices: 33 us -> none  [shift_by(): lax.ppermute(value, axis, [(i, (i + step) % size) for i in range(size)])]
    ppermute x19 -> x24, waiting for transfers between devices: 19.4 us -> 48.4 us  [swap_bit(): return lax.ppermute(value, axis, [(i, i ^ bit) for i in range(size)])]
    ppermute x6 -> x0, starting transfers between devices: 17.9 us -> none  [shift_by(): lax.ppermute(value, axis, [(i, (i + step) % size) for i in range(size)])]
    ppermute x19 -> x24, starting transfers between devices: 14.8 us -> 19.4 us  [swap_bit(): return lax.ppermute(value, axis, [(i, i ^ bit) for i in range(size)])]
    unnamed x16, local copies, waits for them, and re-layouts: 7.8 us -> 6.4 us
  transfers between devices with their start and end apart: 25 -> 24, of which waited for: 9 -> 11; matrix products, arithmetic and copies ran while one was open for 0% -> 0% of each run, Pallas kernels for 11% -> 15%
where the time goes in v4:
time: 88.9 us; the launch traced here: 88.6 us
  waiting for transfers between devices  48.4 us (54%)
  starting transfers between devices  19.4 us (22%)
  Pallas kernels  14 us (16%)
  local copies, waits for them, and re-layouts  6.4 us (7%)
    ppermute x24, waiting for transfers between devices, swap_bit(): return lax.ppermute(value, axis, [(i, i ^ bit) for i in range(size)])  48.4 us
    ppermute x24, starting transfers between devices, swap_bit(): return lax.ppermute(value, axis, [(i, i ^ bit) for i in range(size)])  19.4 us
    pallas_call x14, Pallas kernels, call(): pl.pallas_call(kernel, out_shape=outs, in_specs=in_specs or [VM] * len(ar...  14 us
    unnamed x16, local copies, waits for them, and re-layouts  6.4 us
  transfers between devices with their start and end apart: 24, of which 11 were waited for; matrix products, arithmetic and copies ran while one was open for 0% of the time, Pallas kernels for 15%

profile of v4, /device:TPU:0, one launch (start us, length us, event | category | flops | bytes accessed | tf_op | source)
XLA Modules:
  0.0 88.6 jit_solution(14195953542302489053)
XLA Ops:
  0.0 2.9 %collective-permute-start.12 = (bf16[768,1024]{1,0:T(8,128)(2,1)}, bf16[768,1024]{1,0:T(8,128)(2,1)S(1)}, u32[]{:S(2)}, u32[]{:S(2)}) collective-permute-start(bf16[768,1024]{1,0:T(8,128)(2,1)} %bitcast.21), channel_id=1, source_target_pairs={{0,1},{1,0},{2,3},{3,2},{4,5},{5,4},{6,7},{7,6},{8,9},{9,8},{10,11... | collective-permute-start | bytes 4718600 | tf_op jit(solution)/shard_map/ppermute | solution.py:18
  2.9 1.2 %copy-done.5 = bf16[256,2048]{1,0:T(8,128)(2,1)S(1)} copy-done((bf16[256,2048]{1,0:T(8,128)(2,1)S(1)}, bf16[256,2048]{1,0:T(8,128)(2,1)}, u32[]{:S(2)}) %copy-start.5) | copy-done | bytes 1048600
  4.2 0.7 copy-done.6
  4.9 0.7 copy-done.7
  5.8 1.6 %collective-permute-start.4 = (bf16[64,2176]{1,0:T(8,128)(2,1)S(1)}, bf16[64,2176]{1,0:T(8,128)(2,1)S(1)}, u32[]{:S(2)}, u32[]{:S(2)}) collective-permute-start(bf16[64,2176]{1,0:T(8,128)(2,1)S(1)} %get-tuple-element.44), channel_id=1, source_target_pairs={{0,8},{8,0},{16,24},{24,16},{1,9},{9,1},{17,25},{25,17},{2,10},{10... | collective-permute-start | bytes 835592 | tf_op jit(solution)/shard_map/ppermute | solution.py:18
  7.4 2.5 %collective-permute-start.8 = (bf16[64,2176]{1,0:T(8,128)(2,1)S(1)}, bf16[64,2176]{1,0:T(8,128)(2,1)S(1)}, u32[]{:S(2)}, u32[]{:S(2)}) collective-permute-start(bf16[64,2176]{1,0:T(8,128)(2,1)S(1)} %get-tuple-element.44), channel_id=1, source_target_pairs={{0,24},{8,16},{16,8},{24,0},{1,25},{9,17},{17,9},{25,1},{2,26},{10... | collective-permute-start | bytes 835592 | tf_op jit(solution)/shard_map/ppermute | solution.py:18
  9.9 1.9 %copy-done.1 = bf16[1,2048,768]{2,1,0:T(8,128)(2,1)S(1)} copy-done((bf16[1,2048,768]{2,1,0:T(8,128)(2,1)S(1)}, bf16[1,2048,768]{2,1,0:T(8,128)(2,1)}, u32[]{:S(2)}) %copy-start.1) | copy-done | bytes 3145752
  11.8 1.9 %copy-done.3 = bf16[1,2048,768]{2,1,0:T(8,128)(2,1)S(1)} copy-done((bf16[1,2048,768]{2,1,0:T(8,128)(2,1)S(1)}, bf16[1,2048,768]{2,1,0:T(8,128)(2,1)}, u32[]{:S(2)}) %copy-start.3) | copy-done | bytes 3145752
  13.7 2.0 %shard_map.65 = (bf16[256,768]{1,0:T(8,128)(2,1)S(1)}, f32[256,128]{1,0:T(8,128)S(1)}) custom-call(bf16[256,2048]{1,0:T(8,128)(2,1)S(1)} %copy-done.5, bf16[256,128]{1,0:T(8,128)(2,1)S(1)} %get-tuple-element.41.refs_1_, bf16[2048,768]{1,0:T(8,128)(2,1)S(1)} %bitcast.30, bf16[2048,768]{1,0:T(8,128)(2,1)S(1)} %bitcast.34), custom_call_target="tpu_custom_call" | custom-call | tf_op jit(solution)/shard_map/pallas_call | solution.py:39
  15.7 1.6 %collective-permute-start.5 = (bf16[64,2176]{1,0:T(8,128)(2,1)S(1)}, bf16[64,2176]{1,0:T(8,128)(2,1)S(1)}, u32[]{:S(2)}, u32[]{:S(2)}) collective-permute-start(bf16[64,2176]{1,0:T(8,128)(2,1)S(1)} %collective-permute-done.4.refs_0_), channel_id=1, source_target_pairs={{0,4},{2,6},{4,0},{6,2},{1,5},{3,7},{5,1},{7,3},{8,12},{10,14},{12... | collective-permute-start | bytes 835592 | tf_op jit(solution)/shard_map/ppermute | solution.py:18
  17.3 4.7 %collective-permute-done.8.refs_0_ = bf16[64,2176]{1,0:T(8,128)(2,1)S(1)} collective-permute-done((bf16[64,2176]{1,0:T(8,128)(2,1)S(1)}, bf16[64,2176]{1,0:T(8,128)(2,1)S(1)}, u32[]{:S(2)}, u32[]{:S(2)}) %collective-permute-start.8) | collective-permute-done | bytes 278560 | tf_op jit(solution)/shard_map/ppermute | solution.py:18
  22.1 1.3 %collective-permute-done.5.refs_1_ = bf16[64,2176]{1,0:T(8,128)(2,1)S(1)} collective-permute-done((bf16[64,2176]{1,0:T(8,128)(2,1)S(1)}, bf16[64,2176]{1,0:T(8,128)(2,1)S(1)}, u32[]{:S(2)}, u32[]{:S(2)}) %collective-permute-start.5) | collective-permute-done | bytes 278560 | tf_op jit(solution)/shard_map/ppermute | solution.py:18
  23.4 1.5 %collective-permute-start.9 = (bf16[64,2176]{1,0:T(8,128)(2,1)S(1)}, bf16[64,2176]{1,0:T(8,128)(2,1)S(1)}, u32[]{:S(2)}, u32[]{:S(2)}) collective-permute-start(bf16[64,2176]{1,0:T(8,128)(2,1)S(1)} %collective-permute-done.8.refs_0_), channel_id=1, source_target_pairs={{0,4},{2,6},{4,0},{6,2},{1,5},{3,7},{5,1},{7,3},{8,12},{10,14},{12... | collective-permute-start | bytes 835592 | tf_op jit(solution)/shard_map/ppermute | solution.py:18
  24.9 1.2 %collective-permute-start = (bf16[64,2176]{1,0:T(8,128)(2,1)S(1)}, bf16[64,2176]{1,0:T(8,128)(2,1)S(1)}, u32[]{:S(2)}, u32[]{:S(2)}) collective-permute-start(bf16[64,2176]{1,0:T(8,128)(2,1)S(1)} %get-tuple-element.44), channel_id=1, source_target_pairs={{0,16},{8,24},{16,0},{24,8},{1,17},{9,25},{17,1},{25,9},{2,18},{10... | collective-permute-start | bytes 835592 | tf_op jit(solution)/shard_map/ppermute | solution.py:18
  26.1 1.9 %shard_map.67 = (bf16[256,768]{1,0:T(8,128)(2,1)S(1)}, f32[256,128]{1,0:T(8,128)S(1)}) custom-call(bf16[64,2176]{1,0:T(8,128)(2,1)S(1)} %collective-permute-done.4.refs_0_, bf16[64,2176]{1,0:T(8,128)(2,1)S(1)} %collective-permute-done.5.refs_1_, bf16[64,2176]{1,0:T(8,128)(2,1)S(1)} %collective-permute-done.6.refs_2_, ...), custom_call_target="tpu_custom_call" | custom-call | tf_op jit(solution)/shard_map/pallas_call | solution.py:39
  28.0 4.5 %collective-permute-done.9.refs_1_ = bf16[64,2176]{1,0:T(8,128)(2,1)S(1)} collective-permute-done((bf16[64,2176]{1,0:T(8,128)(2,1)S(1)}, bf16[64,2176]{1,0:T(8,128)(2,1)S(1)}, u32[]{:S(2)}, u32[]{:S(2)}) %collective-permute-start.9) | collective-permute-done | bytes 278560 | tf_op jit(solution)/shard_map/ppermute | solution.py:18
  32.4 8.1 %collective-permute-done.refs_0_ = bf16[64,2176]{1,0:T(8,128)(2,1)S(1)} collective-permute-done((bf16[64,2176]{1,0:T(8,128)(2,1)S(1)}, bf16[64,2176]{1,0:T(8,128)(2,1)S(1)}, u32[]{:S(2)}, u32[]{:S(2)}) %collective-permute-start) | collective-permute-done | bytes 278560 | tf_op jit(solution)/shard_map/ppermute | solution.py:18
  41.1 1.9 %shard_map.68 = (bf16[256,768]{1,0:T(8,128)(2,1)S(1)}, f32[256,128]{1,0:T(8,128)S(1)}) custom-call(bf16[64,2176]{1,0:T(8,128)(2,1)S(1)} %collective-permute-done.8.refs_0_, bf16[64,2176]{1,0:T(8,128)(2,1)S(1)} %collective-permute-done.9.refs_1_, bf16[64,2176]{1,0:T(8,128)(2,1)S(1)} %collective-permute-done.10.refs_2_, ...), custom_call_target="tpu_custom_call" | custom-call | tf_op jit(solution)/shard_map/pallas_call | solution.py:39
  44.2 4.4 %collective-permute-done.1.refs_1_ = bf16[64,2176]{1,0:T(8,128)(2,1)S(1)} collective-permute-done((bf16[64,2176]{1,0:T(8,128)(2,1)S(1)}, bf16[64,2176]{1,0:T(8,128)(2,1)S(1)}, u32[]{:S(2)}, u32[]{:S(2)}) %collective-permute-start.1) | collective-permute-done | bytes 278560 | tf_op jit(solution)/shard_map/ppermute | solution.py:18
  50.1 1.9 %shard_map.66 = (bf16[256,768]{1,0:T(8,128)(2,1)S(1)}, f32[256,128]{1,0:T(8,128)S(1)}) custom-call(bf16[64,2176]{1,0:T(8,128)(2,1)S(1)} %collective-permute-done.refs_0_, bf16[64,2176]{1,0:T(8,128)(2,1)S(1)} %collective-permute-done.1.refs_1_, bf16[64,2176]{1,0:T(8,128)(2,1)S(1)} %collective-permute-done.2.refs_2_, ...), custom_call_target="tpu_custom_call" | custom-call | tf_op jit(solution)/shard_map/pallas_call | solution.py:39
  51.9 0.7 shard_map.70
  54.0 0.7 shard_map.72
  54.7 1.6 %collective-permute-start.17 = (bf16[1,256,512]{2,1,0:T(8,128)(2,1)S(1)}, bf16[1,256,512]{2,1,0:T(8,128)(2,1)S(1)}, u32[]{:S(2)}, u32[]{:S(2)}) collective-permute-start(bf16[1,256,512]{2,1,0:T(8,128)(2,1)S(1)} %get-tuple-element.62), channel_id=1, source_target_pairs={{0,4},{2,6},{4,0},{6,2},{1,5},{3,7},{5,1},{7,3},{8,12},{10,14},{12... | collective-permute-start | bytes 786440 | tf_op jit(solution)/shard_map/ppermute | solution.py:18
  57.0 0.7 shard_map.74
  58.3 4.3 %collective-permute-done.19 = bf16[1,256,512]{2,1,0:T(8,128)(2,1)S(1)} collective-permute-done((bf16[1,256,512]{2,1,0:T(8,128)(2,1)S(1)}, bf16[1,256,512]{2,1,0:T(8,128)(2,1)S(1)}, u32[]{:S(2)}, u32[]{:S(2)}) %collective-permute-start.19) | collective-permute-done | bytes 262176 | tf_op jit(solution)/shard_map/ppermute | solution.py:18
  62.7 2.8 %collective-permute-start.20 = (bf16[256,512]{1,0:T(8,128)(2,1)S(1)}, bf16[256,512]{1,0:T(8,128)(2,1)S(1)}, u32[]{:S(2)}, u32[]{:S(2)}) collective-permute-start(bf16[256,512]{1,0:T(8,128)(2,1)S(1)} %fusion.1), channel_id=1, source_target_pairs={{0,24},{8,16},{16,8},{24,0},{1,25},{9,17},{17,9},{25,1},{2,26},{10... | collective-permute-start | bytes 786440 | tf_op jit(solution)/shard_map/ppermute | solution.py:18
  65.5 2.8 %collective-permute-done.17 = bf16[1,256,512]{2,1,0:T(8,128)(2,1)S(1)} collective-permute-done((bf16[1,256,512]{2,1,0:T(8,128)(2,1)S(1)}, bf16[1,256,512]{2,1,0:T(8,128)(2,1)S(1)}, u32[]{:S(2)}, u32[]{:S(2)}) %collective-permute-start.17) | collective-permute-done | bytes 262176 | tf_op jit(solution)/shard_map/ppermute | solution.py:18
  68.4 4.9 %collective-permute-done.22 = bf16[1,256,512]{2,1,0:T(8,128)(2,1)S(1)} collective-permute-done((bf16[1,256,512]{2,1,0:T(8,128)(2,1)S(1)}, bf16[1,256,512]{2,1,0:T(8,128)(2,1)S(1)}, u32[]{:S(2)}, u32[]{:S(2)}) %collective-permute-start.22) | collective-permute-done | bytes 262176 | tf_op jit(solution)/shard_map/ppermute | solution.py:18
  73.5 0.7 shard_map.76
  74.8 3.8 %collective-permute-done.21.refs_1_ = bf16[256,512]{1,0:T(8,128)(2,1)S(1)} collective-permute-done((bf16[256,512]{1,0:T(8,128)(2,1)S(1)}, bf16[256,512]{1,0:T(8,128)(2,1)S(1)}, u32[]{:S(2)}, u32[]{:S(2)}) %collective-permute-start.21) | collective-permute-done | bytes 262176 | tf_op jit(solution)/shard_map/ppermute | solution.py:18
  78.5 9.2 %collective-permute-done.23.refs_2_ = bf16[256,512]{1,0:T(8,128)(2,1)S(1)} collective-permute-done((bf16[256,512]{1,0:T(8,128)(2,1)S(1)}, bf16[256,512]{1,0:T(8,128)(2,1)S(1)}, u32[]{:S(2)}, u32[]{:S(2)}) %collective-permute-start.23) | collective-permute-done | bytes 262176 | tf_op jit(solution)/shard_map/ppermute | solution.py:18
  87.8 0.9 shard_map.77
  (49 shorter events, 7.0 us)
Async XLA Ops:
  0.0 42.9 %collective-permute-start.12 = (bf16[768,1024]{1,0:T(8,128)(2,1)}, bf16[768,1024]{1,0:T(8,128)(2,1)S(1)}, u32[]{:S(2)}, u32[]{:S(2)}) collective-permute-start(bf16[768,1024]{1,0:T(8,128)(2,1)} %bitcast.21), channel_id=1, source_target_pairs={{0,1},{1,0},{2,3},{3,2},{4,5},{5,4},{6,7},{7,6},{8,9},{9,8},{10,11... | collective-permute-start | bytes 4718600 | tf_op jit(solution)/shard_map/ppermute | solution.py:18
  2.9 1.2 %copy-start.5 = (bf16[256,2048]{1,0:T(8,128)(2,1)S(1)}, bf16[256,2048]{1,0:T(8,128)(2,1)}, u32[]{:S(2)}) copy-start(bf16[256,2048]{1,0:T(8,128)(2,1)} %refs_0_.1) | copy-start | bytes 3145732
  4.2 0.7 copy-start.6
  4.9 0.7 copy-start.7
  5.8 10.0 %collective-permute-start.4 = (bf16[64,2176]{1,0:T(8,128)(2,1)S(1)}, bf16[64,2176]{1,0:T(8,128)(2,1)S(1)}, u32[]{:S(2)}, u32[]{:S(2)}) collective-permute-start(bf16[64,2176]{1,0:T(8,128)(2,1)S(1)} %get-tuple-element.44), channel_id=1, source_target_pairs={{0,8},{8,0},{16,24},{24,16},{1,9},{9,1},{17,25},{25,17},{2,10},{10... | collective-permute-start | bytes 835592 | tf_op jit(solution)/shard_map/ppermute | solution.py:18
  7.4 14.7 %collective-permute-start.8 = (bf16[64,2176]{1,0:T(8,128)(2,1)S(1)}, bf16[64,2176]{1,0:T(8,128)(2,1)S(1)}, u32[]{:S(2)}, u32[]{:S(2)}) collective-permute-start(bf16[64,2176]{1,0:T(8,128)(2,1)S(1)} %get-tuple-element.44), channel_id=1, source_target_pairs={{0,24},{8,16},{16,8},{24,0},{1,25},{9,17},{17,9},{25,1},{2,26},{10... | collective-permute-start | bytes 835592 | tf_op jit(solution)/shard_map/ppermute | solution.py:18
  9.9 1.9 %copy-start.1 = (bf16[1,2048,768]{2,1,0:T(8,128)(2,1)S(1)}, bf16[1,2048,768]{2,1,0:T(8,128)(2,1)}, u32[]{:S(2)}) copy-start(bf16[1,2048,768]{2,1,0:T(8,128)(2,1)} %param.9) | copy-start | bytes 9437188
  11.8 1.9 %copy-start.3 = (bf16[1,2048,768]{2,1,0:T(8,128)(2,1)S(1)}, bf16[1,2048,768]{2,1,0:T(8,128)(2,1)}, u32[]{:S(2)}) copy-start(bf16[1,2048,768]{2,1,0:T(8,128)(2,1)} %param.10) | copy-start | bytes 9437188
  13.7 12.4 %copy-start.2 = (bf16[1,2048,768]{2,1,0:T(8,128)(2,1)S(1)}, bf16[1,2048,768]{2,1,0:T(8,128)(2,1)}, u32[]{:S(2)}) copy-start(bf16[1,2048,768]{2,1,0:T(8,128)(2,1)} %param.9) | copy-start | bytes 9437188
  13.7 12.4 %copy-start.4 = (bf16[1,2048,768]{2,1,0:T(8,128)(2,1)S(1)}, bf16[1,2048,768]{2,1,0:T(8,128)(2,1)}, u32[]{:S(2)}) copy-start(bf16[1,2048,768]{2,1,0:T(8,128)(2,1)} %param.10) | copy-start | bytes 9437188
  15.7 7.6 %collective-permute-start.5 = (bf16[64,2176]{1,0:T(8,128)(2,1)S(1)}, bf16[64,2176]{1,0:T(8,128)(2,1)S(1)}, u32[]{:S(2)}, u32[]{:S(2)}) collective-permute-start(bf16[64,2176]{1,0:T(8,128)(2,1)S(1)} %collective-permute-done.4.refs_0_), channel_id=1, source_target_pairs={{0,4},{2,6},{4,0},{6,2},{1,5},{3,7},{5,1},{7,3},{8,12},{10,14},{12... | collective-permute-start | bytes 835592 | tf_op jit(solution)/shard_map/ppermute | solution.py:18
  17.3 8.8 %collective-permute-start.6 = (bf16[64,2176]{1,0:T(8,128)(2,1)S(1)}, bf16[64,2176]{1,0:T(8,128)(2,1)S(1)}, u32[]{:S(2)}, u32[]{:S(2)}) collective-permute-start(bf16[64,2176]{1,0:T(8,128)(2,1)S(1)} %collective-permute-done.4.refs_0_), channel_id=1, source_target_pairs={{0,2},{2,0},{4,6},{6,4},{1,3},{3,1},{5,7},{7,5},{8,10},{10,8},{12,... | collective-permute-start | bytes 835592 | tf_op jit(solution)/shard_map/ppermute | solution.py:18
  23.4 2.7 %collective-permute-start.7 = (bf16[64,2176]{1,0:T(8,128)(2,1)S(1)}, bf16[64,2176]{1,0:T(8,128)(2,1)S(1)}, u32[]{:S(2)}, u32[]{:S(2)}) collective-permute-start(bf16[64,2176]{1,0:T(8,128)(2,1)S(1)} %collective-permute-done.5.refs_1_), channel_id=1, source_target_pairs={{0,2},{2,0},{4,6},{6,4},{1,3},{3,1},{5,7},{7,5},{8,10},{10,8},{12,... | collective-permute-start | bytes 835592 | tf_op jit(solution)/shard_map/ppermute | solution.py:18
  23.4 9.1 %collective-permute-start.9 = (bf16[64,2176]{1,0:T(8,128)(2,1)S(1)}, bf16[64,2176]{1,0:T(8,128)(2,1)S(1)}, u32[]{:S(2)}, u32[]{:S(2)}) collective-permute-start(bf16[64,2176]{1,0:T(8,128)(2,1)S(1)} %collective-permute-done.8.refs_0_), channel_id=1, source_target_pairs={{0,4},{2,6},{4,0},{6,2},{1,5},{3,7},{5,1},{7,3},{8,12},{10,14},{12... | collective-permute-start | bytes 835592 | tf_op jit(solution)/shard_map/ppermute | solution.py:18
  24.9 15.7 %collective-permute-start = (bf16[64,2176]{1,0:T(8,128)(2,1)S(1)}, bf16[64,2176]{1,0:T(8,128)(2,1)S(1)}, u32[]{:S(2)}, u32[]{:S(2)}) collective-permute-start(bf16[64,2176]{1,0:T(8,128)(2,1)S(1)} %get-tuple-element.44), channel_id=1, source_target_pairs={{0,16},{8,24},{16,0},{24,8},{1,17},{9,25},{17,1},{25,9},{2,18},{10... | collective-permute-start | bytes 835592 | tf_op jit(solution)/shard_map/ppermute | solution.py:18
  26.1 15.0 %collective-permute-start.10 = (bf16[64,2176]{1,0:T(8,128)(2,1)S(1)}, bf16[64,2176]{1,0:T(8,128)(2,1)S(1)}, u32[]{:S(2)}, u32[]{:S(2)}) collective-permute-start(bf16[64,2176]{1,0:T(8,128)(2,1)S(1)} %collective-permute-done.8.refs_0_), channel_id=1, source_target_pairs={{0,2},{2,0},{4,6},{6,4},{1,3},{3,1},{5,7},{7,5},{8,10},{10,8},{12,... | collective-permute-start | bytes 835592 | tf_op jit(solution)/shard_map/ppermute | solution.py:18
  32.4 10.5 %copy-start = (bf16[1,768,1024]{2,1,0:T(8,128)(2,1)S(1)}, bf16[1,768,1024]{2,1,0:T(8,128)(2,1)}, u32[]{:S(2)}) copy-start(bf16[1,768,1024]{2,1,0:T(8,128)(2,1)} %param.11) | copy-start | bytes 4718596
  32.4 8.6 %collective-permute-start.11 = (bf16[64,2176]{1,0:T(8,128)(2,1)S(1)}, bf16[64,2176]{1,0:T(8,128)(2,1)S(1)}, u32[]{:S(2)}, u32[]{:S(2)}) collective-permute-start(bf16[64,2176]{1,0:T(8,128)(2,1)S(1)} %collective-permute-done.9.refs_1_), channel_id=1, source_target_pairs={{0,2},{2,0},{4,6},{6,4},{1,3},{3,1},{5,7},{7,5},{8,10},{10,8},{12,... | collective-permute-start | bytes 835592 | tf_op jit(solution)/shard_map/ppermute | solution.py:18
  40.5 8.0 %collective-permute-start.1 = (bf16[64,2176]{1,0:T(8,128)(2,1)S(1)}, bf16[64,2176]{1,0:T(8,128)(2,1)S(1)}, u32[]{:S(2)}, u32[]{:S(2)}) collective-permute-start(bf16[64,2176]{1,0:T(8,128)(2,1)S(1)} %collective-permute-done.refs_0_), channel_id=1, source_target_pairs={{0,4},{2,6},{4,0},{6,2},{1,5},{3,7},{5,1},{7,3},{8,12},{10,14},{12... | collective-permute-start | bytes 835592 | tf_op jit(solution)/shard_map/ppermute | solution.py:18
  43.6 4.9 %collective-permute-start.13 = (bf16[2,256,512]{2,1,0:T(8,128)(2,1)S(1)}, bf16[2,256,512]{2,1,0:T(8,128)(2,1)S(1)}, u32[]{:S(2)}, u32[]{:S(2)}) collective-permute-start(bf16[2,256,512]{2,1,0:T(8,128)(2,1)S(1)} %shard_map.69), channel_id=1, source_target_pairs={{0,2},{2,0},{4,6},{6,4},{1,3},{3,1},{5,7},{7,5},{8,10},{10,8},{12,... | collective-permute-start | bytes 1572872 | tf_op jit(solution)/shard_map/ppermute | solution.py:18
  43.7 6.0 %collective-permute-start.2 = (bf16[64,2176]{1,0:T(8,128)(2,1)S(1)}, bf16[64,2176]{1,0:T(8,128)(2,1)S(1)}, u32[]{:S(2)}, u32[]{:S(2)}) collective-permute-start(bf16[64,2176]{1,0:T(8,128)(2,1)S(1)} %collective-permute-done.refs_0_), channel_id=1, source_target_pairs={{0,2},{2,0},{4,6},{6,4},{1,3},{3,1},{5,7},{7,5},{8,10},{10,8},{12,... | collective-permute-start | bytes 835592 | tf_op jit(solution)/shard_map/ppermute | solution.py:18
  48.5 1.6 %collective-permute-start.3 = (bf16[64,2176]{1,0:T(8,128)(2,1)S(1)}, bf16[64,2176]{1,0:T(8,128)(2,1)S(1)}, u32[]{:S(2)}, u32[]{:S(2)}) collective-permute-start(bf16[64,2176]{1,0:T(8,128)(2,1)S(1)} %collective-permute-done.1.refs_1_), channel_id=1, source_target_pairs={{0,2},{2,0},{4,6},{6,4},{1,3},{3,1},{5,7},{7,5},{8,10},{10,8},{12,... | collective-permute-start | bytes 835592 | tf_op jit(solution)/shard_map/ppermute | solution.py:18
  49.1 4.9 %collective-permute-start.14 = (bf16[2,256,512]{2,1,0:T(8,128)(2,1)S(1)}, bf16[2,256,512]{2,1,0:T(8,128)(2,1)S(1)}, u32[]{:S(2)}, u32[]{:S(2)}) collective-permute-start(bf16[2,256,512]{2,1,0:T(8,128)(2,1)S(1)} %shard_map.71), channel_id=1, source_target_pairs={{0,2},{2,0},{4,6},{6,4},{1,3},{3,1},{5,7},{7,5},{8,10},{10,8},{12,... | collective-permute-start | bytes 1572872 | tf_op jit(solution)/shard_map/ppermute | solution.py:18
  53.3 3.7 %collective-permute-start.15 = (bf16[2,256,512]{2,1,0:T(8,128)(2,1)S(1)}, bf16[2,256,512]{2,1,0:T(8,128)(2,1)S(1)}, u32[]{:S(2)}, u32[]{:S(2)}) collective-permute-start(bf16[2,256,512]{2,1,0:T(8,128)(2,1)S(1)} %shard_map.73), channel_id=1, source_target_pairs={{0,2},{2,0},{4,6},{6,4},{1,3},{3,1},{5,7},{7,5},{8,10},{10,8},{12,... | collective-permute-start | bytes 1572872 | tf_op jit(solution)/shard_map/ppermute | solution.py:18
  53.5 9.1 %collective-permute-start.19 = (bf16[1,256,512]{2,1,0:T(8,128)(2,1)S(1)}, bf16[1,256,512]{2,1,0:T(8,128)(2,1)S(1)}, u32[]{:S(2)}, u32[]{:S(2)}) collective-permute-start(bf16[1,256,512]{2,1,0:T(8,128)(2,1)S(1)} %get-tuple-element.56), channel_id=1, source_target_pairs={{0,4},{2,6},{4,0},{6,2},{1,5},{3,7},{5,1},{7,3},{8,12},{10,14},{12... | collective-permute-start | bytes 786440 | tf_op jit(solution)/shard_map/ppermute | solution.py:18
  54.7 13.5 %collective-permute-start.17 = (bf16[1,256,512]{2,1,0:T(8,128)(2,1)S(1)}, bf16[1,256,512]{2,1,0:T(8,128)(2,1)S(1)}, u32[]{:S(2)}, u32[]{:S(2)}) collective-permute-start(bf16[1,256,512]{2,1,0:T(8,128)(2,1)S(1)} %get-tuple-element.62), channel_id=1, source_target_pairs={{0,4},{2,6},{4,0},{6,2},{1,5},{3,7},{5,1},{7,3},{8,12},{10,14},{12... | collective-permute-start | bytes 786440 | tf_op jit(solution)/shard_map/ppermute | solution.py:18
  56.9 16.6 %collective-permute-start.16 = (bf16[2,256,512]{2,1,0:T(8,128)(2,1)S(1)}, bf16[2,256,512]{2,1,0:T(8,128)(2,1)S(1)}, u32[]{:S(2)}, u32[]{:S(2)}) collective-permute-start(bf16[2,256,512]{2,1,0:T(8,128)(2,1)S(1)} %shard_map.75), channel_id=1, source_target_pairs={{0,2},{2,0},{4,6},{6,4},{1,3},{3,1},{5,7},{7,5},{8,10},{10,8},{12,... | collective-permute-start | bytes 1572872 | tf_op jit(solution)/shard_map/ppermute | solution.py:18
  57.7 15.6 %collective-permute-start.22 = (bf16[1,256,512]{2,1,0:T(8,128)(2,1)S(1)}, bf16[1,256,512]{2,1,0:T(8,128)(2,1)S(1)}, u32[]{:S(2)}, u32[]{:S(2)}) collective-permute-start(bf16[1,256,512]{2,1,0:T(8,128)(2,1)S(1)} %get-tuple-element.76), channel_id=1, source_target_pairs={{0,4},{2,6},{4,0},{6,2},{1,5},{3,7},{5,1},{7,3},{8,12},{10,14},{12... | collective-permute-start | bytes 786440 | tf_op jit(solution)/shard_map/ppermute | solution.py:18
  62.7 12.1 %collective-permute-start.20 = (bf16[256,512]{1,0:T(8,128)(2,1)S(1)}, bf16[256,512]{1,0:T(8,128)(2,1)S(1)}, u32[]{:S(2)}, u32[]{:S(2)}) collective-permute-start(bf16[256,512]{1,0:T(8,128)(2,1)S(1)} %fusion.1), channel_id=1, source_target_pairs={{0,24},{8,16},{16,8},{24,0},{1,25},{9,17},{17,9},{25,1},{2,26},{10... | collective-permute-start | bytes 786440 | tf_op jit(solution)/shard_map/ppermute | solution.py:18
  68.3 10.2 %collective-permute-start.21 = (bf16[256,512]{1,0:T(8,128)(2,1)S(1)}, bf16[256,512]{1,0:T(8,128)(2,1)S(1)}, u32[]{:S(2)}, u32[]{:S(2)}) collective-permute-start(bf16[256,512]{1,0:T(8,128)(2,1)S(1)} %fusion), channel_id=1, source_target_pairs={{0,8},{8,0},{16,24},{24,16},{1,9},{9,1},{17,25},{25,17},{2,10},{10... | collective-permute-start | bytes 786440 | tf_op jit(solution)/shard_map/ppermute | solution.py:18
  73.4 14.4 %collective-permute-start.23 = (bf16[256,512]{1,0:T(8,128)(2,1)S(1)}, bf16[256,512]{1,0:T(8,128)(2,1)S(1)}, u32[]{:S(2)}, u32[]{:S(2)}) collective-permute-start(bf16[256,512]{1,0:T(8,128)(2,1)S(1)} %fusion.2), channel_id=1, source_target_pairs={{0,16},{8,24},{16,0},{24,8},{1,17},{9,25},{17,1},{25,9},{2,18},{10... | collective-permute-start | bytes 786440 | tf_op jit(solution)/shard_map/ppermute | solution.py:18
  74.2 13.6 %collective-permute-start.18 = (bf16[1,256,512]{2,1,0:T(8,128)(2,1)S(1)}, bf16[1,256,512]{2,1,0:T(8,128)(2,1)S(1)}, u32[]{:S(2)}, u32[]{:S(2)}) collective-permute-start(bf16[1,256,512]{2,1,0:T(8,128)(2,1)S(1)} %get-tuple-element.75), channel_id=1, source_target_pairs={{0,4},{2,6},{4,0},{6,2},{1,5},{3,7},{5,1},{7,3},{8,12},{10,14},{12... | collective-permute-start | bytes 786440 | tf_op jit(solution)/shard_map/ppermute | solution.py:18

commit v5 on v4

--- a/solution.py
+++ b/solution.py
@@ -42,6 +42,7 @@
         in_specs=in_specs or [VM] * len(arrays),
         out_specs=out_specs or jax.tree.map(lambda _: VM, outs),
         scratch_shapes=list(scratch),
+        cost_estimate=cost if flops else None,
         compiler_params=pltpu.CompilerParams(vmem_limit_bytes=12 << 20),
     )(*arrays)
 
@@ -54,37 +55,36 @@
     return lax.axis_index("grp") * lax.axis_size("loc") + lax.axis_index("loc")
 
 
-def prepare_kernel(part, tokens, ids, weights, message, table, ids_here, weights_here, sems):
+def prepare_kernel(part, tokens, routes, message, table, routes_here, sems):
     width = tokens.shape[1]
     local = lax.axis_index("loc")
     copies = [
-        pltpu.make_async_copy(ids, ids_here, sems.at[0]),
-        pltpu.make_async_copy(weights, weights_here, sems.at[1]),
-        pltpu.make_async_copy(tokens.at[rows_at(local, part), :], message.at[:, :width], sems.at[2]),
+        pltpu.make_async_copy(routes, routes_here, sems.at[0]),
+        pltpu.make_async_copy(tokens.at[rows_at(local, part), :], message.at[:, :width], sems.at[1]),
     ]
     for copy in copies:
         copy.start()
     lanes, rows = table.shape[1], table.shape[0]
-    expert = lax.broadcasted_iota(jnp.int32, (lanes, rows), 0)
+    expert = lax.broadcasted_iota(jnp.int32, (lanes, rows), 0).astype(jnp.float32)
     dense = jnp.zeros((lanes, rows), jnp.float32)
     copies[0].wait()
-    copies[1].wait()
-    for k in range(ids.shape[0]):
-        weight = weights_here[k : k + 1, :].astype(jnp.float32)
-        dense = jnp.where(expert == ids_here[k : k + 1, :], weight, dense)
+    choices = routes.shape[0] // 2
+    for k in range(choices):
+        weight = routes_here[choices + k : choices + k + 1, :]
+        dense = jnp.where(expert == routes_here[k : k + 1, :], weight, dense)
     table[...] = dense.T.astype(jnp.bfloat16)
     message[:, width:] = table[rows_at(local, part), :]
-    copies[2].wait()
-
-
-def hidden_kernel(order, part, *refs):
+    copies[1].wait()
+
+
+def hidden_kernel(order, part, own, *refs):
     *pieces, gate, up, hidden, scale, block, routes, sems = refs
     width = gate.shape[0]
     local = lax.axis_index("loc")
     copies = []
     for n, k in enumerate(order):
         at = slice(n * part, (n + 1) * part)
-        if len(pieces) == 2:
+        if own:
             whole = pieces[0].at[rows_at(local ^ k, part), :]
             copies.append(pltpu.make_async_copy(whole, block.at[at, :], sems.at[n]))
             copies[n].start()
@@ -127,13 +127,12 @@
 
 
 def stay_kernel(order, part, bit, with_sum, hidden, scale, *refs):
-    if with_sum:
-        arrived, *refs = refs
+    arrived, refs = refs[:with_sum], refs[with_sum:]
     *shards, keep, message, total = refs
     half = len(shards) // 2
     for place, cols, value in column_results(hidden, scale, shards, total.shape[2], 0):
         if with_sum:
-            value = value + arrived[place, :, cols].astype(jnp.float32)
+            value = value + jnp.concatenate([a[place, :, cols] for a in arrived], axis=0).astype(jnp.float32)
         total[place, :, cols] = value
     for i in range(half):
         keep[i] = total[i]
@@ -170,28 +169,25 @@
     shape = jax.ShapeDtypeStruct
     bf16, f32 = jnp.bfloat16, jnp.float32
 
+    routes = jnp.concatenate([expert_ids.T.astype(f32), router_weights.T.astype(f32)], axis=0)
     message, table = call(
         functools.partial(prepare_kernel, part),
         (shape((part, width + lanes), bf16), shape((rows, lanes), bf16)),
-        (tokens, expert_ids.T, router_weights.T),
-        in_specs=[HBM] * 3,
-        scratch=[
-            pltpu.VMEM(expert_ids.shape[::-1], jnp.int32),
-            pltpu.VMEM(router_weights.shape[::-1], bf16),
-            pltpu.SemaphoreType.DMA((3,)),
-        ],
+        (tokens, routes),
+        in_specs=[HBM] * 2,
+        scratch=[pltpu.VMEM(routes.shape, f32), pltpu.SemaphoreType.DMA((2,))],
     )
 
     down = [w_down[0]]
     for bit in bits_of(tp_size):
         down = down + [swap_bit(value, "tp", bit) for value in down]
 
-    def ffn(pieces):
+    def ffn(pieces, own=False):
         return call(
-            functools.partial(hidden_kernel, order, part),
+            functools.partial(hidden_kernel, order, part, own),
             (shape((rows, hidden_width), bf16), shape((rows, LANES), f32)),
             (*pieces, w_gate[0], w_up[0]),
-            in_specs=[HBM] + [VM] * 3 if len(pieces) == 2 else None,
+            in_specs=[HBM] + [VM] * 3 if own else None,
             scratch=[
                 pltpu.VMEM((rows, width), bf16),
                 pltpu.VMEM((rows, lanes), f32),
@@ -214,7 +210,7 @@
     def stay(hidden, scale, arrived):
         half = tp_size // 2
         return call(
-            functools.partial(stay_kernel, order, part, half * per_shard, len(arrived) > 0),
+            functools.partial(stay_kernel, order, part, half * per_shard, len(arrived)),
             (shape((half, rows, out_cols), f32), shape((half, rows, out_cols), bf16)),
             (hidden, scale, *arrived, *down),
             scratch=[pltpu.VMEM((tp_size, rows, out_cols), f32)],
@@ -233,47 +229,46 @@
             message = jnp.stack([message[:, m] for m in there], axis=1)
             arrived = swap_bit(message.reshape(half, rows, out_cols), "loc", bit)
             keep = keep[:half]
-        return keep[0], arrived[0]
-
-    sent, hidden = {}, {0: ffn([tokens, table])}
+        return keep[0], arrived
+
+    sent = {s: swap_bit(message, "grp", s) for s in partners}
+    turns = partners[1:] + partners[:1] + [0]
+    first, late = turns[0], partners[-1]
+    hidden, left, stayed, sums, back = {}, {}, {}, {}, {}
+
+    def first_half(s):
+        if s not in left:
+            left[s] = [leave(*hidden[s])] if per_shard == 2 else []
+
+    hidden[0] = ffn([tokens, table], own=True)
     for s in partners:
-        sent[s] = swap_bit(message, "grp", s)
-    for n, s in enumerate(partners):
         pieces = [after(sent[s], hidden[0])]
         for bit in reversed(bits_of(group_size)):
-            if n > 0 and bit == 1:
-                pieces[1:] = [after(value, hidden[partners[n - 1]]) for value in pieces[1:]]
+            if bit == 1 and s == late:
+                ready = [hidden[other] for other in partners[:-1]]
+                pieces[1:] = [after(value, ready) for value in pieces[1:]]
             pieces = pieces + [swap_bit(value, "loc", bit) for value in pieces]
+        if s == late:
+            first_half(first)
+            pieces = after(pieces, left[first])
         hidden[s] = ffn(pieces)
 
-    turns = partners[1:2] + partners[:1] + partners[2:] + [0]
-    left, stayed, sums, back = {}, {}, {}, {}
-
-    def first_half(n):
-        if n < len(turns):
-            s = turns[n]
-            order_after = [stayed[turns[n - 2]]] if n > 1 else [left[turns[n - 1]]] if n > 0 else []
-            left[s] = [leave(*after(hidden[s], *order_after))] if per_shard == 2 else []
-
-    first_half(0)
-    first_half(1)
     for n, s in enumerate(turns):
-        order_after = [stayed[turns[n - 1]]] if n > 0 else []
-        stayed[s] = stay(*after(hidden[s], *order_after), left[s])
-        first_half(n + 2)
+        for other in turns[n : n + 2]:
+            first_half(other)
+        stayed[s] = stay(*hidden[s], left[s])
     for n, s in enumerate(turns):
         keep, message = stayed[s]
-        if n > 1:
-            message = after(message, sums[turns[n - 2]][1])
-        keep, arrived = across(keep, message)
-        sums[s] = keep, arrived
+        if n > 0:
+            message = after(message, sums[turns[max(n - 2, 0)]][1])
+        sums[s] = keep, arrived = across(keep, message)
         if s > 0:
-            both = (keep + arrived.astype(f32)).astype(bf16)
+            both = (keep + arrived[0].astype(f32)).astype(bf16)
             back[s] = swap_bit(both, "grp", s)
     return call(
         functools.partial(finish_kernel, order, part),
         shape((rows, out_cols), bf16),
-        (*sums[0], *back.values()),
+        (sums[0][0], sums[0][1][0], *back.values()),
     )
 
 

time: 88.9 us -> 85.7 us (0.964)
  waiting for transfers between devices: 48.4 us -> 42.2 us
  starting transfers between devices: 19.4 us -> 22.4 us
  local copies, waits for them, and re-layouts: 6.4 us -> 5.01 us
  other arithmetic: 0.22 us -> 1.61 us
    ppermute x24, waiting for transfers between devices: 48.4 us -> 42.2 us  [swap_bit(): return lax.ppermute(value, axis, [(i, i ^ bit) for i in range(size)])]
    ppermute x24, starting transfers between devices: 19.4 us -> 22.4 us  [swap_bit(): return lax.ppermute(value, axis, [(i, i ^ bit) for i in range(size)])]
    convert_element_type x3 -> x5, other arithmetic: 0.22 us -> 1.6 us  [the longest x1 0.7 us: body(): expert_ids.T.astype(f32)]
    unnamed x16 -> x12, local copies, waits for them, and re-layouts: 6.4 us -> 5.01 us
  transfers between devices with their start and end apart: 24 -> 24, of which waited for: 11 -> 9; matrix products, arithmetic and copies ran while one was open for 0% -> 2% of each run, Pallas kernels for 15% -> 15%
where the time goes in v5:
time: 85.7 us; the launch traced here: 85.4 us
  waiting for transfers between devices  42.2 us (49%)
  starting transfers between devices  22.4 us (26%)
  Pallas kernels  14 us (16%)
  local copies, waits for them, and re-layouts  5.01 us (6%)
  other arithmetic  1.61 us (2%)
    ppermute x24, waiting for transfers between devices, swap_bit(): return lax.ppermute(value, axis, [(i, i ^ bit) for i in range(size)])  42.2 us
    ppermute x24, starting transfers between devices, swap_bit(): return lax.ppermute(value, axis, [(i, i ^ bit) for i in range(size)])  22.4 us
    pallas_call x14, Pallas kernels, call(): pl.pallas_call(kernel, out_shape=outs, in_specs=in_specs or [VM] * len(ar...  14 us
    unnamed x12, local copies, waits for them, and re-layouts  5.01 us
  transfers between devices with their start and end apart: 24, of which 9 were waited for; matrix products, arithmetic and copies ran while one was open for 2% of the time, Pallas kernels for 15%

profile of v5, /device:TPU:0, one launch (start us, length us, event | category | flops | bytes accessed | tf_op | source)
XLA Modules:
  0.0 85.4 jit_solution(27953332979072729)
XLA Ops:
  0.0 2.9 %collective-permute-start = (bf16[768,1024]{1,0:T(8,128)(2,1)}, bf16[768,1024]{1,0:T(8,128)(2,1)S(1)}, u32[]{:S(2)}, u32[]{:S(2)}) collective-permute-start(bf16[768,1024]{1,0:T(8,128)(2,1)} %bitcast.15), channel_id=1, source_target_pairs={{0,1},{1,0},{2,3},{3,2},{4,5},{5,4},{6,7},{7,6},{8,9},{9,8},{10,11... | collective-permute-start | bytes 4718600 | tf_op jit(solution)/shard_map/ppermute | solution.py:18
  2.9 0.7 convert_bitcast_fusion
  3.6 0.7 convert_bitcast_fusion.1
  4.3 1.2 %copy-done.5 = bf16[256,2048]{1,0:T(8,128)(2,1)S(1)} copy-done((bf16[256,2048]{1,0:T(8,128)(2,1)S(1)}, bf16[256,2048]{1,0:T(8,128)(2,1)}, u32[]{:S(2)}) %copy-start.5) | copy-done | bytes 1048600
  5.8 3.7 %collective-permute-start.8 = (bf16[64,2176]{1,0:T(8,128)(2,1)S(1)}, bf16[64,2176]{1,0:T(8,128)(2,1)S(1)}, u32[]{:S(2)}, u32[]{:S(2)}) collective-permute-start(bf16[64,2176]{1,0:T(8,128)(2,1)S(1)} %get-tuple-element.39), channel_id=1, source_target_pairs={{0,24},{8,16},{16,8},{24,0},{1,25},{9,17},{17,9},{25,1},{2,26},{10... | collective-permute-start | bytes 835592 | tf_op jit(solution)/shard_map/ppermute | solution.py:18
  9.4 1.9 %copy-done.1 = bf16[1,2048,768]{2,1,0:T(8,128)(2,1)S(1)} copy-done((bf16[1,2048,768]{2,1,0:T(8,128)(2,1)S(1)}, bf16[1,2048,768]{2,1,0:T(8,128)(2,1)}, u32[]{:S(2)}) %copy-start.1) | copy-done | bytes 3145752
  11.3 1.9 %copy-done.3 = bf16[1,2048,768]{2,1,0:T(8,128)(2,1)S(1)} copy-done((bf16[1,2048,768]{2,1,0:T(8,128)(2,1)S(1)}, bf16[1,2048,768]{2,1,0:T(8,128)(2,1)}, u32[]{:S(2)}) %copy-start.3) | copy-done | bytes 3145752
  13.2 2.0 %shard_map.65 = (bf16[256,768]{1,0:T(8,128)(2,1)S(1)}, f32[256,128]{1,0:T(8,128)S(1)}) custom-call(bf16[256,2048]{1,0:T(8,128)(2,1)S(1)} %copy-done.5, bf16[256,128]{1,0:T(8,128)(2,1)S(1)} %get-tuple-element.34.refs_1_, bf16[2048,768]{1,0:T(8,128)(2,1)S(1)} %bitcast.24, bf16[2048,768]{1,0:T(8,128)(2,1)S(1)} %bitcast.28), custom_call_target="tpu_custom_call" | custom-call | flops 1610612736 | bytes 7929856 | tf_op jit(solution)/shard_map/pallas_call | solution.py:39
  15.3 2.0 %collective-permute-done.8.refs_0_ = bf16[64,2176]{1,0:T(8,128)(2,1)S(1)} collective-permute-done((bf16[64,2176]{1,0:T(8,128)(2,1)S(1)}, bf16[64,2176]{1,0:T(8,128)(2,1)S(1)}, u32[]{:S(2)}, u32[]{:S(2)}) %collective-permute-start.8) | collective-permute-done | bytes 278560 | tf_op jit(solution)/shard_map/ppermute | solution.py:18
  17.3 1.5 %collective-permute-start.9 = (bf16[64,2176]{1,0:T(8,128)(2,1)S(1)}, bf16[64,2176]{1,0:T(8,128)(2,1)S(1)}, u32[]{:S(2)}, u32[]{:S(2)}) collective-permute-start(bf16[64,2176]{1,0:T(8,128)(2,1)S(1)} %collective-permute-done.8.refs_0_), channel_id=1, source_target_pairs={{0,4},{2,6},{4,0},{6,2},{1,5},{3,7},{5,1},{7,3},{8,12},{10,14},{12... | collective-permute-start | bytes 835592 | tf_op jit(solution)/shard_map/ppermute | solution.py:18
  18.8 5.3 %collective-permute-start.2 = (bf16[64,2176]{1,0:T(8,128)(2,1)S(1)}, bf16[64,2176]{1,0:T(8,128)(2,1)S(1)}, u32[]{:S(2)}, u32[]{:S(2)}) collective-permute-start(bf16[64,2176]{1,0:T(8,128)(2,1)S(1)} %get-tuple-element.39), channel_id=1, source_target_pairs={{0,16},{8,24},{16,0},{24,8},{1,17},{9,25},{17,1},{25,9},{2,18},{10... | collective-permute-start | bytes 835592 | tf_op jit(solution)/shard_map/ppermute | solution.py:18
  25.1 10.1 %collective-permute-done.2.refs_0_ = bf16[64,2176]{1,0:T(8,128)(2,1)S(1)} collective-permute-done((bf16[64,2176]{1,0:T(8,128)(2,1)S(1)}, bf16[64,2176]{1,0:T(8,128)(2,1)S(1)}, u32[]{:S(2)}, u32[]{:S(2)}) %collective-permute-start.2) | collective-permute-done | bytes 278560 | tf_op jit(solution)/shard_map/ppermute | solution.py:18
  36.0 1.9 %shard_map.69 = (bf16[256,768]{1,0:T(8,128)(2,1)S(1)}, f32[256,128]{1,0:T(8,128)S(1)}) custom-call(bf16[64,2176]{1,0:T(8,128)(2,1)S(1)} %collective-permute-done.8.refs_0_, bf16[64,2176]{1,0:T(8,128)(2,1)S(1)} %collective-permute-done.9.refs_1_, bf16[64,2176]{1,0:T(8,128)(2,1)S(1)} %collective-permute-done.10.refs_2_, ...), custom_call_target="tpu_custom_call" | custom-call | flops 1610612736 | bytes 7929856 | tf_op jit(solution)/shard_map/pallas_call | solution.py:39
  37.8 0.6 shard_map.70
  39.1 1.9 %shard_map.68 = (bf16[256,768]{1,0:T(8,128)(2,1)S(1)}, f32[256,128]{1,0:T(8,128)S(1)}) custom-call(bf16[64,2176]{1,0:T(8,128)(2,1)S(1)} %collective-permute-done.4.refs_0_, bf16[64,2176]{1,0:T(8,128)(2,1)S(1)} %collective-permute-done.5.refs_1_, bf16[64,2176]{1,0:T(8,128)(2,1)S(1)} %collective-permute-done.6.refs_2_, ...), custom_call_target="tpu_custom_call" | custom-call | flops 1610612736 | bytes 7929856 | tf_op jit(solution)/shard_map/pallas_call | solution.py:39
  40.9 3.4 %collective-permute-done.3.refs_1_ = bf16[64,2176]{1,0:T(8,128)(2,1)S(1)} collective-permute-done((bf16[64,2176]{1,0:T(8,128)(2,1)S(1)}, bf16[64,2176]{1,0:T(8,128)(2,1)S(1)}, u32[]{:S(2)}, u32[]{:S(2)}) %collective-permute-start.3) | collective-permute-done | bytes 278560 | tf_op jit(solution)/shard_map/ppermute | solution.py:18
  44.3 0.6 shard_map.66
  45.5 0.6 shard_map.75
  46.2 1.9 %shard_map.71 = (bf16[256,768]{1,0:T(8,128)(2,1)S(1)}, f32[256,128]{1,0:T(8,128)S(1)}) custom-call(bf16[64,2176]{1,0:T(8,128)(2,1)S(1)} %collective-permute-done.2.refs_0_, bf16[64,2176]{1,0:T(8,128)(2,1)S(1)} %collective-permute-done.3.refs_1_, bf16[64,2176]{1,0:T(8,128)(2,1)S(1)} %collective-permute-done.12.refs_2_, ...), custom_call_target="tpu_custom_call" | custom-call | flops 1610612736 | bytes 7929856 | tf_op jit(solution)/shard_map/pallas_call | solution.py:39
  48.1 0.6 shard_map.72
  49.2 0.7 shard_map.74
  50.5 0.7 shard_map.67
  51.2 0.7 shard_map.76
  51.9 6.3 %collective-permute-done.16 = bf16[1,256,512]{2,1,0:T(8,128)(2,1)S(1)} collective-permute-done((bf16[1,256,512]{2,1,0:T(8,128)(2,1)S(1)}, bf16[1,256,512]{2,1,0:T(8,128)(2,1)S(1)}, u32[]{:S(2)}, u32[]{:S(2)}) %collective-permute-start.16) | collective-permute-done | bytes 262176 | tf_op jit(solution)/shard_map/ppermute | solution.py:18
  58.8 0.7 shard_map.73
  59.5 1.6 %collective-permute-start.17 = (bf16[1,256,512]{2,1,0:T(8,128)(2,1)S(1)}, bf16[1,256,512]{2,1,0:T(8,128)(2,1)S(1)}, u32[]{:S(2)}, u32[]{:S(2)}) collective-permute-start(bf16[1,256,512]{2,1,0:T(8,128)(2,1)S(1)} %get-tuple-element.56), channel_id=1, source_target_pairs={{0,4},{2,6},{4,0},{6,2},{1,5},{3,7},{5,1},{7,3},{8,12},{10,14},{12... | collective-permute-start | bytes 786440 | tf_op jit(solution)/shard_map/ppermute | solution.py:18
  61.1 1.9 %collective-permute-start.19 = (bf16[256,512]{1,0:T(8,128)(2,1)S(1)}, bf16[256,512]{1,0:T(8,128)(2,1)S(1)}, u32[]{:S(2)}, u32[]{:S(2)}) collective-permute-start(bf16[256,512]{1,0:T(8,128)(2,1)S(1)} %fusion), channel_id=1, source_target_pairs={{0,24},{8,16},{16,8},{24,0},{1,25},{9,17},{17,9},{25,1},{2,26},{10... | collective-permute-start | bytes 786440 | tf_op jit(solution)/shard_map/ppermute | solution.py:18
  63.0 4.5 %collective-permute-done.22 = bf16[1,256,512]{2,1,0:T(8,128)(2,1)S(1)} collective-permute-done((bf16[1,256,512]{2,1,0:T(8,128)(2,1)S(1)}, bf16[1,256,512]{2,1,0:T(8,128)(2,1)S(1)}, u32[]{:S(2)}, u32[]{:S(2)}) %collective-permute-start.22) | collective-permute-done | bytes 262176 | tf_op jit(solution)/shard_map/ppermute | solution.py:18
  67.7 3.6 %collective-permute-done.17 = bf16[1,256,512]{2,1,0:T(8,128)(2,1)S(1)} collective-permute-done((bf16[1,256,512]{2,1,0:T(8,128)(2,1)S(1)}, bf16[1,256,512]{2,1,0:T(8,128)(2,1)S(1)}, u32[]{:S(2)}, u32[]{:S(2)}) %collective-permute-start.17) | collective-permute-done | bytes 262176 | tf_op jit(solution)/shard_map/ppermute | solution.py:18
  72.3 5.4 %collective-permute-done.23.refs_2_ = bf16[256,512]{1,0:T(8,128)(2,1)S(1)} collective-permute-done((bf16[256,512]{1,0:T(8,128)(2,1)S(1)}, bf16[256,512]{1,0:T(8,128)(2,1)S(1)}, u32[]{:S(2)}, u32[]{:S(2)}) %collective-permute-start.23) | collective-permute-done | bytes 262176 | tf_op jit(solution)/shard_map/ppermute | solution.py:18
  77.8 6.8 %collective-permute-done.20.refs_1_ = bf16[256,512]{1,0:T(8,128)(2,1)S(1)} collective-permute-done((bf16[256,512]{1,0:T(8,128)(2,1)S(1)}, bf16[256,512]{1,0:T(8,128)(2,1)S(1)}, u32[]{:S(2)}, u32[]{:S(2)}) %collective-permute-start.20) | collective-permute-done | bytes 262176 | tf_op jit(solution)/shard_map/ppermute | solution.py:18
  84.6 0.9 %shard_map.77 = bf16[256,512]{1,0:T(8,128)(2,1)} custom-call(f32[256,512]{1,0:T(8,128)S(1)} %bitcast.32, bf16[256,512]{1,0:T(8,128)(2,1)S(1)} %bitcast.33, bf16[256,512]{1,0:T(8,128)(2,1)S(1)} %collective-permute-done.19.refs_0_, bf16[256,512]{1,0:T(8,128)(2,1)S(1)} %collective-permute-done.20.refs_1_, bf16[256,512]{1,0:T(8,128)(2,1)S(1)} %collective-permute-done.23.refs_2_), custom_call_target="tpu_custom_call" | custom-call | tf_op jit(solution)/shard_map/pallas_call | solution.py:39
  (48 shorter events, 6.2 us)
Async XLA Ops:
  0.0 37.8 %collective-permute-start = (bf16[768,1024]{1,0:T(8,128)(2,1)}, bf16[768,1024]{1,0:T(8,128)(2,1)S(1)}, u32[]{:S(2)}, u32[]{:S(2)}) collective-permute-start(bf16[768,1024]{1,0:T(8,128)(2,1)} %bitcast.15), channel_id=1, source_target_pairs={{0,1},{1,0},{2,3},{3,2},{4,5},{5,4},{6,7},{7,6},{8,9},{9,8},{10,11... | collective-permute-start | bytes 4718600 | tf_op jit(solution)/shard_map/ppermute | solution.py:18
  4.3 1.2 %copy-start.5 = (bf16[256,2048]{1,0:T(8,128)(2,1)S(1)}, bf16[256,2048]{1,0:T(8,128)(2,1)}, u32[]{:S(2)}) copy-start(bf16[256,2048]{1,0:T(8,128)(2,1)} %refs_0_.1) | copy-start | bytes 3145732
  5.8 11.5 %collective-permute-start.8 = (bf16[64,2176]{1,0:T(8,128)(2,1)S(1)}, bf16[64,2176]{1,0:T(8,128)(2,1)S(1)}, u32[]{:S(2)}, u32[]{:S(2)}) collective-permute-start(bf16[64,2176]{1,0:T(8,128)(2,1)S(1)} %get-tuple-element.39), channel_id=1, source_target_pairs={{0,24},{8,16},{16,8},{24,0},{1,25},{9,17},{17,9},{25,1},{2,26},{10... | collective-permute-start | bytes 835592 | tf_op jit(solution)/shard_map/ppermute | solution.py:18
  9.4 14.6 %collective-permute-start.4 = (bf16[64,2176]{1,0:T(8,128)(2,1)S(1)}, bf16[64,2176]{1,0:T(8,128)(2,1)S(1)}, u32[]{:S(2)}, u32[]{:S(2)}) collective-permute-start(bf16[64,2176]{1,0:T(8,128)(2,1)S(1)} %get-tuple-element.39), channel_id=1, source_target_pairs={{0,8},{8,0},{16,24},{24,16},{1,9},{9,1},{17,25},{25,17},{2,10},{10... | collective-permute-start | bytes 835592 | tf_op jit(solution)/shard_map/ppermute | solution.py:18
  9.4 1.9 %copy-start.1 = (bf16[1,2048,768]{2,1,0:T(8,128)(2,1)S(1)}, bf16[1,2048,768]{2,1,0:T(8,128)(2,1)}, u32[]{:S(2)}) copy-start(bf16[1,2048,768]{2,1,0:T(8,128)(2,1)} %param.9) | copy-start | bytes 9437188
  11.3 1.9 %copy-start.3 = (bf16[1,2048,768]{2,1,0:T(8,128)(2,1)S(1)}, bf16[1,2048,768]{2,1,0:T(8,128)(2,1)}, u32[]{:S(2)}) copy-start(bf16[1,2048,768]{2,1,0:T(8,128)(2,1)} %param.10) | copy-start | bytes 9437188
  13.2 22.7 %copy-start.2 = (bf16[1,2048,768]{2,1,0:T(8,128)(2,1)S(1)}, bf16[1,2048,768]{2,1,0:T(8,128)(2,1)}, u32[]{:S(2)}) copy-start(bf16[1,2048,768]{2,1,0:T(8,128)(2,1)} %param.9) | copy-start | bytes 9437188
  13.2 22.7 %copy-start.4 = (bf16[1,2048,768]{2,1,0:T(8,128)(2,1)S(1)}, bf16[1,2048,768]{2,1,0:T(8,128)(2,1)}, u32[]{:S(2)}) copy-start(bf16[1,2048,768]{2,1,0:T(8,128)(2,1)} %param.10) | copy-start | bytes 9437188
  17.3 20.6 %copy-start = (bf16[1,768,1024]{2,1,0:T(8,128)(2,1)S(1)}, bf16[1,768,1024]{2,1,0:T(8,128)(2,1)}, u32[]{:S(2)}) copy-start(bf16[1,768,1024]{2,1,0:T(8,128)(2,1)} %param.11) | copy-start | bytes 4718596
  17.3 7.3 %collective-permute-start.9 = (bf16[64,2176]{1,0:T(8,128)(2,1)S(1)}, bf16[64,2176]{1,0:T(8,128)(2,1)S(1)}, u32[]{:S(2)}, u32[]{:S(2)}) collective-permute-start(bf16[64,2176]{1,0:T(8,128)(2,1)S(1)} %collective-permute-done.8.refs_0_), channel_id=1, source_target_pairs={{0,4},{2,6},{4,0},{6,2},{1,5},{3,7},{5,1},{7,3},{8,12},{10,14},{12... | collective-permute-start | bytes 835592 | tf_op jit(solution)/shard_map/ppermute | solution.py:18
  18.8 16.4 %collective-permute-start.2 = (bf16[64,2176]{1,0:T(8,128)(2,1)S(1)}, bf16[64,2176]{1,0:T(8,128)(2,1)S(1)}, u32[]{:S(2)}, u32[]{:S(2)}) collective-permute-start(bf16[64,2176]{1,0:T(8,128)(2,1)S(1)} %get-tuple-element.39), channel_id=1, source_target_pairs={{0,16},{8,24},{16,0},{24,8},{1,17},{9,25},{17,1},{25,9},{2,18},{10... | collective-permute-start | bytes 835592 | tf_op jit(solution)/shard_map/ppermute | solution.py:18
  24.1 11.2 %collective-permute-start.5 = (bf16[64,2176]{1,0:T(8,128)(2,1)S(1)}, bf16[64,2176]{1,0:T(8,128)(2,1)S(1)}, u32[]{:S(2)}, u32[]{:S(2)}) collective-permute-start(bf16[64,2176]{1,0:T(8,128)(2,1)S(1)} %collective-permute-done.4.refs_0_), channel_id=1, source_target_pairs={{0,4},{2,6},{4,0},{6,2},{1,5},{3,7},{5,1},{7,3},{8,12},{10,14},{12... | collective-permute-start | bytes 835592 | tf_op jit(solution)/shard_map/ppermute | solution.py:18
  24.6 11.2 %collective-permute-start.10 = (bf16[64,2176]{1,0:T(8,128)(2,1)S(1)}, bf16[64,2176]{1,0:T(8,128)(2,1)S(1)}, u32[]{:S(2)}, u32[]{:S(2)}) collective-permute-start(bf16[64,2176]{1,0:T(8,128)(2,1)S(1)} %collective-permute-done.8.refs_0_), channel_id=1, source_target_pairs={{0,2},{2,0},{4,6},{6,4},{1,3},{3,1},{5,7},{7,5},{8,10},{10,8},{12,... | collective-permute-start | bytes 835592 | tf_op jit(solution)/shard_map/ppermute | solution.py:18
  24.6 11.4 %collective-permute-start.11 = (bf16[64,2176]{1,0:T(8,128)(2,1)S(1)}, bf16[64,2176]{1,0:T(8,128)(2,1)S(1)}, u32[]{:S(2)}, u32[]{:S(2)}) collective-permute-start(bf16[64,2176]{1,0:T(8,128)(2,1)S(1)} %collective-permute-done.9.refs_1_), channel_id=1, source_target_pairs={{0,2},{2,0},{4,6},{6,4},{1,3},{3,1},{5,7},{7,5},{8,10},{10,8},{12,... | collective-permute-start | bytes 835592 | tf_op jit(solution)/shard_map/ppermute | solution.py:18
  35.2 3.9 %collective-permute-start.6 = (bf16[64,2176]{1,0:T(8,128)(2,1)S(1)}, bf16[64,2176]{1,0:T(8,128)(2,1)S(1)}, u32[]{:S(2)}, u32[]{:S(2)}) collective-permute-start(bf16[64,2176]{1,0:T(8,128)(2,1)S(1)} %collective-permute-done.4.refs_0_), channel_id=1, source_target_pairs={{0,2},{2,0},{4,6},{6,4},{1,3},{3,1},{5,7},{7,5},{8,10},{10,8},{12,... | collective-permute-start | bytes 835592 | tf_op jit(solution)/shard_map/ppermute | solution.py:18
  35.2 9.1 %collective-permute-start.3 = (bf16[64,2176]{1,0:T(8,128)(2,1)S(1)}, bf16[64,2176]{1,0:T(8,128)(2,1)S(1)}, u32[]{:S(2)}, u32[]{:S(2)}) collective-permute-start(bf16[64,2176]{1,0:T(8,128)(2,1)S(1)} %collective-permute-done.2.refs_0_), channel_id=1, source_target_pairs={{0,4},{2,6},{4,0},{6,2},{1,5},{3,7},{5,1},{7,3},{8,12},{10,14},{12... | collective-permute-start | bytes 835592 | tf_op jit(solution)/shard_map/ppermute | solution.py:18
  35.7 3.3 %collective-permute-start.7 = (bf16[64,2176]{1,0:T(8,128)(2,1)S(1)}, bf16[64,2176]{1,0:T(8,128)(2,1)S(1)}, u32[]{:S(2)}, u32[]{:S(2)}) collective-permute-start(bf16[64,2176]{1,0:T(8,128)(2,1)S(1)} %collective-permute-done.5.refs_1_), channel_id=1, source_target_pairs={{0,2},{2,0},{4,6},{6,4},{1,3},{3,1},{5,7},{7,5},{8,10},{10,8},{12,... | collective-permute-start | bytes 835592 | tf_op jit(solution)/shard_map/ppermute | solution.py:18
  38.5 7.7 %collective-permute-start.14 = (bf16[2,256,512]{2,1,0:T(8,128)(2,1)S(1)}, bf16[2,256,512]{2,1,0:T(8,128)(2,1)S(1)}, u32[]{:S(2)}, u32[]{:S(2)}) collective-permute-start(bf16[2,256,512]{2,1,0:T(8,128)(2,1)S(1)} %shard_map.70), channel_id=1, source_target_pairs={{0,2},{2,0},{4,6},{6,4},{1,3},{3,1},{5,7},{7,5},{8,10},{10,8},{12,... | collective-permute-start | bytes 1572872 | tf_op jit(solution)/shard_map/ppermute | solution.py:18
  38.8 7.4 %collective-permute-start.12 = (bf16[64,2176]{1,0:T(8,128)(2,1)S(1)}, bf16[64,2176]{1,0:T(8,128)(2,1)S(1)}, u32[]{:S(2)}, u32[]{:S(2)}) collective-permute-start(bf16[64,2176]{1,0:T(8,128)(2,1)S(1)} %collective-permute-done.2.refs_0_), channel_id=1, source_target_pairs={{0,2},{2,0},{4,6},{6,4},{1,3},{3,1},{5,7},{7,5},{8,10},{10,8},{12,... | collective-permute-start | bytes 835592 | tf_op jit(solution)/shard_map/ppermute | solution.py:18
  44.3 1.9 %collective-permute-start.13 = (bf16[64,2176]{1,0:T(8,128)(2,1)S(1)}, bf16[64,2176]{1,0:T(8,128)(2,1)S(1)}, u32[]{:S(2)}, u32[]{:S(2)}) collective-permute-start(bf16[64,2176]{1,0:T(8,128)(2,1)S(1)} %collective-permute-done.3.refs_1_), channel_id=1, source_target_pairs={{0,2},{2,0},{4,6},{6,4},{1,3},{3,1},{5,7},{7,5},{8,10},{10,8},{12,... | collective-permute-start | bytes 835592 | tf_op jit(solution)/shard_map/ppermute | solution.py:18
  44.9 5.6 %collective-permute-start.1 = (bf16[2,256,512]{2,1,0:T(8,128)(2,1)S(1)}, bf16[2,256,512]{2,1,0:T(8,128)(2,1)S(1)}, u32[]{:S(2)}, u32[]{:S(2)}) collective-permute-start(bf16[2,256,512]{2,1,0:T(8,128)(2,1)S(1)} %shard_map.66), channel_id=1, source_target_pairs={{0,2},{2,0},{4,6},{6,4},{1,3},{3,1},{5,7},{7,5},{8,10},{10,8},{12,... | collective-permute-start | bytes 1572872 | tf_op jit(solution)/shard_map/ppermute | solution.py:18
  46.1 5.1 %collective-permute-start.21 = (bf16[2,256,512]{2,1,0:T(8,128)(2,1)S(1)}, bf16[2,256,512]{2,1,0:T(8,128)(2,1)S(1)}, u32[]{:S(2)}, u32[]{:S(2)}) collective-permute-start(bf16[2,256,512]{2,1,0:T(8,128)(2,1)S(1)} %shard_map.75), channel_id=1, source_target_pairs={{0,2},{2,0},{4,6},{6,4},{1,3},{3,1},{5,7},{7,5},{8,10},{10,8},{12,... | collective-permute-start | bytes 1572872 | tf_op jit(solution)/shard_map/ppermute | solution.py:18
  48.7 10.1 %collective-permute-start.15 = (bf16[2,256,512]{2,1,0:T(8,128)(2,1)S(1)}, bf16[2,256,512]{2,1,0:T(8,128)(2,1)S(1)}, u32[]{:S(2)}, u32[]{:S(2)}) collective-permute-start(bf16[2,256,512]{2,1,0:T(8,128)(2,1)S(1)} %shard_map.72), channel_id=1, source_target_pairs={{0,2},{2,0},{4,6},{6,4},{1,3},{3,1},{5,7},{7,5},{8,10},{10,8},{12,... | collective-permute-start | bytes 1572872 | tf_op jit(solution)/shard_map/ppermute | solution.py:18
  49.9 8.3 %collective-permute-start.16 = (bf16[1,256,512]{2,1,0:T(8,128)(2,1)S(1)}, bf16[1,256,512]{2,1,0:T(8,128)(2,1)S(1)}, u32[]{:S(2)}, u32[]{:S(2)}) collective-permute-start(bf16[1,256,512]{2,1,0:T(8,128)(2,1)S(1)} %get-tuple-element.55), channel_id=1, source_target_pairs={{0,4},{2,6},{4,0},{6,2},{1,5},{3,7},{5,1},{7,3},{8,12},{10,14},{12... | collective-permute-start | bytes 786440 | tf_op jit(solution)/shard_map/ppermute | solution.py:18
  58.3 9.2 %collective-permute-start.22 = (bf16[1,256,512]{2,1,0:T(8,128)(2,1)S(1)}, bf16[1,256,512]{2,1,0:T(8,128)(2,1)S(1)}, u32[]{:S(2)}, u32[]{:S(2)}) collective-permute-start(bf16[1,256,512]{2,1,0:T(8,128)(2,1)S(1)} %get-tuple-element.62), channel_id=1, source_target_pairs={{0,4},{2,6},{4,0},{6,2},{1,5},{3,7},{5,1},{7,3},{8,12},{10,14},{12... | collective-permute-start | bytes 786440 | tf_op jit(solution)/shard_map/ppermute | solution.py:18
  59.5 11.8 %collective-permute-start.17 = (bf16[1,256,512]{2,1,0:T(8,128)(2,1)S(1)}, bf16[1,256,512]{2,1,0:T(8,128)(2,1)S(1)}, u32[]{:S(2)}, u32[]{:S(2)}) collective-permute-start(bf16[1,256,512]{2,1,0:T(8,128)(2,1)S(1)} %get-tuple-element.56), channel_id=1, source_target_pairs={{0,4},{2,6},{4,0},{6,2},{1,5},{3,7},{5,1},{7,3},{8,12},{10,14},{12... | collective-permute-start | bytes 786440 | tf_op jit(solution)/shard_map/ppermute | solution.py:18
  61.1 11.2 %collective-permute-start.19 = (bf16[256,512]{1,0:T(8,128)(2,1)S(1)}, bf16[256,512]{1,0:T(8,128)(2,1)S(1)}, u32[]{:S(2)}, u32[]{:S(2)}) collective-permute-start(bf16[256,512]{1,0:T(8,128)(2,1)S(1)} %fusion), channel_id=1, source_target_pairs={{0,24},{8,16},{16,8},{24,0},{1,25},{9,17},{17,9},{25,1},{2,26},{10... | collective-permute-start | bytes 786440 | tf_op jit(solution)/shard_map/ppermute | solution.py:18
  67.6 10.1 %collective-permute-start.23 = (bf16[256,512]{1,0:T(8,128)(2,1)S(1)}, bf16[256,512]{1,0:T(8,128)(2,1)S(1)}, u32[]{:S(2)}, u32[]{:S(2)}) collective-permute-start(bf16[256,512]{1,0:T(8,128)(2,1)S(1)} %fusion.2), channel_id=1, source_target_pairs={{0,8},{8,0},{16,24},{24,16},{1,9},{9,1},{17,25},{25,17},{2,10},{10... | collective-permute-start | bytes 786440 | tf_op jit(solution)/shard_map/ppermute | solution.py:18
  71.3 6.5 %collective-permute-start.18 = (bf16[1,256,512]{2,1,0:T(8,128)(2,1)S(1)}, bf16[1,256,512]{2,1,0:T(8,128)(2,1)S(1)}, u32[]{:S(2)}, u32[]{:S(2)}) collective-permute-start(bf16[1,256,512]{2,1,0:T(8,128)(2,1)S(1)} %get-tuple-element.57), channel_id=1, source_target_pairs={{0,4},{2,6},{4,0},{6,2},{1,5},{3,7},{5,1},{7,3},{8,12},{10,14},{12... | collective-permute-start | bytes 786440 | tf_op jit(solution)/shard_map/ppermute | solution.py:18
  71.9 12.7 %collective-permute-start.20 = (bf16[256,512]{1,0:T(8,128)(2,1)S(1)}, bf16[256,512]{1,0:T(8,128)(2,1)S(1)}, u32[]{:S(2)}, u32[]{:S(2)}) collective-permute-start(bf16[256,512]{1,0:T(8,128)(2,1)S(1)} %fusion.1), channel_id=1, source_target_pairs={{0,16},{8,24},{16,0},{24,8},{1,17},{9,25},{17,1},{25,9},{2,18},{10... | collective-permute-start | bytes 786440 | tf_op jit(solution)/shard_map/ppermute | solution.py:18

commit v6 on v5

--- a/solution.py
+++ b/solution.py
@@ -165,7 +165,7 @@
     per_shard = group_size // tp_size
     lanes = -(-groups * group_size // LANES) * LANES
     order = part_order(group_size)
-    partners = [1] + list(range(groups - 1, 1, -1))
+    partners = list(range(1, groups))
     shape = jax.ShapeDtypeStruct
     bf16, f32 = jnp.bfloat16, jnp.float32
 

time: 85.7 us -> 84.4 us (0.985); the launches traced: 85.4 us -> 82.7 us
  waiting for transfers between devices: 42.2 us -> 28.6 us
  starting transfers between devices: 22.4 us -> 33.4 us
    ppermute x24, waiting for transfers between devices: 42.2 us -> 28.6 us  [swap_bit(): return lax.ppermute(value, axis, [(i, i ^ bit) for i in range(size)])]
    ppermute x24, starting transfers between devices: 22.4 us -> 33.4 us  [swap_bit(): return lax.ppermute(value, axis, [(i, i ^ bit) for i in range(size)])]
  transfers between devices with their start and end apart: 24 -> 24, of which waited for: 9 -> 9; matrix products, arithmetic and copies ran while one was open for 2% -> 2% of each run, Pallas kernels for 15% -> 16%
where the time goes in v6:
time: 84.4 us; the launch traced here: 82.7 us
  starting transfers between devices  33.4 us (40%)
  waiting for transfers between devices  28.6 us (34%)
  Pallas kernels  14 us (17%)
  local copies, waits for them, and re-layouts  5.01 us (6%)
  other arithmetic  1.61 us (2%)
    ppermute x24, starting transfers between devices, swap_bit(): return lax.ppermute(value, axis, [(i, i ^ bit) for i in range(size)])  33.4 us
    ppermute x24, waiting for transfers between devices, swap_bit(): return lax.ppermute(value, axis, [(i, i ^ bit) for i in range(size)])  28.6 us
    pallas_call x14, Pallas kernels, call(): pl.pallas_call(kernel, out_shape=outs, in_specs=in_specs or [VM] * len(ar...  14 us
    unnamed x12, local copies, waits for them, and re-layouts  5.01 us
  transfers between devices with their start and end apart: 24, of which 9 were waited for; matrix products, arithmetic and copies ran while one was open for 2% of the time, Pallas kernels for 16%

profile of v6, /device:TPU:0, one launch (start us, length us, event | category | flops | bytes accessed | tf_op | source)
XLA Modules:
  0.0 82.7 jit_solution(12185278780618356454)
XLA Ops:
  0.0 2.9 %collective-permute-start = (bf16[768,1024]{1,0:T(8,128)(2,1)}, bf16[768,1024]{1,0:T(8,128)(2,1)S(1)}, u32[]{:S(2)}, u32[]{:S(2)}) collective-permute-start(bf16[768,1024]{1,0:T(8,128)(2,1)} %bitcast.15), channel_id=1, source_target_pairs={{0,1},{1,0},{2,3},{3,2},{4,5},{5,4},{6,7},{7,6},{8,9},{9,8},{10,11... | collective-permute-start | bytes 4718600 | tf_op jit(solution)/shard_map/ppermute | solution.py:18
  3.6 0.7 convert_bitcast_fusion.1
  4.3 1.2 %copy-done.5 = bf16[256,2048]{1,0:T(8,128)(2,1)S(1)} copy-done((bf16[256,2048]{1,0:T(8,128)(2,1)S(1)}, bf16[256,2048]{1,0:T(8,128)(2,1)}, u32[]{:S(2)}) %copy-start.5) | copy-done | bytes 1048600
  5.8 2.7 %collective-permute-start.8 = (bf16[64,2176]{1,0:T(8,128)(2,1)S(1)}, bf16[64,2176]{1,0:T(8,128)(2,1)S(1)}, u32[]{:S(2)}, u32[]{:S(2)}) collective-permute-start(bf16[64,2176]{1,0:T(8,128)(2,1)S(1)} %get-tuple-element.39), channel_id=1, source_target_pairs={{0,16},{8,24},{16,0},{24,8},{1,17},{9,25},{17,1},{25,9},{2,18},{10... | collective-permute-start | bytes 835592 | tf_op jit(solution)/shard_map/ppermute | solution.py:18
  8.4 1.6 %collective-permute-start.4 = (bf16[64,2176]{1,0:T(8,128)(2,1)S(1)}, bf16[64,2176]{1,0:T(8,128)(2,1)S(1)}, u32[]{:S(2)}, u32[]{:S(2)}) collective-permute-start(bf16[64,2176]{1,0:T(8,128)(2,1)S(1)} %get-tuple-element.39), channel_id=1, source_target_pairs={{0,8},{8,0},{16,24},{24,16},{1,9},{9,1},{17,25},{25,17},{2,10},{10... | collective-permute-start | bytes 835592 | tf_op jit(solution)/shard_map/ppermute | solution.py:18
  10.0 1.9 %copy-done.1 = bf16[1,2048,768]{2,1,0:T(8,128)(2,1)S(1)} copy-done((bf16[1,2048,768]{2,1,0:T(8,128)(2,1)S(1)}, bf16[1,2048,768]{2,1,0:T(8,128)(2,1)}, u32[]{:S(2)}) %copy-start.1) | copy-done | bytes 3145752
  11.9 1.9 %copy-done.3 = bf16[1,2048,768]{2,1,0:T(8,128)(2,1)S(1)} copy-done((bf16[1,2048,768]{2,1,0:T(8,128)(2,1)S(1)}, bf16[1,2048,768]{2,1,0:T(8,128)(2,1)}, u32[]{:S(2)}) %copy-start.3) | copy-done | bytes 3145752
  13.8 2.0 %shard_map.65 = (bf16[256,768]{1,0:T(8,128)(2,1)S(1)}, f32[256,128]{1,0:T(8,128)S(1)}) custom-call(bf16[256,2048]{1,0:T(8,128)(2,1)S(1)} %copy-done.5, bf16[256,128]{1,0:T(8,128)(2,1)S(1)} %get-tuple-element.34.refs_1_, bf16[2048,768]{1,0:T(8,128)(2,1)S(1)} %bitcast.24, bf16[2048,768]{1,0:T(8,128)(2,1)S(1)} %bitcast.28), custom_call_target="tpu_custom_call" | custom-call | flops 1610612736 | bytes 7929856 | tf_op jit(solution)/shard_map/pallas_call | solution.py:39
  15.8 5.1 %collective-permute-done.8.refs_0_ = bf16[64,2176]{1,0:T(8,128)(2,1)S(1)} collective-permute-done((bf16[64,2176]{1,0:T(8,128)(2,1)S(1)}, bf16[64,2176]{1,0:T(8,128)(2,1)S(1)}, u32[]{:S(2)}, u32[]{:S(2)}) %collective-permute-start.8) | collective-permute-done | bytes 278560 | tf_op jit(solution)/shard_map/ppermute | solution.py:18
  20.9 1.5 %collective-permute-start.9 = (bf16[64,2176]{1,0:T(8,128)(2,1)S(1)}, bf16[64,2176]{1,0:T(8,128)(2,1)S(1)}, u32[]{:S(2)}, u32[]{:S(2)}) collective-permute-start(bf16[64,2176]{1,0:T(8,128)(2,1)S(1)} %collective-permute-done.8.refs_0_), channel_id=1, source_target_pairs={{0,4},{2,6},{4,0},{6,2},{1,5},{3,7},{5,1},{7,3},{8,12},{10,14},{12... | collective-permute-start | bytes 835592 | tf_op jit(solution)/shard_map/ppermute | solution.py:18
  22.5 3.4 %collective-permute-start.2 = (bf16[64,2176]{1,0:T(8,128)(2,1)S(1)}, bf16[64,2176]{1,0:T(8,128)(2,1)S(1)}, u32[]{:S(2)}, u32[]{:S(2)}) collective-permute-start(bf16[64,2176]{1,0:T(8,128)(2,1)S(1)} %get-tuple-element.39), channel_id=1, source_target_pairs={{0,24},{8,16},{16,8},{24,0},{1,25},{9,17},{17,9},{25,1},{2,26},{10... | collective-permute-start | bytes 835592 | tf_op jit(solution)/shard_map/ppermute | solution.py:18
  26.4 2.5 %collective-permute-done.9.refs_1_ = bf16[64,2176]{1,0:T(8,128)(2,1)S(1)} collective-permute-done((bf16[64,2176]{1,0:T(8,128)(2,1)S(1)}, bf16[64,2176]{1,0:T(8,128)(2,1)S(1)}, u32[]{:S(2)}, u32[]{:S(2)}) %collective-permute-start.9) | collective-permute-done | bytes 278560 | tf_op jit(solution)/shard_map/ppermute | solution.py:18
  28.9 3.6 %collective-permute-done.2.refs_0_ = bf16[64,2176]{1,0:T(8,128)(2,1)S(1)} collective-permute-done((bf16[64,2176]{1,0:T(8,128)(2,1)S(1)}, bf16[64,2176]{1,0:T(8,128)(2,1)S(1)}, u32[]{:S(2)}, u32[]{:S(2)}) %collective-permute-start.2) | collective-permute-done | bytes 278560 | tf_op jit(solution)/shard_map/ppermute | solution.py:18
  32.5 1.8 %collective-permute-done.5.refs_1_ = bf16[64,2176]{1,0:T(8,128)(2,1)S(1)} collective-permute-done((bf16[64,2176]{1,0:T(8,128)(2,1)S(1)}, bf16[64,2176]{1,0:T(8,128)(2,1)S(1)}, u32[]{:S(2)}, u32[]{:S(2)}) %collective-permute-start.5) | collective-permute-done | bytes 278560 | tf_op jit(solution)/shard_map/ppermute | solution.py:18
  34.4 1.5 %collective-permute-start.3 = (bf16[64,2176]{1,0:T(8,128)(2,1)S(1)}, bf16[64,2176]{1,0:T(8,128)(2,1)S(1)}, u32[]{:S(2)}, u32[]{:S(2)}) collective-permute-start(bf16[64,2176]{1,0:T(8,128)(2,1)S(1)} %collective-permute-done.2.refs_0_), channel_id=1, source_target_pairs={{0,4},{2,6},{4,0},{6,2},{1,5},{3,7},{5,1},{7,3},{8,12},{10,14},{12... | collective-permute-start | bytes 835592 | tf_op jit(solution)/shard_map/ppermute | solution.py:18
  35.9 1.9 %shard_map.69 = (bf16[256,768]{1,0:T(8,128)(2,1)S(1)}, f32[256,128]{1,0:T(8,128)S(1)}) custom-call(bf16[64,2176]{1,0:T(8,128)(2,1)S(1)} %collective-permute-done.8.refs_0_, bf16[64,2176]{1,0:T(8,128)(2,1)S(1)} %collective-permute-done.9.refs_1_, bf16[64,2176]{1,0:T(8,128)(2,1)S(1)} %collective-permute-done.10.refs_2_, ...), custom_call_target="tpu_custom_call" | custom-call | flops 1610612736 | bytes 7929856 | tf_op jit(solution)/shard_map/pallas_call | solution.py:39
  39.1 1.9 %shard_map.68 = (bf16[256,768]{1,0:T(8,128)(2,1)S(1)}, f32[256,128]{1,0:T(8,128)S(1)}) custom-call(bf16[64,2176]{1,0:T(8,128)(2,1)S(1)} %collective-permute-done.4.refs_0_, bf16[64,2176]{1,0:T(8,128)(2,1)S(1)} %collective-permute-done.5.refs_1_, bf16[64,2176]{1,0:T(8,128)(2,1)S(1)} %collective-permute-done.6.refs_2_, ...), custom_call_target="tpu_custom_call" | custom-call | flops 1610612736 | bytes 7929856 | tf_op jit(solution)/shard_map/pallas_call | solution.py:39
  40.9 1.0 %collective-permute-done.3.refs_1_ = bf16[64,2176]{1,0:T(8,128)(2,1)S(1)} collective-permute-done((bf16[64,2176]{1,0:T(8,128)(2,1)S(1)}, bf16[64,2176]{1,0:T(8,128)(2,1)S(1)}, u32[]{:S(2)}, u32[]{:S(2)}) %collective-permute-start.3) | collective-permute-done | bytes 278560 | tf_op jit(solution)/shard_map/ppermute | solution.py:18
  43.9 1.9 %shard_map.71 = (bf16[256,768]{1,0:T(8,128)(2,1)S(1)}, f32[256,128]{1,0:T(8,128)S(1)}) custom-call(bf16[64,2176]{1,0:T(8,128)(2,1)S(1)} %collective-permute-done.2.refs_0_, bf16[64,2176]{1,0:T(8,128)(2,1)S(1)} %collective-permute-done.3.refs_1_, bf16[64,2176]{1,0:T(8,128)(2,1)S(1)} %collective-permute-done.12.refs_2_, ...), custom_call_target="tpu_custom_call" | custom-call | flops 1610612736 | bytes 7929856 | tf_op jit(solution)/shard_map/pallas_call | solution.py:39
  47.6 1.2 %collective-permute-start.16 = (bf16[1,256,512]{2,1,0:T(8,128)(2,1)S(1)}, bf16[1,256,512]{2,1,0:T(8,128)(2,1)S(1)}, u32[]{:S(2)}, u32[]{:S(2)}) collective-permute-start(bf16[1,256,512]{2,1,0:T(8,128)(2,1)S(1)} %get-tuple-element.55), channel_id=1, source_target_pairs={{0,4},{2,6},{4,0},{6,2},{1,5},{3,7},{5,1},{7,3},{8,12},{10,14},{12... | collective-permute-start | bytes 786440 | tf_op jit(solution)/shard_map/ppermute | solution.py:18
  48.8 0.7 shard_map.67
  49.5 0.7 shard_map.76
  50.3 5.7 %collective-permute-done.16 = bf16[1,256,512]{2,1,0:T(8,128)(2,1)S(1)} collective-permute-done((bf16[1,256,512]{2,1,0:T(8,128)(2,1)S(1)}, bf16[1,256,512]{2,1,0:T(8,128)(2,1)S(1)}, u32[]{:S(2)}, u32[]{:S(2)}) %collective-permute-start.16) | collective-permute-done | bytes 262176 | tf_op jit(solution)/shard_map/ppermute | solution.py:18
  55.9 1.2 %collective-permute-start.22 = (bf16[1,256,512]{2,1,0:T(8,128)(2,1)S(1)}, bf16[1,256,512]{2,1,0:T(8,128)(2,1)S(1)}, u32[]{:S(2)}, u32[]{:S(2)}) collective-permute-start(bf16[1,256,512]{2,1,0:T(8,128)(2,1)S(1)} %get-tuple-element.62), channel_id=1, source_target_pairs={{0,4},{2,6},{4,0},{6,2},{1,5},{3,7},{5,1},{7,3},{8,12},{10,14},{12... | collective-permute-start | bytes 786440 | tf_op jit(solution)/shard_map/ppermute | solution.py:18
  57.8 0.9 %collective-permute-start.17 = (bf16[1,256,512]{2,1,0:T(8,128)(2,1)S(1)}, bf16[1,256,512]{2,1,0:T(8,128)(2,1)S(1)}, u32[]{:S(2)}, u32[]{:S(2)}) collective-permute-start(bf16[1,256,512]{2,1,0:T(8,128)(2,1)S(1)} %get-tuple-element.56), channel_id=1, source_target_pairs={{0,4},{2,6},{4,0},{6,2},{1,5},{3,7},{5,1},{7,3},{8,12},{10,14},{12... | collective-permute-start | bytes 786440 | tf_op jit(solution)/shard_map/ppermute | solution.py:18
  58.8 4.2 %collective-permute-start.19 = (bf16[256,512]{1,0:T(8,128)(2,1)S(1)}, bf16[256,512]{1,0:T(8,128)(2,1)S(1)}, u32[]{:S(2)}, u32[]{:S(2)}) collective-permute-start(bf16[256,512]{1,0:T(8,128)(2,1)S(1)} %fusion), channel_id=1, source_target_pairs={{0,16},{8,24},{16,0},{24,8},{1,17},{9,25},{17,1},{25,9},{2,18},{10... | collective-permute-start | bytes 786440 | tf_op jit(solution)/shard_map/ppermute | solution.py:18
  63.0 2.2 %collective-permute-done.22 = bf16[1,256,512]{2,1,0:T(8,128)(2,1)S(1)} collective-permute-done((bf16[1,256,512]{2,1,0:T(8,128)(2,1)S(1)}, bf16[1,256,512]{2,1,0:T(8,128)(2,1)S(1)}, u32[]{:S(2)}, u32[]{:S(2)}) %collective-permute-start.22) | collective-permute-done | bytes 262176 | tf_op jit(solution)/shard_map/ppermute | solution.py:18
  65.2 4.5 %collective-permute-start.23 = (bf16[256,512]{1,0:T(8,128)(2,1)S(1)}, bf16[256,512]{1,0:T(8,128)(2,1)S(1)}, u32[]{:S(2)}, u32[]{:S(2)}) collective-permute-start(bf16[256,512]{1,0:T(8,128)(2,1)S(1)} %fusion.2), channel_id=1, source_target_pairs={{0,8},{8,0},{16,24},{24,16},{1,9},{9,1},{17,25},{25,17},{2,10},{10... | collective-permute-start | bytes 786440 | tf_op jit(solution)/shard_map/ppermute | solution.py:18
  70.3 5.0 %collective-permute-start.20 = (bf16[256,512]{1,0:T(8,128)(2,1)S(1)}, bf16[256,512]{1,0:T(8,128)(2,1)S(1)}, u32[]{:S(2)}, u32[]{:S(2)}) collective-permute-start(bf16[256,512]{1,0:T(8,128)(2,1)S(1)} %fusion.1), channel_id=1, source_target_pairs={{0,24},{8,16},{16,8},{24,0},{1,25},{9,17},{17,9},{25,1},{2,26},{10... | collective-permute-start | bytes 786440 | tf_op jit(solution)/shard_map/ppermute | solution.py:18
  75.3 2.2 %collective-permute-done.23.refs_2_ = bf16[256,512]{1,0:T(8,128)(2,1)S(1)} collective-permute-done((bf16[256,512]{1,0:T(8,128)(2,1)S(1)}, bf16[256,512]{1,0:T(8,128)(2,1)S(1)}, u32[]{:S(2)}, u32[]{:S(2)}) %collective-permute-start.23) | collective-permute-done | bytes 262176 | tf_op jit(solution)/shard_map/ppermute | solution.py:18
  77.5 4.4 %collective-permute-done.20.refs_1_ = bf16[256,512]{1,0:T(8,128)(2,1)S(1)} collective-permute-done((bf16[256,512]{1,0:T(8,128)(2,1)S(1)}, bf16[256,512]{1,0:T(8,128)(2,1)S(1)}, u32[]{:S(2)}, u32[]{:S(2)}) %collective-permute-start.20) | collective-permute-done | bytes 262176 | tf_op jit(solution)/shard_map/ppermute | solution.py:18
  81.9 0.9 %shard_map.77 = bf16[256,512]{1,0:T(8,128)(2,1)} custom-call(f32[256,512]{1,0:T(8,128)S(1)} %bitcast.32, bf16[256,512]{1,0:T(8,128)(2,1)S(1)} %bitcast.33, bf16[256,512]{1,0:T(8,128)(2,1)S(1)} %collective-permute-done.19.refs_0_, bf16[256,512]{1,0:T(8,128)(2,1)S(1)} %collective-permute-done.20.refs_1_, bf16[256,512]{1,0:T(8,128)(2,1)S(1)} %collective-permute-done.23.refs_2_), custom_call_target="tpu_custom_call" | custom-call | tf_op jit(solution)/shard_map/pallas_call | solution.py:39
  (48 shorter events, 7.9 us)
Async XLA Ops:
  0.0 37.8 %collective-permute-start = (bf16[768,1024]{1,0:T(8,128)(2,1)}, bf16[768,1024]{1,0:T(8,128)(2,1)S(1)}, u32[]{:S(2)}, u32[]{:S(2)}) collective-permute-start(bf16[768,1024]{1,0:T(8,128)(2,1)} %bitcast.15), channel_id=1, source_target_pairs={{0,1},{1,0},{2,3},{3,2},{4,5},{5,4},{6,7},{7,6},{8,9},{9,8},{10,11... | collective-permute-start | bytes 4718600 | tf_op jit(solution)/shard_map/ppermute | solution.py:18
  4.3 1.2 %copy-start.5 = (bf16[256,2048]{1,0:T(8,128)(2,1)S(1)}, bf16[256,2048]{1,0:T(8,128)(2,1)}, u32[]{:S(2)}) copy-start(bf16[256,2048]{1,0:T(8,128)(2,1)} %refs_0_.1) | copy-start | bytes 3145732
  5.8 15.2 %collective-permute-start.8 = (bf16[64,2176]{1,0:T(8,128)(2,1)S(1)}, bf16[64,2176]{1,0:T(8,128)(2,1)S(1)}, u32[]{:S(2)}, u32[]{:S(2)}) collective-permute-start(bf16[64,2176]{1,0:T(8,128)(2,1)S(1)} %get-tuple-element.39), channel_id=1, source_target_pairs={{0,16},{8,24},{16,0},{24,8},{1,17},{9,25},{17,1},{25,9},{2,18},{10... | collective-permute-start | bytes 835592 | tf_op jit(solution)/shard_map/ppermute | solution.py:18
  8.4 17.4 %collective-permute-start.4 = (bf16[64,2176]{1,0:T(8,128)(2,1)S(1)}, bf16[64,2176]{1,0:T(8,128)(2,1)S(1)}, u32[]{:S(2)}, u32[]{:S(2)}) collective-permute-start(bf16[64,2176]{1,0:T(8,128)(2,1)S(1)} %get-tuple-element.39), channel_id=1, source_target_pairs={{0,8},{8,0},{16,24},{24,16},{1,9},{9,1},{17,25},{25,17},{2,10},{10... | collective-permute-start | bytes 835592 | tf_op jit(solution)/shard_map/ppermute | solution.py:18
  10.0 1.9 %copy-start.1 = (bf16[1,2048,768]{2,1,0:T(8,128)(2,1)S(1)}, bf16[1,2048,768]{2,1,0:T(8,128)(2,1)}, u32[]{:S(2)}) copy-start(bf16[1,2048,768]{2,1,0:T(8,128)(2,1)} %param.9) | copy-start | bytes 9437188
  11.9 1.9 %copy-start.3 = (bf16[1,2048,768]{2,1,0:T(8,128)(2,1)S(1)}, bf16[1,2048,768]{2,1,0:T(8,128)(2,1)}, u32[]{:S(2)}) copy-start(bf16[1,2048,768]{2,1,0:T(8,128)(2,1)} %param.10) | copy-start | bytes 9437188
  13.8 22.1 %copy-start.2 = (bf16[1,2048,768]{2,1,0:T(8,128)(2,1)S(1)}, bf16[1,2048,768]{2,1,0:T(8,128)(2,1)}, u32[]{:S(2)}) copy-start(bf16[1,2048,768]{2,1,0:T(8,128)(2,1)} %param.9) | copy-start | bytes 9437188
  13.8 22.1 %copy-start.4 = (bf16[1,2048,768]{2,1,0:T(8,128)(2,1)S(1)}, bf16[1,2048,768]{2,1,0:T(8,128)(2,1)}, u32[]{:S(2)}) copy-start(bf16[1,2048,768]{2,1,0:T(8,128)(2,1)} %param.10) | copy-start | bytes 9437188
  20.9 16.9 %copy-start = (bf16[1,768,1024]{2,1,0:T(8,128)(2,1)S(1)}, bf16[1,768,1024]{2,1,0:T(8,128)(2,1)}, u32[]{:S(2)}) copy-start(bf16[1,768,1024]{2,1,0:T(8,128)(2,1)} %param.11) | copy-start | bytes 4718596
  20.9 7.9 %collective-permute-start.9 = (bf16[64,2176]{1,0:T(8,128)(2,1)S(1)}, bf16[64,2176]{1,0:T(8,128)(2,1)S(1)}, u32[]{:S(2)}, u32[]{:S(2)}) collective-permute-start(bf16[64,2176]{1,0:T(8,128)(2,1)S(1)} %collective-permute-done.8.refs_0_), channel_id=1, source_target_pairs={{0,4},{2,6},{4,0},{6,2},{1,5},{3,7},{5,1},{7,3},{8,12},{10,14},{12... | collective-permute-start | bytes 835592 | tf_op jit(solution)/shard_map/ppermute | solution.py:18
  22.5 10.0 %collective-permute-start.2 = (bf16[64,2176]{1,0:T(8,128)(2,1)S(1)}, bf16[64,2176]{1,0:T(8,128)(2,1)S(1)}, u32[]{:S(2)}, u32[]{:S(2)}) collective-permute-start(bf16[64,2176]{1,0:T(8,128)(2,1)S(1)} %get-tuple-element.39), channel_id=1, source_target_pairs={{0,24},{8,16},{16,8},{24,0},{1,25},{9,17},{17,9},{25,1},{2,26},{10... | collective-permute-start | bytes 835592 | tf_op jit(solution)/shard_map/ppermute | solution.py:18
  25.9 8.5 %collective-permute-start.5 = (bf16[64,2176]{1,0:T(8,128)(2,1)S(1)}, bf16[64,2176]{1,0:T(8,128)(2,1)S(1)}, u32[]{:S(2)}, u32[]{:S(2)}) collective-permute-start(bf16[64,2176]{1,0:T(8,128)(2,1)S(1)} %collective-permute-done.4.refs_0_), channel_id=1, source_target_pairs={{0,4},{2,6},{4,0},{6,2},{1,5},{3,7},{5,1},{7,3},{8,12},{10,14},{12... | collective-permute-start | bytes 835592 | tf_op jit(solution)/shard_map/ppermute | solution.py:18
  26.4 9.5 %collective-permute-start.10 = (bf16[64,2176]{1,0:T(8,128)(2,1)S(1)}, bf16[64,2176]{1,0:T(8,128)(2,1)S(1)}, u32[]{:S(2)}, u32[]{:S(2)}) collective-permute-start(bf16[64,2176]{1,0:T(8,128)(2,1)S(1)} %collective-permute-done.8.refs_0_), channel_id=1, source_target_pairs={{0,2},{2,0},{4,6},{6,4},{1,3},{3,1},{5,7},{7,5},{8,10},{10,8},{12,... | collective-permute-start | bytes 835592 | tf_op jit(solution)/shard_map/ppermute | solution.py:18
  28.9 7.0 %collective-permute-start.11 = (bf16[64,2176]{1,0:T(8,128)(2,1)S(1)}, bf16[64,2176]{1,0:T(8,128)(2,1)S(1)}, u32[]{:S(2)}, u32[]{:S(2)}) collective-permute-start(bf16[64,2176]{1,0:T(8,128)(2,1)S(1)} %collective-permute-done.9.refs_1_), channel_id=1, source_target_pairs={{0,2},{2,0},{4,6},{6,4},{1,3},{3,1},{5,7},{7,5},{8,10},{10,8},{12,... | collective-permute-start | bytes 835592 | tf_op jit(solution)/shard_map/ppermute | solution.py:18
  32.5 6.5 %collective-permute-start.6 = (bf16[64,2176]{1,0:T(8,128)(2,1)S(1)}, bf16[64,2176]{1,0:T(8,128)(2,1)S(1)}, u32[]{:S(2)}, u32[]{:S(2)}) collective-permute-start(bf16[64,2176]{1,0:T(8,128)(2,1)S(1)} %collective-permute-done.4.refs_0_), channel_id=1, source_target_pairs={{0,2},{2,0},{4,6},{6,4},{1,3},{3,1},{5,7},{7,5},{8,10},{10,8},{12,... | collective-permute-start | bytes 835592 | tf_op jit(solution)/shard_map/ppermute | solution.py:18
  34.4 7.6 %collective-permute-start.3 = (bf16[64,2176]{1,0:T(8,128)(2,1)S(1)}, bf16[64,2176]{1,0:T(8,128)(2,1)S(1)}, u32[]{:S(2)}, u32[]{:S(2)}) collective-permute-start(bf16[64,2176]{1,0:T(8,128)(2,1)S(1)} %collective-permute-done.2.refs_0_), channel_id=1, source_target_pairs={{0,4},{2,6},{4,0},{6,2},{1,5},{3,7},{5,1},{7,3},{8,12},{10,14},{12... | collective-permute-start | bytes 835592 | tf_op jit(solution)/shard_map/ppermute | solution.py:18
  35.9 3.2 %collective-permute-start.7 = (bf16[64,2176]{1,0:T(8,128)(2,1)S(1)}, bf16[64,2176]{1,0:T(8,128)(2,1)S(1)}, u32[]{:S(2)}, u32[]{:S(2)}) collective-permute-start(bf16[64,2176]{1,0:T(8,128)(2,1)S(1)} %collective-permute-done.5.refs_1_), channel_id=1, source_target_pairs={{0,2},{2,0},{4,6},{6,4},{1,3},{3,1},{5,7},{7,5},{8,10},{10,8},{12,... | collective-permute-start | bytes 835592 | tf_op jit(solution)/shard_map/ppermute | solution.py:18
  38.4 5.4 %collective-permute-start.14 = (bf16[2,256,512]{2,1,0:T(8,128)(2,1)S(1)}, bf16[2,256,512]{2,1,0:T(8,128)(2,1)S(1)}, u32[]{:S(2)}, u32[]{:S(2)}) collective-permute-start(bf16[2,256,512]{2,1,0:T(8,128)(2,1)S(1)} %shard_map.70), channel_id=1, source_target_pairs={{0,2},{2,0},{4,6},{6,4},{1,3},{3,1},{5,7},{7,5},{8,10},{10,8},{12,... | collective-permute-start | bytes 1572872 | tf_op jit(solution)/shard_map/ppermute | solution.py:18
  39.0 4.9 %collective-permute-start.12 = (bf16[64,2176]{1,0:T(8,128)(2,1)S(1)}, bf16[64,2176]{1,0:T(8,128)(2,1)S(1)}, u32[]{:S(2)}, u32[]{:S(2)}) collective-permute-start(bf16[64,2176]{1,0:T(8,128)(2,1)S(1)} %collective-permute-done.2.refs_0_), channel_id=1, source_target_pairs={{0,2},{2,0},{4,6},{6,4},{1,3},{3,1},{5,7},{7,5},{8,10},{10,8},{12,... | collective-permute-start | bytes 835592 | tf_op jit(solution)/shard_map/ppermute | solution.py:18
  41.9 1.9 %collective-permute-start.13 = (bf16[64,2176]{1,0:T(8,128)(2,1)S(1)}, bf16[64,2176]{1,0:T(8,128)(2,1)S(1)}, u32[]{:S(2)}, u32[]{:S(2)}) collective-permute-start(bf16[64,2176]{1,0:T(8,128)(2,1)S(1)} %collective-permute-done.3.refs_1_), channel_id=1, source_target_pairs={{0,2},{2,0},{4,6},{6,4},{1,3},{3,1},{5,7},{7,5},{8,10},{10,8},{12,... | collective-permute-start | bytes 835592 | tf_op jit(solution)/shard_map/ppermute | solution.py:18
  42.6 6.2 %collective-permute-start.1 = (bf16[2,256,512]{2,1,0:T(8,128)(2,1)S(1)}, bf16[2,256,512]{2,1,0:T(8,128)(2,1)S(1)}, u32[]{:S(2)}, u32[]{:S(2)}) collective-permute-start(bf16[2,256,512]{2,1,0:T(8,128)(2,1)S(1)} %shard_map.66), channel_id=1, source_target_pairs={{0,2},{2,0},{4,6},{6,4},{1,3},{3,1},{5,7},{7,5},{8,10},{10,8},{12,... | collective-permute-start | bytes 1572872 | tf_op jit(solution)/shard_map/ppermute | solution.py:18
  43.8 5.8 %collective-permute-start.21 = (bf16[2,256,512]{2,1,0:T(8,128)(2,1)S(1)}, bf16[2,256,512]{2,1,0:T(8,128)(2,1)S(1)}, u32[]{:S(2)}, u32[]{:S(2)}) collective-permute-start(bf16[2,256,512]{2,1,0:T(8,128)(2,1)S(1)} %shard_map.75), channel_id=1, source_target_pairs={{0,2},{2,0},{4,6},{6,4},{1,3},{3,1},{5,7},{7,5},{8,10},{10,8},{12,... | collective-permute-start | bytes 1572872 | tf_op jit(solution)/shard_map/ppermute | solution.py:18
  46.4 10.7 %collective-permute-start.15 = (bf16[2,256,512]{2,1,0:T(8,128)(2,1)S(1)}, bf16[2,256,512]{2,1,0:T(8,128)(2,1)S(1)}, u32[]{:S(2)}, u32[]{:S(2)}) collective-permute-start(bf16[2,256,512]{2,1,0:T(8,128)(2,1)S(1)} %shard_map.72), channel_id=1, source_target_pairs={{0,2},{2,0},{4,6},{6,4},{1,3},{3,1},{5,7},{7,5},{8,10},{10,8},{12,... | collective-permute-start | bytes 1572872 | tf_op jit(solution)/shard_map/ppermute | solution.py:18
  47.6 8.3 %collective-permute-start.16 = (bf16[1,256,512]{2,1,0:T(8,128)(2,1)S(1)}, bf16[1,256,512]{2,1,0:T(8,128)(2,1)S(1)}, u32[]{:S(2)}, u32[]{:S(2)}) collective-permute-start(bf16[1,256,512]{2,1,0:T(8,128)(2,1)S(1)} %get-tuple-element.55), channel_id=1, source_target_pairs={{0,4},{2,6},{4,0},{6,2},{1,5},{3,7},{5,1},{7,3},{8,12},{10,14},{12... | collective-permute-start | bytes 786440 | tf_op jit(solution)/shard_map/ppermute | solution.py:18
  55.9 9.2 %collective-permute-start.22 = (bf16[1,256,512]{2,1,0:T(8,128)(2,1)S(1)}, bf16[1,256,512]{2,1,0:T(8,128)(2,1)S(1)}, u32[]{:S(2)}, u32[]{:S(2)}) collective-permute-start(bf16[1,256,512]{2,1,0:T(8,128)(2,1)S(1)} %get-tuple-element.62), channel_id=1, source_target_pairs={{0,4},{2,6},{4,0},{6,2},{1,5},{3,7},{5,1},{7,3},{8,12},{10,14},{12... | collective-permute-start | bytes 786440 | tf_op jit(solution)/shard_map/ppermute | solution.py:18
  57.8 11.9 %collective-permute-start.17 = (bf16[1,256,512]{2,1,0:T(8,128)(2,1)S(1)}, bf16[1,256,512]{2,1,0:T(8,128)(2,1)S(1)}, u32[]{:S(2)}, u32[]{:S(2)}) collective-permute-start(bf16[1,256,512]{2,1,0:T(8,128)(2,1)S(1)} %get-tuple-element.56), channel_id=1, source_target_pairs={{0,4},{2,6},{4,0},{6,2},{1,5},{3,7},{5,1},{7,3},{8,12},{10,14},{12... | collective-permute-start | bytes 786440 | tf_op jit(solution)/shard_map/ppermute | solution.py:18
  58.8 16.5 %collective-permute-start.19 = (bf16[256,512]{1,0:T(8,128)(2,1)S(1)}, bf16[256,512]{1,0:T(8,128)(2,1)S(1)}, u32[]{:S(2)}, u32[]{:S(2)}) collective-permute-start(bf16[256,512]{1,0:T(8,128)(2,1)S(1)} %fusion), channel_id=1, source_target_pairs={{0,16},{8,24},{16,0},{24,8},{1,17},{9,25},{17,1},{25,9},{2,18},{10... | collective-permute-start | bytes 786440 | tf_op jit(solution)/shard_map/ppermute | solution.py:18
  65.2 12.2 %collective-permute-start.23 = (bf16[256,512]{1,0:T(8,128)(2,1)S(1)}, bf16[256,512]{1,0:T(8,128)(2,1)S(1)}, u32[]{:S(2)}, u32[]{:S(2)}) collective-permute-start(bf16[256,512]{1,0:T(8,128)(2,1)S(1)} %fusion.2), channel_id=1, source_target_pairs={{0,8},{8,0},{16,24},{24,16},{1,9},{9,1},{17,25},{25,17},{2,10},{10... | collective-permute-start | bytes 786440 | tf_op jit(solution)/shard_map/ppermute | solution.py:18
  69.7 7.7 %collective-permute-start.18 = (bf16[1,256,512]{2,1,0:T(8,128)(2,1)S(1)}, bf16[1,256,512]{2,1,0:T(8,128)(2,1)S(1)}, u32[]{:S(2)}, u32[]{:S(2)}) collective-permute-start(bf16[1,256,512]{2,1,0:T(8,128)(2,1)S(1)} %get-tuple-element.57), channel_id=1, source_target_pairs={{0,4},{2,6},{4,0},{6,2},{1,5},{3,7},{5,1},{7,3},{8,12},{10,14},{12... | collective-permute-start | bytes 786440 | tf_op jit(solution)/shard_map/ppermute | solution.py:18
  70.3 11.6 %collective-permute-start.20 = (bf16[256,512]{1,0:T(8,128)(2,1)S(1)}, bf16[256,512]{1,0:T(8,128)(2,1)S(1)}, u32[]{:S(2)}, u32[]{:S(2)}) collective-permute-start(bf16[256,512]{1,0:T(8,128)(2,1)S(1)} %fusion.1), channel_id=1, source_target_pairs={{0,24},{8,16},{16,8},{24,0},{1,25},{9,17},{17,9},{25,1},{2,26},{10... | collective-permute-start | bytes 786440 | tf_op jit(solution)/shard_map/ppermute | solution.py:18

commit v7 on v6

--- a/solution.py
+++ b/solution.py
@@ -259,7 +259,7 @@
         stayed[s] = stay(*hidden[s], left[s])
     for n, s in enumerate(turns):
         keep, message = stayed[s]
-        if n > 0:
+        if n > 1:
             message = after(message, sums[turns[max(n - 2, 0)]][1])
         sums[s] = keep, arrived = across(keep, message)
         if s > 0:

time: 84.4 us -> 84.4 us (level)
  no operation moved by 1% of the time
where the time goes in v7:
time: 84.4 us; the launch traced here: 82.7 us
  starting transfers between devices  33.4 us (40%)
  waiting for transfers between devices  28.6 us (34%)
  Pallas kernels  14 us (17%)
  local copies, waits for them, and re-layouts  5.01 us (6%)
  other arithmetic  1.61 us (2%)
    ppermute x24, starting transfers between devices, swap_bit(): return lax.ppermute(value, axis, [(i, i ^ bit) for i in range(size)])  33.4 us
    ppermute x24, waiting for transfers between devices, swap_bit(): return lax.ppermute(value, axis, [(i, i ^ bit) for i in range(size)])  28.6 us
    pallas_call x14, Pallas kernels, call(): pl.pallas_call(kernel, out_shape=outs, in_specs=in_specs or [VM] * len(ar...  14 us
    unnamed x12, local copies, waits for them, and re-layouts  5.01 us
  transfers between devices with their start and end apart: 24, of which 9 were waited for; matrix products, arithmetic and copies ran while one was open for 2% of the time, Pallas kernels for 16%

profile of v7, /device:TPU:0, one launch (start us, length us, event | category | flops | bytes accessed | tf_op | source)
XLA Modules:
  0.0 82.7 jit_solution(12185278780618356454)
XLA Ops:
  0.0 2.9 %collective-permute-start = (bf16[768,1024]{1,0:T(8,128)(2,1)}, bf16[768,1024]{1,0:T(8,128)(2,1)S(1)}, u32[]{:S(2)}, u32[]{:S(2)}) collective-permute-start(bf16[768,1024]{1,0:T(8,128)(2,1)} %bitcast.15), channel_id=1, source_target_pairs={{0,1},{1,0},{2,3},{3,2},{4,5},{5,4},{6,7},{7,6},{8,9},{9,8},{10,11... | collective-permute-start | bytes 4718600 | tf_op jit(solution)/shard_map/ppermute | solution.py:18
  3.6 0.7 convert_bitcast_fusion.1
  4.3 1.2 %copy-done.5 = bf16[256,2048]{1,0:T(8,128)(2,1)S(1)} copy-done((bf16[256,2048]{1,0:T(8,128)(2,1)S(1)}, bf16[256,2048]{1,0:T(8,128)(2,1)}, u32[]{:S(2)}) %copy-start.5) | copy-done | bytes 1048600
  5.8 2.7 %collective-permute-start.8 = (bf16[64,2176]{1,0:T(8,128)(2,1)S(1)}, bf16[64,2176]{1,0:T(8,128)(2,1)S(1)}, u32[]{:S(2)}, u32[]{:S(2)}) collective-permute-start(bf16[64,2176]{1,0:T(8,128)(2,1)S(1)} %get-tuple-element.38), channel_id=1, source_target_pairs={{0,16},{8,24},{16,0},{24,8},{1,17},{9,25},{17,1},{25,9},{2,18},{10... | collective-permute-start | bytes 835592 | tf_op jit(solution)/shard_map/ppermute | solution.py:18
  8.4 1.6 %collective-permute-start.4 = (bf16[64,2176]{1,0:T(8,128)(2,1)S(1)}, bf16[64,2176]{1,0:T(8,128)(2,1)S(1)}, u32[]{:S(2)}, u32[]{:S(2)}) collective-permute-start(bf16[64,2176]{1,0:T(8,128)(2,1)S(1)} %get-tuple-element.38), channel_id=1, source_target_pairs={{0,8},{8,0},{16,24},{24,16},{1,9},{9,1},{17,25},{25,17},{2,10},{10... | collective-permute-start | bytes 835592 | tf_op jit(solution)/shard_map/ppermute | solution.py:18
  10.0 1.9 %copy-done.1 = bf16[1,2048,768]{2,1,0:T(8,128)(2,1)S(1)} copy-done((bf16[1,2048,768]{2,1,0:T(8,128)(2,1)S(1)}, bf16[1,2048,768]{2,1,0:T(8,128)(2,1)}, u32[]{:S(2)}) %copy-start.1) | copy-done | bytes 3145752
  11.9 1.9 %copy-done.3 = bf16[1,2048,768]{2,1,0:T(8,128)(2,1)S(1)} copy-done((bf16[1,2048,768]{2,1,0:T(8,128)(2,1)S(1)}, bf16[1,2048,768]{2,1,0:T(8,128)(2,1)}, u32[]{:S(2)}) %copy-start.3) | copy-done | bytes 3145752
  13.8 2.0 %shard_map.65 = (bf16[256,768]{1,0:T(8,128)(2,1)S(1)}, f32[256,128]{1,0:T(8,128)S(1)}) custom-call(bf16[256,2048]{1,0:T(8,128)(2,1)S(1)} %copy-done.5, bf16[256,128]{1,0:T(8,128)(2,1)S(1)} %get-tuple-element.33.refs_1_, bf16[2048,768]{1,0:T(8,128)(2,1)S(1)} %bitcast.24, bf16[2048,768]{1,0:T(8,128)(2,1)S(1)} %bitcast.28), custom_call_target="tpu_custom_call" | custom-call | flops 1610612736 | bytes 7929856 | tf_op jit(solution)/shard_map/pallas_call | solution.py:39
  15.8 5.1 %collective-permute-done.8.refs_0_ = bf16[64,2176]{1,0:T(8,128)(2,1)S(1)} collective-permute-done((bf16[64,2176]{1,0:T(8,128)(2,1)S(1)}, bf16[64,2176]{1,0:T(8,128)(2,1)S(1)}, u32[]{:S(2)}, u32[]{:S(2)}) %collective-permute-start.8) | collective-permute-done | bytes 278560 | tf_op jit(solution)/shard_map/ppermute | solution.py:18
  20.9 1.5 %collective-permute-start.9 = (bf16[64,2176]{1,0:T(8,128)(2,1)S(1)}, bf16[64,2176]{1,0:T(8,128)(2,1)S(1)}, u32[]{:S(2)}, u32[]{:S(2)}) collective-permute-start(bf16[64,2176]{1,0:T(8,128)(2,1)S(1)} %collective-permute-done.8.refs_0_), channel_id=1, source_target_pairs={{0,4},{2,6},{4,0},{6,2},{1,5},{3,7},{5,1},{7,3},{8,12},{10,14},{12... | collective-permute-start | bytes 835592 | tf_op jit(solution)/shard_map/ppermute | solution.py:18
  22.5 3.4 %collective-permute-start.2 = (bf16[64,2176]{1,0:T(8,128)(2,1)S(1)}, bf16[64,2176]{1,0:T(8,128)(2,1)S(1)}, u32[]{:S(2)}, u32[]{:S(2)}) collective-permute-start(bf16[64,2176]{1,0:T(8,128)(2,1)S(1)} %get-tuple-element.38), channel_id=1, source_target_pairs={{0,24},{8,16},{16,8},{24,0},{1,25},{9,17},{17,9},{25,1},{2,26},{10... | collective-permute-start | bytes 835592 | tf_op jit(solution)/shard_map/ppermute | solution.py:18
  26.4 2.5 %collective-permute-done.9.refs_1_ = bf16[64,2176]{1,0:T(8,128)(2,1)S(1)} collective-permute-done((bf16[64,2176]{1,0:T(8,128)(2,1)S(1)}, bf16[64,2176]{1,0:T(8,128)(2,1)S(1)}, u32[]{:S(2)}, u32[]{:S(2)}) %collective-permute-start.9) | collective-permute-done | bytes 278560 | tf_op jit(solution)/shard_map/ppermute | solution.py:18
  28.9 3.6 %collective-permute-done.2.refs_0_ = bf16[64,2176]{1,0:T(8,128)(2,1)S(1)} collective-permute-done((bf16[64,2176]{1,0:T(8,128)(2,1)S(1)}, bf16[64,2176]{1,0:T(8,128)(2,1)S(1)}, u32[]{:S(2)}, u32[]{:S(2)}) %collective-permute-start.2) | collective-permute-done | bytes 278560 | tf_op jit(solution)/shard_map/ppermute | solution.py:18
  32.5 1.8 %collective-permute-done.5.refs_1_ = bf16[64,2176]{1,0:T(8,128)(2,1)S(1)} collective-permute-done((bf16[64,2176]{1,0:T(8,128)(2,1)S(1)}, bf16[64,2176]{1,0:T(8,128)(2,1)S(1)}, u32[]{:S(2)}, u32[]{:S(2)}) %collective-permute-start.5) | collective-permute-done | bytes 278560 | tf_op jit(solution)/shard_map/ppermute | solution.py:18
  34.4 1.5 %collective-permute-start.3 = (bf16[64,2176]{1,0:T(8,128)(2,1)S(1)}, bf16[64,2176]{1,0:T(8,128)(2,1)S(1)}, u32[]{:S(2)}, u32[]{:S(2)}) collective-permute-start(bf16[64,2176]{1,0:T(8,128)(2,1)S(1)} %collective-permute-done.2.refs_0_), channel_id=1, source_target_pairs={{0,4},{2,6},{4,0},{6,2},{1,5},{3,7},{5,1},{7,3},{8,12},{10,14},{12... | collective-permute-start | bytes 835592 | tf_op jit(solution)/shard_map/ppermute | solution.py:18
  35.9 1.9 %shard_map.69 = (bf16[256,768]{1,0:T(8,128)(2,1)S(1)}, f32[256,128]{1,0:T(8,128)S(1)}) custom-call(bf16[64,2176]{1,0:T(8,128)(2,1)S(1)} %collective-permute-done.8.refs_0_, bf16[64,2176]{1,0:T(8,128)(2,1)S(1)} %collective-permute-done.9.refs_1_, bf16[64,2176]{1,0:T(8,128)(2,1)S(1)} %collective-permute-done.10.refs_2_, ...), custom_call_target="tpu_custom_call" | custom-call | flops 1610612736 | bytes 7929856 | tf_op jit(solution)/shard_map/pallas_call | solution.py:39
  39.1 1.9 %shard_map.68 = (bf16[256,768]{1,0:T(8,128)(2,1)S(1)}, f32[256,128]{1,0:T(8,128)S(1)}) custom-call(bf16[64,2176]{1,0:T(8,128)(2,1)S(1)} %collective-permute-done.4.refs_0_, bf16[64,2176]{1,0:T(8,128)(2,1)S(1)} %collective-permute-done.5.refs_1_, bf16[64,2176]{1,0:T(8,128)(2,1)S(1)} %collective-permute-done.6.refs_2_, ...), custom_call_target="tpu_custom_call" | custom-call | flops 1610612736 | bytes 7929856 | tf_op jit(solution)/shard_map/pallas_call | solution.py:39
  40.9 1.0 %collective-permute-done.3.refs_1_ = bf16[64,2176]{1,0:T(8,128)(2,1)S(1)} collective-permute-done((bf16[64,2176]{1,0:T(8,128)(2,1)S(1)}, bf16[64,2176]{1,0:T(8,128)(2,1)S(1)}, u32[]{:S(2)}, u32[]{:S(2)}) %collective-permute-start.3) | collective-permute-done | bytes 278560 | tf_op jit(solution)/shard_map/ppermute | solution.py:18
  43.9 1.9 %shard_map.71 = (bf16[256,768]{1,0:T(8,128)(2,1)S(1)}, f32[256,128]{1,0:T(8,128)S(1)}) custom-call(bf16[64,2176]{1,0:T(8,128)(2,1)S(1)} %collective-permute-done.2.refs_0_, bf16[64,2176]{1,0:T(8,128)(2,1)S(1)} %collective-permute-done.3.refs_1_, bf16[64,2176]{1,0:T(8,128)(2,1)S(1)} %collective-permute-done.12.refs_2_, ...), custom_call_target="tpu_custom_call" | custom-call | flops 1610612736 | bytes 7929856 | tf_op jit(solution)/shard_map/pallas_call | solution.py:39
  47.6 1.2 %collective-permute-start.18 = (bf16[1,256,512]{2,1,0:T(8,128)(2,1)S(1)}, bf16[1,256,512]{2,1,0:T(8,128)(2,1)S(1)}, u32[]{:S(2)}, u32[]{:S(2)}) collective-permute-start(bf16[1,256,512]{2,1,0:T(8,128)(2,1)S(1)} %get-tuple-element.56), channel_id=1, source_target_pairs={{0,4},{2,6},{4,0},{6,2},{1,5},{3,7},{5,1},{7,3},{8,12},{10,14},{12... | collective-permute-start | bytes 786440 | tf_op jit(solution)/shard_map/ppermute | solution.py:18
  48.8 0.7 shard_map.67
  49.5 0.7 shard_map.76
  50.3 5.7 %collective-permute-done.18 = bf16[1,256,512]{2,1,0:T(8,128)(2,1)S(1)} collective-permute-done((bf16[1,256,512]{2,1,0:T(8,128)(2,1)S(1)}, bf16[1,256,512]{2,1,0:T(8,128)(2,1)S(1)}, u32[]{:S(2)}, u32[]{:S(2)}) %collective-permute-start.18) | collective-permute-done | bytes 262176 | tf_op jit(solution)/shard_map/ppermute | solution.py:18
  55.9 1.2 %collective-permute-start.22 = (bf16[1,256,512]{2,1,0:T(8,128)(2,1)S(1)}, bf16[1,256,512]{2,1,0:T(8,128)(2,1)S(1)}, u32[]{:S(2)}, u32[]{:S(2)}) collective-permute-start(bf16[1,256,512]{2,1,0:T(8,128)(2,1)S(1)} %get-tuple-element.60), channel_id=1, source_target_pairs={{0,4},{2,6},{4,0},{6,2},{1,5},{3,7},{5,1},{7,3},{8,12},{10,14},{12... | collective-permute-start | bytes 786440 | tf_op jit(solution)/shard_map/ppermute | solution.py:18
  57.8 0.9 %collective-permute-start.16 = (bf16[1,256,512]{2,1,0:T(8,128)(2,1)S(1)}, bf16[1,256,512]{2,1,0:T(8,128)(2,1)S(1)}, u32[]{:S(2)}, u32[]{:S(2)}) collective-permute-start(bf16[1,256,512]{2,1,0:T(8,128)(2,1)S(1)} %get-tuple-element.53), channel_id=1, source_target_pairs={{0,4},{2,6},{4,0},{6,2},{1,5},{3,7},{5,1},{7,3},{8,12},{10,14},{12... | collective-permute-start | bytes 786440 | tf_op jit(solution)/shard_map/ppermute | solution.py:18
  58.8 4.2 %collective-permute-start.19 = (bf16[256,512]{1,0:T(8,128)(2,1)S(1)}, bf16[256,512]{1,0:T(8,128)(2,1)S(1)}, u32[]{:S(2)}, u32[]{:S(2)}) collective-permute-start(bf16[256,512]{1,0:T(8,128)(2,1)S(1)} %fusion), channel_id=1, source_target_pairs={{0,16},{8,24},{16,0},{24,8},{1,17},{9,25},{17,1},{25,9},{2,18},{10... | collective-permute-start | bytes 786440 | tf_op jit(solution)/shard_map/ppermute | solution.py:18
  63.0 2.2 %collective-permute-done.22 = bf16[1,256,512]{2,1,0:T(8,128)(2,1)S(1)} collective-permute-done((bf16[1,256,512]{2,1,0:T(8,128)(2,1)S(1)}, bf16[1,256,512]{2,1,0:T(8,128)(2,1)S(1)}, u32[]{:S(2)}, u32[]{:S(2)}) %collective-permute-start.22) | collective-permute-done | bytes 262176 | tf_op jit(solution)/shard_map/ppermute | solution.py:18
  65.2 4.5 %collective-permute-start.23 = (bf16[256,512]{1,0:T(8,128)(2,1)S(1)}, bf16[256,512]{1,0:T(8,128)(2,1)S(1)}, u32[]{:S(2)}, u32[]{:S(2)}) collective-permute-start(bf16[256,512]{1,0:T(8,128)(2,1)S(1)} %fusion.2), channel_id=1, source_target_pairs={{0,8},{8,0},{16,24},{24,16},{1,9},{9,1},{17,25},{25,17},{2,10},{10... | collective-permute-start | bytes 786440 | tf_op jit(solution)/shard_map/ppermute | solution.py:18
  70.3 5.0 %collective-permute-start.20 = (bf16[256,512]{1,0:T(8,128)(2,1)S(1)}, bf16[256,512]{1,0:T(8,128)(2,1)S(1)}, u32[]{:S(2)}, u32[]{:S(2)}) collective-permute-start(bf16[256,512]{1,0:T(8,128)(2,1)S(1)} %fusion.1), channel_id=1, source_target_pairs={{0,24},{8,16},{16,8},{24,0},{1,25},{9,17},{17,9},{25,1},{2,26},{10... | collective-permute-start | bytes 786440 | tf_op jit(solution)/shard_map/ppermute | solution.py:18
  75.3 2.2 %collective-permute-done.23.refs_2_ = bf16[256,512]{1,0:T(8,128)(2,1)S(1)} collective-permute-done((bf16[256,512]{1,0:T(8,128)(2,1)S(1)}, bf16[256,512]{1,0:T(8,128)(2,1)S(1)}, u32[]{:S(2)}, u32[]{:S(2)}) %collective-permute-start.23) | collective-permute-done | bytes 262176 | tf_op jit(solution)/shard_map/ppermute | solution.py:18
  77.5 4.4 %collective-permute-done.20.refs_1_ = bf16[256,512]{1,0:T(8,128)(2,1)S(1)} collective-permute-done((bf16[256,512]{1,0:T(8,128)(2,1)S(1)}, bf16[256,512]{1,0:T(8,128)(2,1)S(1)}, u32[]{:S(2)}, u32[]{:S(2)}) %collective-permute-start.20) | collective-permute-done | bytes 262176 | tf_op jit(solution)/shard_map/ppermute | solution.py:18
  81.9 0.9 %shard_map.77 = bf16[256,512]{1,0:T(8,128)(2,1)} custom-call(f32[256,512]{1,0:T(8,128)S(1)} %bitcast.32, bf16[256,512]{1,0:T(8,128)(2,1)S(1)} %bitcast.33, bf16[256,512]{1,0:T(8,128)(2,1)S(1)} %collective-permute-done.19.refs_0_, bf16[256,512]{1,0:T(8,128)(2,1)S(1)} %collective-permute-done.20.refs_1_, bf16[256,512]{1,0:T(8,128)(2,1)S(1)} %collective-permute-done.23.refs_2_), custom_call_target="tpu_custom_call" | custom-call | tf_op jit(solution)/shard_map/pallas_call | solution.py:39
  (48 shorter events, 7.9 us)
Async XLA Ops:
  0.0 37.8 %collective-permute-start = (bf16[768,1024]{1,0:T(8,128)(2,1)}, bf16[768,1024]{1,0:T(8,128)(2,1)S(1)}, u32[]{:S(2)}, u32[]{:S(2)}) collective-permute-start(bf16[768,1024]{1,0:T(8,128)(2,1)} %bitcast.15), channel_id=1, source_target_pairs={{0,1},{1,0},{2,3},{3,2},{4,5},{5,4},{6,7},{7,6},{8,9},{9,8},{10,11... | collective-permute-start | bytes 4718600 | tf_op jit(solution)/shard_map/ppermute | solution.py:18
  4.3 1.2 %copy-start.5 = (bf16[256,2048]{1,0:T(8,128)(2,1)S(1)}, bf16[256,2048]{1,0:T(8,128)(2,1)}, u32[]{:S(2)}) copy-start(bf16[256,2048]{1,0:T(8,128)(2,1)} %refs_0_.1) | copy-start | bytes 3145732
  5.8 15.2 %collective-permute-start.8 = (bf16[64,2176]{1,0:T(8,128)(2,1)S(1)}, bf16[64,2176]{1,0:T(8,128)(2,1)S(1)}, u32[]{:S(2)}, u32[]{:S(2)}) collective-permute-start(bf16[64,2176]{1,0:T(8,128)(2,1)S(1)} %get-tuple-element.38), channel_id=1, source_target_pairs={{0,16},{8,24},{16,0},{24,8},{1,17},{9,25},{17,1},{25,9},{2,18},{10... | collective-permute-start | bytes 835592 | tf_op jit(solution)/shard_map/ppermute | solution.py:18
  8.4 17.4 %collective-permute-start.4 = (bf16[64,2176]{1,0:T(8,128)(2,1)S(1)}, bf16[64,2176]{1,0:T(8,128)(2,1)S(1)}, u32[]{:S(2)}, u32[]{:S(2)}) collective-permute-start(bf16[64,2176]{1,0:T(8,128)(2,1)S(1)} %get-tuple-element.38), channel_id=1, source_target_pairs={{0,8},{8,0},{16,24},{24,16},{1,9},{9,1},{17,25},{25,17},{2,10},{10... | collective-permute-start | bytes 835592 | tf_op jit(solution)/shard_map/ppermute | solution.py:18
  10.0 1.9 %copy-start.1 = (bf16[1,2048,768]{2,1,0:T(8,128)(2,1)S(1)}, bf16[1,2048,768]{2,1,0:T(8,128)(2,1)}, u32[]{:S(2)}) copy-start(bf16[1,2048,768]{2,1,0:T(8,128)(2,1)} %param.9) | copy-start | bytes 9437188
  11.9 1.9 %copy-start.3 = (bf16[1,2048,768]{2,1,0:T(8,128)(2,1)S(1)}, bf16[1,2048,768]{2,1,0:T(8,128)(2,1)}, u32[]{:S(2)}) copy-start(bf16[1,2048,768]{2,1,0:T(8,128)(2,1)} %param.10) | copy-start | bytes 9437188
  13.8 22.1 %copy-start.2 = (bf16[1,2048,768]{2,1,0:T(8,128)(2,1)S(1)}, bf16[1,2048,768]{2,1,0:T(8,128)(2,1)}, u32[]{:S(2)}) copy-start(bf16[1,2048,768]{2,1,0:T(8,128)(2,1)} %param.9) | copy-start | bytes 9437188
  13.8 22.1 %copy-start.4 = (bf16[1,2048,768]{2,1,0:T(8,128)(2,1)S(1)}, bf16[1,2048,768]{2,1,0:T(8,128)(2,1)}, u32[]{:S(2)}) copy-start(bf16[1,2048,768]{2,1,0:T(8,128)(2,1)} %param.10) | copy-start | bytes 9437188
  20.9 16.9 %copy-start = (bf16[1,768,1024]{2,1,0:T(8,128)(2,1)S(1)}, bf16[1,768,1024]{2,1,0:T(8,128)(2,1)}, u32[]{:S(2)}) copy-start(bf16[1,768,1024]{2,1,0:T(8,128)(2,1)} %param.11) | copy-start | bytes 4718596
  20.9 7.9 %collective-permute-start.9 = (bf16[64,2176]{1,0:T(8,128)(2,1)S(1)}, bf16[64,2176]{1,0:T(8,128)(2,1)S(1)}, u32[]{:S(2)}, u32[]{:S(2)}) collective-permute-start(bf16[64,2176]{1,0:T(8,128)(2,1)S(1)} %collective-permute-done.8.refs_0_), channel_id=1, source_target_pairs={{0,4},{2,6},{4,0},{6,2},{1,5},{3,7},{5,1},{7,3},{8,12},{10,14},{12... | collective-permute-start | bytes 835592 | tf_op jit(solution)/shard_map/ppermute | solution.py:18
  22.5 10.0 %collective-permute-start.2 = (bf16[64,2176]{1,0:T(8,128)(2,1)S(1)}, bf16[64,2176]{1,0:T(8,128)(2,1)S(1)}, u32[]{:S(2)}, u32[]{:S(2)}) collective-permute-start(bf16[64,2176]{1,0:T(8,128)(2,1)S(1)} %get-tuple-element.38), channel_id=1, source_target_pairs={{0,24},{8,16},{16,8},{24,0},{1,25},{9,17},{17,9},{25,1},{2,26},{10... | collective-permute-start | bytes 835592 | tf_op jit(solution)/shard_map/ppermute | solution.py:18
  25.9 8.5 %collective-permute-start.5 = (bf16[64,2176]{1,0:T(8,128)(2,1)S(1)}, bf16[64,2176]{1,0:T(8,128)(2,1)S(1)}, u32[]{:S(2)}, u32[]{:S(2)}) collective-permute-start(bf16[64,2176]{1,0:T(8,128)(2,1)S(1)} %collective-permute-done.4.refs_0_), channel_id=1, source_target_pairs={{0,4},{2,6},{4,0},{6,2},{1,5},{3,7},{5,1},{7,3},{8,12},{10,14},{12... | collective-permute-start | bytes 835592 | tf_op jit(solution)/shard_map/ppermute | solution.py:18
  26.4 9.5 %collective-permute-start.10 = (bf16[64,2176]{1,0:T(8,128)(2,1)S(1)}, bf16[64,2176]{1,0:T(8,128)(2,1)S(1)}, u32[]{:S(2)}, u32[]{:S(2)}) collective-permute-start(bf16[64,2176]{1,0:T(8,128)(2,1)S(1)} %collective-permute-done.8.refs_0_), channel_id=1, source_target_pairs={{0,2},{2,0},{4,6},{6,4},{1,3},{3,1},{5,7},{7,5},{8,10},{10,8},{12,... | collective-permute-start | bytes 835592 | tf_op jit(solution)/shard_map/ppermute | solution.py:18
  28.9 7.0 %collective-permute-start.11 = (bf16[64,2176]{1,0:T(8,128)(2,1)S(1)}, bf16[64,2176]{1,0:T(8,128)(2,1)S(1)}, u32[]{:S(2)}, u32[]{:S(2)}) collective-permute-start(bf16[64,2176]{1,0:T(8,128)(2,1)S(1)} %collective-permute-done.9.refs_1_), channel_id=1, source_target_pairs={{0,2},{2,0},{4,6},{6,4},{1,3},{3,1},{5,7},{7,5},{8,10},{10,8},{12,... | collective-permute-start | bytes 835592 | tf_op jit(solution)/shard_map/ppermute | solution.py:18
  32.5 6.5 %collective-permute-start.6 = (bf16[64,2176]{1,0:T(8,128)(2,1)S(1)}, bf16[64,2176]{1,0:T(8,128)(2,1)S(1)}, u32[]{:S(2)}, u32[]{:S(2)}) collective-permute-start(bf16[64,2176]{1,0:T(8,128)(2,1)S(1)} %collective-permute-done.4.refs_0_), channel_id=1, source_target_pairs={{0,2},{2,0},{4,6},{6,4},{1,3},{3,1},{5,7},{7,5},{8,10},{10,8},{12,... | collective-permute-start | bytes 835592 | tf_op jit(solution)/shard_map/ppermute | solution.py:18
  34.4 7.6 %collective-permute-start.3 = (bf16[64,2176]{1,0:T(8,128)(2,1)S(1)}, bf16[64,2176]{1,0:T(8,128)(2,1)S(1)}, u32[]{:S(2)}, u32[]{:S(2)}) collective-permute-start(bf16[64,2176]{1,0:T(8,128)(2,1)S(1)} %collective-permute-done.2.refs_0_), channel_id=1, source_target_pairs={{0,4},{2,6},{4,0},{6,2},{1,5},{3,7},{5,1},{7,3},{8,12},{10,14},{12... | collective-permute-start | bytes 835592 | tf_op jit(solution)/shard_map/ppermute | solution.py:18
  35.9 3.2 %collective-permute-start.7 = (bf16[64,2176]{1,0:T(8,128)(2,1)S(1)}, bf16[64,2176]{1,0:T(8,128)(2,1)S(1)}, u32[]{:S(2)}, u32[]{:S(2)}) collective-permute-start(bf16[64,2176]{1,0:T(8,128)(2,1)S(1)} %collective-permute-done.5.refs_1_), channel_id=1, source_target_pairs={{0,2},{2,0},{4,6},{6,4},{1,3},{3,1},{5,7},{7,5},{8,10},{10,8},{12,... | collective-permute-start | bytes 835592 | tf_op jit(solution)/shard_map/ppermute | solution.py:18
  38.4 5.4 %collective-permute-start.14 = (bf16[2,256,512]{2,1,0:T(8,128)(2,1)S(1)}, bf16[2,256,512]{2,1,0:T(8,128)(2,1)S(1)}, u32[]{:S(2)}, u32[]{:S(2)}) collective-permute-start(bf16[2,256,512]{2,1,0:T(8,128)(2,1)S(1)} %shard_map.70), channel_id=1, source_target_pairs={{0,2},{2,0},{4,6},{6,4},{1,3},{3,1},{5,7},{7,5},{8,10},{10,8},{12,... | collective-permute-start | bytes 1572872 | tf_op jit(solution)/shard_map/ppermute | solution.py:18
  39.0 4.9 %collective-permute-start.12 = (bf16[64,2176]{1,0:T(8,128)(2,1)S(1)}, bf16[64,2176]{1,0:T(8,128)(2,1)S(1)}, u32[]{:S(2)}, u32[]{:S(2)}) collective-permute-start(bf16[64,2176]{1,0:T(8,128)(2,1)S(1)} %collective-permute-done.2.refs_0_), channel_id=1, source_target_pairs={{0,2},{2,0},{4,6},{6,4},{1,3},{3,1},{5,7},{7,5},{8,10},{10,8},{12,... | collective-permute-start | bytes 835592 | tf_op jit(solution)/shard_map/ppermute | solution.py:18
  41.9 1.9 %collective-permute-start.13 = (bf16[64,2176]{1,0:T(8,128)(2,1)S(1)}, bf16[64,2176]{1,0:T(8,128)(2,1)S(1)}, u32[]{:S(2)}, u32[]{:S(2)}) collective-permute-start(bf16[64,2176]{1,0:T(8,128)(2,1)S(1)} %collective-permute-done.3.refs_1_), channel_id=1, source_target_pairs={{0,2},{2,0},{4,6},{6,4},{1,3},{3,1},{5,7},{7,5},{8,10},{10,8},{12,... | collective-permute-start | bytes 835592 | tf_op jit(solution)/shard_map/ppermute | solution.py:18
  42.6 6.2 %collective-permute-start.1 = (bf16[2,256,512]{2,1,0:T(8,128)(2,1)S(1)}, bf16[2,256,512]{2,1,0:T(8,128)(2,1)S(1)}, u32[]{:S(2)}, u32[]{:S(2)}) collective-permute-start(bf16[2,256,512]{2,1,0:T(8,128)(2,1)S(1)} %shard_map.66), channel_id=1, source_target_pairs={{0,2},{2,0},{4,6},{6,4},{1,3},{3,1},{5,7},{7,5},{8,10},{10,8},{12,... | collective-permute-start | bytes 1572872 | tf_op jit(solution)/shard_map/ppermute | solution.py:18
  43.8 5.8 %collective-permute-start.21 = (bf16[2,256,512]{2,1,0:T(8,128)(2,1)S(1)}, bf16[2,256,512]{2,1,0:T(8,128)(2,1)S(1)}, u32[]{:S(2)}, u32[]{:S(2)}) collective-permute-start(bf16[2,256,512]{2,1,0:T(8,128)(2,1)S(1)} %shard_map.75), channel_id=1, source_target_pairs={{0,2},{2,0},{4,6},{6,4},{1,3},{3,1},{5,7},{7,5},{8,10},{10,8},{12,... | collective-permute-start | bytes 1572872 | tf_op jit(solution)/shard_map/ppermute | solution.py:18
  46.4 10.7 %collective-permute-start.15 = (bf16[2,256,512]{2,1,0:T(8,128)(2,1)S(1)}, bf16[2,256,512]{2,1,0:T(8,128)(2,1)S(1)}, u32[]{:S(2)}, u32[]{:S(2)}) collective-permute-start(bf16[2,256,512]{2,1,0:T(8,128)(2,1)S(1)} %shard_map.72), channel_id=1, source_target_pairs={{0,2},{2,0},{4,6},{6,4},{1,3},{3,1},{5,7},{7,5},{8,10},{10,8},{12,... | collective-permute-start | bytes 1572872 | tf_op jit(solution)/shard_map/ppermute | solution.py:18
  47.6 8.3 %collective-permute-start.18 = (bf16[1,256,512]{2,1,0:T(8,128)(2,1)S(1)}, bf16[1,256,512]{2,1,0:T(8,128)(2,1)S(1)}, u32[]{:S(2)}, u32[]{:S(2)}) collective-permute-start(bf16[1,256,512]{2,1,0:T(8,128)(2,1)S(1)} %get-tuple-element.56), channel_id=1, source_target_pairs={{0,4},{2,6},{4,0},{6,2},{1,5},{3,7},{5,1},{7,3},{8,12},{10,14},{12... | collective-permute-start | bytes 786440 | tf_op jit(solution)/shard_map/ppermute | solution.py:18
  55.9 9.2 %collective-permute-start.22 = (bf16[1,256,512]{2,1,0:T(8,128)(2,1)S(1)}, bf16[1,256,512]{2,1,0:T(8,128)(2,1)S(1)}, u32[]{:S(2)}, u32[]{:S(2)}) collective-permute-start(bf16[1,256,512]{2,1,0:T(8,128)(2,1)S(1)} %get-tuple-element.60), channel_id=1, source_target_pairs={{0,4},{2,6},{4,0},{6,2},{1,5},{3,7},{5,1},{7,3},{8,12},{10,14},{12... | collective-permute-start | bytes 786440 | tf_op jit(solution)/shard_map/ppermute | solution.py:18
  57.8 11.9 %collective-permute-start.16 = (bf16[1,256,512]{2,1,0:T(8,128)(2,1)S(1)}, bf16[1,256,512]{2,1,0:T(8,128)(2,1)S(1)}, u32[]{:S(2)}, u32[]{:S(2)}) collective-permute-start(bf16[1,256,512]{2,1,0:T(8,128)(2,1)S(1)} %get-tuple-element.53), channel_id=1, source_target_pairs={{0,4},{2,6},{4,0},{6,2},{1,5},{3,7},{5,1},{7,3},{8,12},{10,14},{12... | collective-permute-start | bytes 786440 | tf_op jit(solution)/shard_map/ppermute | solution.py:18
  58.8 16.5 %collective-permute-start.19 = (bf16[256,512]{1,0:T(8,128)(2,1)S(1)}, bf16[256,512]{1,0:T(8,128)(2,1)S(1)}, u32[]{:S(2)}, u32[]{:S(2)}) collective-permute-start(bf16[256,512]{1,0:T(8,128)(2,1)S(1)} %fusion), channel_id=1, source_target_pairs={{0,16},{8,24},{16,0},{24,8},{1,17},{9,25},{17,1},{25,9},{2,18},{10... | collective-permute-start | bytes 786440 | tf_op jit(solution)/shard_map/ppermute | solution.py:18
  65.2 12.2 %collective-permute-start.23 = (bf16[256,512]{1,0:T(8,128)(2,1)S(1)}, bf16[256,512]{1,0:T(8,128)(2,1)S(1)}, u32[]{:S(2)}, u32[]{:S(2)}) collective-permute-start(bf16[256,512]{1,0:T(8,128)(2,1)S(1)} %fusion.2), channel_id=1, source_target_pairs={{0,8},{8,0},{16,24},{24,16},{1,9},{9,1},{17,25},{25,17},{2,10},{10... | collective-permute-start | bytes 786440 | tf_op jit(solution)/shard_map/ppermute | solution.py:18
  69.7 7.7 %collective-permute-start.17 = (bf16[1,256,512]{2,1,0:T(8,128)(2,1)S(1)}, bf16[1,256,512]{2,1,0:T(8,128)(2,1)S(1)}, u32[]{:S(2)}, u32[]{:S(2)}) collective-permute-start(bf16[1,256,512]{2,1,0:T(8,128)(2,1)S(1)} %get-tuple-element.54), channel_id=1, source_target_pairs={{0,4},{2,6},{4,0},{6,2},{1,5},{3,7},{5,1},{7,3},{8,12},{10,14},{12... | collective-permute-start | bytes 786440 | tf_op jit(solution)/shard_map/ppermute | solution.py:18
  70.3 11.6 %collective-permute-start.20 = (bf16[256,512]{1,0:T(8,128)(2,1)S(1)}, bf16[256,512]{1,0:T(8,128)(2,1)S(1)}, u32[]{:S(2)}, u32[]{:S(2)}) collective-permute-start(bf16[256,512]{1,0:T(8,128)(2,1)S(1)} %fusion.1), channel_id=1, source_target_pairs={{0,24},{8,16},{16,8},{24,0},{1,25},{9,17},{17,9},{25,1},{2,26},{10... | collective-permute-start | bytes 786440 | tf_op jit(solution)/shard_map/ppermute | solution.py:18
